TPU v7x, 512 devices: a whole 4x4x16 slice. The times are simulated.
512 devices in a mesh: lon: 64 (over z_lo, x, core), lat: 8 (over z_hi, y).
Axes of the slice: x: 4, y: 4, z: 16 (z_hi: 2, z_lo: 8; z = z_hi * 8 + z_lo), core: 2. Of those that a mesh axis runs over, the one named last changes fastest.
Arguments:
- fields: bfloat16 [2, 96, 1536, 192], P(None, 'lat', 'lon'), may hold values from -50 to 50
- fine_bias: float32 [16, 1, 6, 23, 144], P('lat'), may hold values from -4 to 304
- fine_qkv: bfloat16 [192, 576], replicated, may hold values from -0.4375 to 0.4375
- fine_proj: bfloat16 [192, 192], replicated, may hold values from -0.4375 to 0.4375
- fine_up: bfloat16 [192, 768], replicated, may hold values from -0.4375 to 0.4375
- fine_down: bfloat16 [768, 192], replicated, may hold values from -0.21875 to 0.21875
- merge_weight: bfloat16 [768, 384], replicated, may hold values from -0.21875 to 0.21875
- coarse_bias: float32 [8, 1, 12, 23, 144], P('lat'), may hold values from -4 to 304
- coarse_qkv: bfloat16 [384, 1152], replicated, may hold values from -0.3125 to 0.3125
- coarse_proj: bfloat16 [384, 384], replicated, may hold values from -0.3125 to 0.3125
- coarse_up: bfloat16 [384, 1536], replicated, may hold values from -0.3125 to 0.3125
- coarse_down: bfloat16 [1536, 384], replicated, may hold values from -0.15625 to 0.15625
Outputs:
- coarse_fields: bfloat16 [2, 48, 768, 384], P(None, 'lat', 'lon')
All inputs are finite; a program needn't handle non-finite values.
Results may differ from a plain program's by a relative error of at most 0.024.
Values may be sent and summed in bfloat16 or wider, within the bound.
No kernel may reach another device: no remote copies, remote signals or barrier semaphores. Data moves between devices by JAX's collectives and lax.ppermute only.
A program may use at most 128 MiB of HBM per device.

v0:
```python
import jax
import jax.numpy as jnp
from jax import lax
from jax.sharding import PartitionSpec as P

HD = 32
WZ = 2
WLAT = 6
WLON = 12


EPSILON = 1e-05


def from_behind(shard, axis, by):
    peers = lax.axis_size(axis)
    return lax.ppermute(shard, axis, [(i, (i + by) % peers) for i in range(peers)])


def layer_norm(values):
    centred = values - jnp.mean(values, axis=-1, keepdims=True)
    variance = jnp.mean(centred * centred, axis=-1, keepdims=True)
    return centred * lax.rsqrt(variance + EPSILON)


def expand_bias(bias_table):
    offsets = jnp.arange(WLON, dtype=jnp.int32)
    distance = jnp.arange(2 * WLON - 1, dtype=jnp.int32)
    one_hot = (
        offsets[:, None, None] - offsets[None, :, None] + WLON - 1 == distance[None, None, :]
    ).astype(jnp.float32)
    expanded = jnp.einsum("lzhdc,qkd->lzhcqk", bias_table, one_hot, precision=lax.Precision.HIGHEST)
    row_windows = bias_table.shape[0]
    level_windows = bias_table.shape[1]
    head_count = bias_table.shape[2]
    expanded = expanded.reshape(
        row_windows, level_windows, head_count, WZ, WZ, WLAT, WLAT, WLON, WLON
    )
    expanded = expanded.transpose(1, 0, 2, 3, 5, 7, 4, 6, 8)
    return expanded.reshape(
        level_windows, row_windows, head_count, WZ * WLAT * WLON, WZ * WLAT * WLON
    )


def window_valid(level_count, row_count, row_offset, row_total):
    level_wrap = (jnp.arange(level_count, dtype=jnp.int32) == level_count - 1).astype(jnp.int32)
    row_wrap = (
        row_offset + jnp.arange(row_count, dtype=jnp.int32) >= row_total - WLAT // 2
    ).astype(jnp.int32)
    region = level_wrap[:, None] * 2 + row_wrap[None, :]
    region = region.reshape(level_count // WZ, WZ, row_count // WLAT, WLAT).transpose(0, 2, 1, 3)
    region = jnp.broadcast_to(region[..., None], region.shape + (WLON,))
    region = region.reshape(level_count // WZ, row_count // WLAT, WZ * WLAT * WLON)
    return region[..., :, None] == region[..., None, :]


def attend(tokens, w_qkv, w_proj, full_bias, pair_valid):
    level_count, row_count, column_count, feature_width = tokens.shape
    head_count = feature_width // HD
    normed = layer_norm(tokens.astype(jnp.float32)).astype(jnp.bfloat16)
    projected = jnp.dot(
        normed.reshape(-1, feature_width), w_qkv, preferred_element_type=jnp.float32
    ).astype(jnp.bfloat16)
    projected = projected.reshape(
        level_count // WZ,
        WZ,
        row_count // WLAT,
        WLAT,
        column_count // WLON,
        WLON,
        3,
        head_count,
        HD,
    )
    projected = projected.transpose(6, 0, 2, 4, 7, 1, 3, 5, 8)
    projected = projected.reshape(
        3,
        level_count // WZ,
        row_count // WLAT,
        column_count // WLON,
        head_count,
        WZ * WLAT * WLON,
        HD,
    )
    masked_bias = jnp.where(pair_valid[:, :, None], full_bias, -1e30)
    scores = jnp.einsum(
        "zlohqd,zlohkd->zlohqk", projected[0], projected[1], preferred_element_type=jnp.float32
    )
    scores = scores * HD ** (-0.5) + masked_bias[:, :, None]
    weights_soft = jax.nn.softmax(scores, axis=-1).astype(jnp.bfloat16)
    mixed = jnp.einsum(
        "zlohqk,zlohkd->zlohqd", weights_soft, projected[2], preferred_element_type=jnp.float32
    ).astype(jnp.bfloat16)
    mixed = mixed.reshape(
        level_count // WZ, row_count // WLAT, column_count // WLON, head_count, WZ, WLAT, WLON, HD
    )
    mixed = mixed.transpose(0, 4, 1, 5, 2, 6, 3, 7).reshape(-1, feature_width)
    output = jnp.dot(mixed, w_proj, preferred_element_type=jnp.float32)
    return output.reshape(level_count, row_count, column_count, feature_width)


def feed_forward(tokens, w_up, w_down):
    feature_width = tokens.shape[-1]
    normed = layer_norm(tokens.astype(jnp.float32)).astype(jnp.bfloat16).reshape(-1, feature_width)
    hidden = jax.nn.gelu(
        jnp.dot(normed, w_up, preferred_element_type=jnp.float32), approximate=False
    ).astype(jnp.bfloat16)
    output = tokens.astype(jnp.float32).reshape(-1, feature_width) + jnp.dot(
        hidden, w_down, preferred_element_type=jnp.float32
    )
    return output.astype(jnp.bfloat16).reshape(tokens.shape)


def shift_grid(tokens):
    rolled = jnp.roll(tokens, -1, axis=0)
    column_shift = WLON // 2
    row_shift = WLAT // 2
    arrived = from_behind(rolled[:, :, :column_shift], "lon", -1)
    rolled = jnp.concatenate([rolled[:, :, column_shift:], arrived], axis=2)
    arrived = from_behind(rolled[:, :row_shift], "lat", -1)
    return jnp.concatenate([rolled[:, row_shift:], arrived], axis=1)


def roll_back(tokens):
    column_shift = WLON // 2
    row_shift = WLAT // 2
    arrived = from_behind(tokens[:, -row_shift:], "lat", 1)
    restored = jnp.concatenate([arrived, tokens[:, :-row_shift]], axis=1)
    arrived = from_behind(restored[:, :, -column_shift:], "lon", 1)
    restored = jnp.concatenate([arrived, restored[:, :, :-column_shift]], axis=2)
    return jnp.roll(restored, 1, axis=0)


def patch_merge(tokens, merge_matrix):
    level_count, row_count, column_count, feature_width = tokens.shape
    grouped = tokens.reshape(
        level_count, row_count // 2, 2, column_count // 2, 2, feature_width
    ).transpose(0, 1, 3, 2, 4, 5)
    grouped = grouped.reshape(-1, 4 * feature_width)
    normed = layer_norm(grouped.astype(jnp.float32)).astype(jnp.bfloat16)
    merged = jnp.dot(normed, merge_matrix, preferred_element_type=jnp.float32).astype(jnp.bfloat16)
    return merged.reshape(level_count, row_count // 2, column_count // 2, merge_matrix.shape[1])


def body(
    fields,
    fine_bias,
    fine_qkv,
    fine_proj,
    fine_up,
    fine_down,
    merge_weight,
    coarse_bias,
    coarse_qkv,
    coarse_proj,
    coarse_up,
    coarse_down,
):
    lat_rank = lax.axis_index("lat")
    lat_count = lax.axis_size("lat")

    def swin_block(tokens, w_qkv, w_proj, w_up, w_down, bias_table):
        level_count = tokens.shape[0]
        row_count = tokens.shape[1]
        rolled = shift_grid(tokens)
        full_bias = expand_bias(bias_table)
        pair_valid = window_valid(
            level_count, row_count, lat_rank * row_count, row_count * lat_count
        )
        attended = (
            rolled.astype(jnp.float32) + attend(rolled, w_qkv, w_proj, full_bias, pair_valid)
        ).astype(jnp.bfloat16)
        finished = feed_forward(roll_back(attended), w_up, w_down)
        return finished

    fine_field = swin_block(fields, fine_qkv, fine_proj, fine_up, fine_down, fine_bias)
    merged = patch_merge(fine_field, merge_weight)
    return swin_block(merged, coarse_qkv, coarse_proj, coarse_up, coarse_down, coarse_bias)


def solution(mesh):
    return jax.shard_map(
        body,
        mesh=mesh,
        in_specs=(
            P(None, "lat", "lon", None),
            P("lat", None, None, None, None),
            P(),
            P(),
            P(),
            P(),
            P(),
            P("lat", None, None, None, None),
            P(),
            P(),
            P(),
            P(),
        ),
        out_specs=P(None, "lat", "lon", None),
        check_vma=False,
    )
```

profile of v0, /device:TPU:0, one launch (start us, length us, event | category | flops | bytes accessed | tf_op | source)
XLA Modules:
  0.0 215.5 jit_solution(668119298900925750)
XLA Ops:
  1.8 9.4 %collective-permute-start = (bf16[2,12,6,192]{3,2,1,0:T(8,128)(2,1)}, bf16[2,12,6,192]{3,2,1,0:T(8,128)(2,1)}, u32[]{:S(2)}, u32[]{:S(2)}) collective-permute-start(bf16[2,12,6,192]{3,2,1,0:T(8,128)(2,1)} %pad_maximum_fusion.5), channel_id=1, source_target_pairs={{0,504},{8,0},{16,8},{24,16},{32,24},{40,32},{48,40},{56,48},{64,5... | collective-permute-start | bytes 165896 | tf_op jit(solution)/shard_map/ppermute | solution.py:17
  13.2 8.9 %convolution_bitcast_fusion.1 = f32[1,2,6,2,6,12,2,6,12]{8,7,4,6,3,2,1,5,0:T(8,128)} fusion(f32[2,6,2,2,6,6,23]{6,0,5,4,3,2,1:T(2,128)S(1)} %bitcast.95, s32[12,12]{1,0:T(8,128)S(1)} %subtract_add_fusion), kind=kOutput, calls=%fused_computation.3 | convolution fusion | flops 68680944 | bytes 1154880 | tf_op jit(solution)/shard_map/lzhdc,qkd->lzhcqk/dot_general | solution.py:32
  22.0 12.1 %copy.34 = f32[1,2,6,2,6,12,2,6,12]{8,7,6,5,4,3,2,1,0:T(8,128)} copy(f32[1,2,6,2,6,12,2,6,12]{8,7,4,6,3,2,1,5,0:T(8,128)} %convolution_bitcast_fusion.1) | data formatting | bytes 1990656 | tf_op jit(solution)/shard_map/transpose | solution.py:39
  34.1 10.2 %reshape.467 = f32[2,6,144,144]{3,2,1,0:T(8,128)} reshape(f32[1,2,6,2,6,12,2,6,12]{8,7,6,5,4,3,2,1,0:T(8,128)} %copy.34) | data formatting | bytes 1990656 | tf_op jit(solution)/shard_map/reshape | solution.py:40
  44.3 1.7 broadcast_select_fusion
  46.2 2.0 copy.35
  50.1 10.8 %collective-permute-start.1 = (bf16[2,3,24,192]{3,2,1,0:T(8,128)(2,1)S(1)}, bf16[2,3,24,192]{3,2,1,0:T(8,128)(2,1)S(1)}, u32[]{:S(2)}, u32[]{:S(2)}) collective-permute-start(bf16[2,3,24,192]{3,2,1,0:T(8,128)(2,1)S(1)} %pad_maximum_fusion.7), channel_id=1, source_target_pairs={{0,7},{1,0},{2,1},{3,2},{4,3},{5,4},{6,5},{7,6},{8,15},{9,8},{10,9... | collective-permute-start | bytes 165896 | tf_op jit(solution)/shard_map/ppermute | solution.py:17
  64.9 3.9 %reshape.462 = bf16[1,2,2,6,2,12,3,6,32]{8,7,6,5,4,3,2,1,0:T(8,128)(2,1)} reshape(bf16[576,576]{1,0:T(8,128)(2,1)S(1)} %convolution_convert_fusion.1) | data formatting | bytes 1327104 | tf_op jit(solution)/shard_map/reshape | solution.py:64
  68.9 3.0 %fusion.197 = (bf16[1,1,2,2,6,2,6,12,32]{8,4,0,7,3,6,2,5,1:T(8,128)(2,1)S(1)}, bf16[1,1,2,2,6,2,6,12,32]{8,4,0,7,3,6,2,5,1:T(8,128)(2,1)S(1)}, bf16[1,1,2,2,6,2,6,12,32]{8,4,0,7,3,6,2,5,1:T(8,128)(2,1)S(1)}) fusion(bf16[3,1,2,2,6,2,6,12,32]{8,4,0,7,3,6,2,5,1:T(8,128)(2,1)} %bitcast.92), kind=kLoop, calls=%fused_computation.276 | loop fusion | bytes 1327104 | tf_op jit(solution)/shard_map/slice | solution.py:92
  75.5 2.1 fusion.205
  78.1 1.9 copy.39
  80.0 1.5 copy.40
  81.5 1.4 dot_general.68
  82.9 1.3 fusion.18
  84.3 1.9 collective-permute-start.2
  86.2 8.8 %convolution_bitcast_fusion = f32[1,1,12,2,6,12,2,6,12]{2,8,7,4,6,3,5,0,1:T(8,128)} fusion(f32[12,2,2,6,6,23,1]{5,0,4,3,2,1,6:T(8,128)S(1)} %bitcast.96, s32[12,12]{1,0:T(8,128)S(1)} %subtract_add_fusion), kind=kOutput, calls=%fused_computation.2 | convolution fusion | flops 68680944 | bytes 1154880 | tf_op jit(solution)/shard_map/lzhdc,qkd->lzhcqk/dot_general | solution.py:32
  95.1 6.7 %collective-permute-done.2 = bf16[2,3,24,192]{3,2,1,0:T(8,128)(2,1)S(1)} collective-permute-done((bf16[2,3,24,192]{3,2,1,0:T(8,128)(2,1)S(1)}, bf16[2,3,24,192]{3,2,1,0:T(8,128)(2,1)S(1)}, u32[]{:S(2)}, u32[]{:S(2)}) %collective-permute-start.2) | collective-permute-done | bytes 55328 | tf_op jit(solution)/shard_map/ppermute | solution.py:17
  101.8 2.1 collective-permute-start.3
  103.9 12.5 %collective-permute-done.3 = bf16[2,12,6,192]{3,2,1,0:T(8,128)(2,1)S(1)} collective-permute-done((bf16[2,12,6,192]{3,2,1,0:T(8,128)(2,1)S(1)}, bf16[2,12,6,192]{3,2,1,0:T(8,128)(2,1)S(1)}, u32[]{:S(2)}, u32[]{:S(2)}) %collective-permute-start.3) | collective-permute-done | bytes 55328 | tf_op jit(solution)/shard_map/ppermute | solution.py:17
  117.5 5.4 %fusion.21 = f32[576,192]{0,1:T(8,128)S(1)} fusion(f32[576,192]{0,1:T(8,128)S(1)} %copy.41, bf16[768,192]{0,1:T(8,128)(2,1)S(1)} %copy-done.9, bf16[192,768]{1,0:T(8,128)(2,1)} %param.16, f32[576,192]{1,0:T(8,128)S(1)} %bitcast.101, f32[576]{0:T(1024)S(1)} %rsqrt.58, f32[576]{0:T(1024)S(1)} %div.64), kind=kOutput, calls=%fused_computation.42 | convolution fusion | flops 369156096 | bytes 1921536 | tf_op jit(solution)/shard_map/dot_general | solution.py:108
  126.0 1.9 collective-permute-start.4
  128.2 4.0 %collective-permute-done.4 = bf16[2,6,6,384]{3,2,1,0:T(8,128)(2,1)S(1)} collective-permute-done((bf16[2,6,6,384]{3,2,1,0:T(8,128)(2,1)S(1)}, bf16[2,6,6,384]{3,2,1,0:T(8,128)(2,1)S(1)}, u32[]{:S(2)}, u32[]{:S(2)}) %collective-permute-start.4) | collective-permute-done | bytes 55328 | tf_op jit(solution)/shard_map/ppermute | solution.py:17
  132.3 6.4 %collective-permute-start.5 = (bf16[2,3,12,384]{3,2,1,0:T(8,128)(2,1)S(1)}, bf16[2,3,12,384]{3,2,1,0:T(8,128)(2,1)S(1)}, u32[]{:S(2)}, u32[]{:S(2)}) collective-permute-start(bf16[2,3,12,384]{3,2,1,0:T(8,128)(2,1)S(1)} %get-tuple-element.20), channel_id=1, source_target_pairs={{0,7},{1,0},{2,1},{3,2},{4,3},{5,4},{6,5},{7,6},{8,15},{9,8},{10,9... | collective-permute-start | bytes 165896 | tf_op jit(solution)/shard_map/ppermute | solution.py:17
  138.8 21.6 %copy.75 = f32[1,1,12,2,6,12,2,6,12]{5,4,3,8,7,6,2,1,0:T(8,128)} copy(f32[1,1,12,2,6,12,2,6,12]{2,8,7,4,6,3,5,0,1:T(8,128)} %convolution_bitcast_fusion) | data formatting | bytes 1990656 | tf_op jit(solution)/shard_map/reshape | solution.py:40
  160.4 10.3 %reshape.492 = f32[12,144,144]{1,2,0:T(8,128)} reshape(f32[1,1,12,2,6,12,2,6,12]{5,4,3,8,7,6,2,1,0:T(8,128)} %copy.75) | data formatting | bytes 1990656 | tf_op jit(solution)/shard_map/reshape | solution.py:40
  171.7 1.4 reshape.470
  175.7 1.6 convolution_convert_fusion.2
  178.8 1.9 collective-permute-start.6
  180.7 15.1 %collective-permute-done.6 = bf16[2,3,12,384]{3,2,1,0:T(8,128)(2,1)S(1)} collective-permute-done((bf16[2,3,12,384]{3,2,1,0:T(8,128)(2,1)S(1)}, bf16[2,3,12,384]{3,2,1,0:T(8,128)(2,1)S(1)}, u32[]{:S(2)}, u32[]{:S(2)}) %collective-permute-start.6) | collective-permute-done | bytes 55328 | tf_op jit(solution)/shard_map/ppermute | solution.py:17
  195.9 1.9 collective-permute-start.7
  197.8 12.5 %collective-permute-done.7 = bf16[2,6,6,384]{3,2,1,0:T(8,128)(2,1)S(1)} collective-permute-done((bf16[2,6,6,384]{3,2,1,0:T(8,128)(2,1)S(1)}, bf16[2,6,6,384]{3,2,1,0:T(8,128)(2,1)S(1)}, u32[]{:S(2)}, u32[]{:S(2)}) %collective-permute-start.7) | collective-permute-done | bytes 55328 | tf_op jit(solution)/shard_map/ppermute | solution.py:17
  211.0 3.8 %fusion.25 = bf16[144,384]{1,0:T(8,128)(2,1)S(1)} fusion(f32[144,384]{1,0:T(8,128)S(1)} %reshape.483, bf16[1536,384]{1,0:T(8,128)(2,1)S(1)} %copy-done, bf16[384,1536]{1,0:T(8,128)(2,1)} %param.22, f32[144]{0:T(256)S(1)} %rsqrt.64, f32[144]{0:T(256)S(1)} %div.75), kind=kOutput, calls=%fused_computation.49 | convolution fusion | flops 354392064 | bytes 2692224 | tf_op jit(solution)/shard_map/dot_general | solution.py:108
  (118 shorter events, 24.5 us)
Async XLA Ops:
  0.0 211.0 %copy-start = (bf16[1536,384]{1,0:T(8,128)(2,1)S(1)}, bf16[1536,384]{1,0:T(8,128)(2,1)}, u32[]{:S(2)}) copy-start(bf16[1536,384]{1,0:T(8,128)(2,1)} %param.23) | copy-start | bytes 3538948
  1.8 47.5 %collective-permute-start = (bf16[2,12,6,192]{3,2,1,0:T(8,128)(2,1)}, bf16[2,12,6,192]{3,2,1,0:T(8,128)(2,1)}, u32[]{:S(2)}, u32[]{:S(2)}) collective-permute-start(bf16[2,12,6,192]{3,2,1,0:T(8,128)(2,1)} %pad_maximum_fusion.5), channel_id=1, source_target_pairs={{0,504},{8,0},{16,8},{24,16},{32,24},{40,32},{48,40},{56,48},{64,5... | collective-permute-start | bytes 165896 | tf_op jit(solution)/shard_map/ppermute | solution.py:17
  46.1 2.0 copy-start.8
  50.1 12.6 %collective-permute-start.1 = (bf16[2,3,24,192]{3,2,1,0:T(8,128)(2,1)S(1)}, bf16[2,3,24,192]{3,2,1,0:T(8,128)(2,1)S(1)}, u32[]{:S(2)}, u32[]{:S(2)}) collective-permute-start(bf16[2,3,24,192]{3,2,1,0:T(8,128)(2,1)S(1)} %pad_maximum_fusion.7), channel_id=1, source_target_pairs={{0,7},{1,0},{2,1},{3,2},{4,3},{5,4},{6,5},{7,6},{8,15},{9,8},{10,9... | collective-permute-start | bytes 165896 | tf_op jit(solution)/shard_map/ppermute | solution.py:17
  61.9 7.0 %copy-start.3 = (bf16[2,9,24,192]{3,2,1,0:T(8,128)(2,1)}, bf16[2,9,24,192]{3,2,1,0:T(8,128)(2,1)S(1)}, u32[]{:S(2)}) copy-start(bf16[2,9,24,192]{3,2,1,0:T(8,128)(2,1)S(1)} %fusion.112) | copy-start | bytes 497668
  62.7 0.6 copy-start.5
  74.0 1.5 copy-start.2
  84.3 17.4 %collective-permute-start.2 = (bf16[2,3,24,192]{3,2,1,0:T(8,128)(2,1)S(1)}, bf16[2,3,24,192]{3,2,1,0:T(8,128)(2,1)S(1)}, u32[]{:S(2)}, u32[]{:S(2)}) collective-permute-start(bf16[2,3,24,192]{3,2,1,0:T(8,128)(2,1)S(1)} %slice.149), channel_id=1, source_target_pairs={{0,1},{1,2},{2,3},{3,4},{4,5},{5,6},{6,7},{7,0},{8,9},{9,10},{10,1... | collective-permute-start | bytes 165896 | tf_op jit(solution)/shard_map/ppermute | solution.py:17
  101.8 14.6 %collective-permute-start.3 = (bf16[2,12,6,192]{3,2,1,0:T(8,128)(2,1)S(1)}, bf16[2,12,6,192]{3,2,1,0:T(8,128)(2,1)S(1)}, u32[]{:S(2)}, u32[]{:S(2)}) collective-permute-start(bf16[2,12,6,192]{3,2,1,0:T(8,128)(2,1)S(1)} %pad_maximum_fusion.4), channel_id=1, source_target_pairs={{0,8},{8,16},{16,24},{24,32},{32,40},{40,48},{48,56},{56,64},{64,7... | collective-permute-start | bytes 165896 | tf_op jit(solution)/shard_map/ppermute | solution.py:17
  116.5 1.0 copy-start.9
  123.5 2.1 copy-start.6
  126.0 6.2 %collective-permute-start.4 = (bf16[2,6,6,384]{3,2,1,0:T(8,128)(2,1)S(1)}, bf16[2,6,6,384]{3,2,1,0:T(8,128)(2,1)S(1)}, u32[]{:S(2)}, u32[]{:S(2)}) collective-permute-start(bf16[2,6,6,384]{3,2,1,0:T(8,128)(2,1)S(1)} %get-tuple-element.22), channel_id=1, source_target_pairs={{0,504},{8,0},{16,8},{24,16},{32,24},{40,32},{48,40},{56,48},{64,5... | collective-permute-start | bytes 165896 | tf_op jit(solution)/shard_map/ppermute | solution.py:17
  132.3 38.4 %collective-permute-start.5 = (bf16[2,3,12,384]{3,2,1,0:T(8,128)(2,1)S(1)}, bf16[2,3,12,384]{3,2,1,0:T(8,128)(2,1)S(1)}, u32[]{:S(2)}, u32[]{:S(2)}) collective-permute-start(bf16[2,3,12,384]{3,2,1,0:T(8,128)(2,1)S(1)} %get-tuple-element.20), channel_id=1, source_target_pairs={{0,7},{1,0},{2,1},{3,2},{4,3},{5,4},{6,5},{7,6},{8,15},{9,8},{10,9... | collective-permute-start | bytes 165896 | tf_op jit(solution)/shard_map/ppermute | solution.py:17
  160.4 10.9 %copy-start.4 = (bf16[384,1152]{1,0:T(8,128)(2,1)S(1)}, bf16[384,1152]{1,0:T(8,128)(2,1)}, u32[]{:S(2)}) copy-start(bf16[384,1152]{1,0:T(8,128)(2,1)} %param.20) | copy-start | bytes 2654212
  173.1 1.7 copy-start.1
  177.3 1.2 copy-start.7
  178.8 17.1 %collective-permute-start.6 = (bf16[2,3,12,384]{3,2,1,0:T(8,128)(2,1)S(1)}, bf16[2,3,12,384]{3,2,1,0:T(8,128)(2,1)S(1)}, u32[]{:S(2)}, u32[]{:S(2)}) collective-permute-start(bf16[2,3,12,384]{3,2,1,0:T(8,128)(2,1)S(1)} %get-tuple-element.17), channel_id=1, source_target_pairs={{0,1},{1,2},{2,3},{3,4},{4,5},{5,6},{6,7},{7,0},{8,9},{9,10},{10,1... | collective-permute-start | bytes 165896 | tf_op jit(solution)/shard_map/ppermute | solution.py:17
  195.9 14.4 %collective-permute-start.7 = (bf16[2,6,6,384]{3,2,1,0:T(8,128)(2,1)S(1)}, bf16[2,6,6,384]{3,2,1,0:T(8,128)(2,1)S(1)}, u32[]{:S(2)}, u32[]{:S(2)}) collective-permute-start(bf16[2,6,6,384]{3,2,1,0:T(8,128)(2,1)S(1)} %fusion.129), channel_id=1, source_target_pairs={{0,8},{8,16},{16,24},{24,32},{32,40},{40,48},{48,56},{56,64},{64,7... | collective-permute-start | bytes 165896 | tf_op jit(solution)/shard_map/ppermute | solution.py:17
where the time goes:
time: 217 us; the launch traced here: 216 us
  local copies, waits for them, and re-layouts  82.6 us (38%)
  waiting for transfers between devices  51.6 us (24%)
  starting transfers between devices  36.5 us (17%)
  matrix products  33.8 us (16%)
  other arithmetic  10.2 us (5%)
    ppermute x8, waiting for transfers between devices, from_behind(): lax.ppermute(shard, axis, [(i, (i + by) % peers) for i in range(peers)])  51.6 us
    reshape x3, local copies, waits for them, and re-layouts, expand_bias(): expanded.reshape(level_windows, row_windows, head_count, WZ * WLAT * WLON...  42.2 us
    ppermute x8, starting transfers between devices, from_behind(): lax.ppermute(shard, axis, [(i, (i + by) % peers) for i in range(peers)])  36.5 us
    dot_general x2, matrix products, expand_bias(): jnp.einsum('lzhdc,qkd->lzhcqk', bias_table, one_hot, precision=lax.Precis...  17.7 us
    transpose x1, local copies, waits for them, and re-layouts, expand_bias(): expanded = expanded.transpose(1, 0, 2, 3, 5, 7, 4, 6, 8)  12.1 us
    dot_general x2, matrix products, feed_forward(): jnp.dot(hidden, w_down, preferred_element_type=jnp.float32)  9.15 us
    reshape x2, local copies, waits for them, and re-layouts, attend(): projected.reshape(level_count // WZ, WZ, row_count // WLAT, WLAT, column_...  5.3 us
    slice x3, local copies, waits for them, and re-layouts, attend(): projected[2]  4.83 us
  transfers between devices with their start and end apart: 8, of which 6 were waited for; matrix products, arithmetic and copies ran while one was open for 37% of the time, Pallas kernels for 0%

commit v1 on v0

v1 whole, which is shorter than its diff:
```python
import functools

import jax
import jax.numpy as jnp
from jax import lax
from jax.experimental import pallas as pl
from jax.experimental.pallas import tpu as pltpu
from jax.sharding import PartitionSpec as P

HD = 32
WZ = 2
WLAT = 6
WLON = 12
CELLS = WZ * WLAT * WLON
LINES = WZ * WLAT
SPAN = 2 * WLON - 1
EPSILON = 1e-05
MASKED = -1e30
VMEM_LIMIT = 40 * 1024 * 1024

f32 = jnp.float32
bf16 = jnp.bfloat16


def from_behind(shard, axis, by):
    peers = lax.axis_size(axis)
    return lax.ppermute(shard, axis, [(i, (i + by) % peers) for i in range(peers)])


def normalise(values):
    centred = values - jnp.mean(values, axis=-1, keepdims=True)
    variance = jnp.mean(centred * centred, axis=-1, keepdims=True)
    return (centred * lax.rsqrt(variance + EPSILON)).astype(bf16)


def dot(a, b):
    return jnp.dot(a, b, preferred_element_type=f32)


def dot_nt(a, b):
    return lax.dot_general(a, b, (((1,), (1,)), ((), ())), preferred_element_type=f32)


def gelu(x):
    return 0.5 * x * (1.0 + lax.erf(x * (2.0**-0.5)))


def feed_forward(x, up_ref, down_ref):
    hidden = gelu(dot(normalise(x), up_ref[...])).astype(bf16)
    return (x + dot(hidden, down_ref[...])).astype(bf16).astype(f32)


def three_parts(x):
    high = x.astype(bf16)
    rest = x - high.astype(f32)
    middle = rest.astype(bf16)
    low = (rest - middle.astype(f32)).astype(bf16)
    return high, middle, low


def iota(shape, axis):
    return lax.broadcasted_iota(jnp.int32, shape, axis)


def bias_kernel(last_ref, fine_ref, coarse_ref, fine_out, coarse_out, stacked, spread_from):
    stacked[...] = jnp.zeros_like(stacked)
    spread_from[...] = jnp.zeros_like(spread_from)
    row = iota((CELLS, CELLS), 0)
    key, query = row // LINES, row % LINES
    column = ((query // WLAT * WZ + key // WLAT) * WLAT + query % WLAT) * WLAT + key % WLAT
    pick = (iota((CELLS, CELLS), 1) == column).astype(f32).astype(bf16)
    row = iota((LINES * 32, 384), 0)
    lane = iota((LINES * 32, 384), 1)
    spread = (lane == (SPAN - 1 - row % 32) * LINES + row // 32) & (row % 32 < SPAN)
    spread = spread.astype(f32).astype(bf16)
    row, lane = iota((6 * LINES, 384), 0) % LINES, iota((6 * LINES, 384), 1) % LINES
    levels_differ = row // WLAT != lane // WLAT
    rows_differ = (row % WLAT >= WLAT // 2) != (lane % WLAT >= WLAT // 2)

    def expand(table_of, out_of, last):
        for head in range(6):
            stacked[head * 24 : head * 24 + SPAN, :] = table_of(head)
        picked = sum(dot_nt(pick, part) for part in three_parts(stacked[...]))
        for head in range(6):
            for key in range(LINES):
                spread_from[head * LINES : (head + 1) * LINES, key * 32 : key * 32 + 24] = picked[
                    key * LINES : (key + 1) * LINES, head * 24 : (head + 1) * 24
                ]
        flat = sum(dot(part, spread) for part in three_parts(spread_from[...]))
        if last is None:
            apart = levels_differ
        else:
            apart = levels_differ | (rows_differ & (last > 0))
        flat = jnp.where(apart, MASKED, flat)
        for o in range(WLON):
            start = (WLON - 1 - o) * LINES
            piece = flat[:, start : start + CELLS]
            for head in range(6):
                out_of(head, o * LINES, piece[head * LINES : (head + 1) * LINES])

    def put_fine(n):
        def put(head, at, piece):
            fine_out[n, head, at : at + LINES, :] = piece

        return put

    def put_coarse(base):
        def put(head, at, piece):
            coarse_out[base + head, at : at + LINES, :] = piece

        return put

    last = last_ref[0]
    expand(lambda head: fine_ref[0, 0, head], put_fine(0), None)
    expand(lambda head: fine_ref[1, 0, head], put_fine(1), last)
    expand(lambda head: coarse_ref[0, 0, head], put_coarse(0), last)
    expand(lambda head: coarse_ref[0, 0, 6 + head], put_coarse(6), last)


def attend_group(q, k, v, bias, heads):
    queries, width = q.shape
    of_head = iota((queries, width), 1) // HD
    big = jnp.concatenate([jnp.where(of_head == h, q, 0.0) for h in range(heads)], axis=0)
    scores = dot_nt(big.astype(bf16), k) * HD ** (-0.5) + bias.reshape(heads * queries, CELLS)
    top = jnp.max(scores, axis=-1, keepdims=True)
    weights = jnp.exp(scores - top)
    total = jnp.sum(weights, axis=-1, keepdims=True)
    mixed = dot(weights.astype(bf16), v) * (1.0 / total)
    out = jnp.zeros((queries, width), f32)
    for h in range(heads):
        out = jnp.where(of_head == h, mixed[h * queries : (h + 1) * queries], out)
    return out


def tiles_of(rows, width):
    return ((-(-width // 128), rows, 128), f32)


def put(ref, at, rows, stride, values):
    width = values.shape[-1]
    for t in range(ref.shape[0]):
        piece = values[:, t * 128 : min((t + 1) * 128, width)]
        if piece.shape[-1] < 128:
            piece = jnp.concatenate([piece, jnp.zeros((rows, 128 - piece.shape[-1]), f32)], axis=-1)
        ref[t, pl.ds(at, rows, stride=stride), :] = piece


def get(ref, at, rows, stride, width):
    pieces = [ref[t, pl.ds(at, rows, stride=stride), :] for t in range(ref.shape[0])]
    return jnp.concatenate(pieces, axis=-1)[:, :width]


def fine_attention_kernel(
    own_ref, below_ref, right_ref, bias_ref, qkv_ref, proj_ref, out_ref, send_ref, x_ref, a_ref, w_ref, s_ref
):
    for z in range(WZ):
        for rho in range(2 * WLAT):
            n, a = divmod(rho, WLAT)
            line = own_ref[1 - z, 3 + rho] if rho < 9 else below_ref[1 - z, rho - 9]
            put(x_ref, n * 576 + z * WLAT + a, 24, LINES, line.astype(f32))
            put(x_ref, n * 576 + 288 + z * WLAT + a, 24, LINES, right_ref[1 - z, rho].astype(f32))
    for n in range(2):
        normed = normalise(get(x_ref, n * 576 + 72, 432, 1, 192))
        q = dot(normed, qkv_ref[:, 0:192]).astype(bf16).astype(f32)
        k = dot(normed, qkv_ref[:, 192:384]).astype(bf16)
        v = dot(normed, qkv_ref[:, 384:576]).astype(bf16)
        left, right = [], []
        for window, start, stop in ((0, 72, 144), (1, 0, 144), (2, 0, 72)):
            at = window * CELLS
            q_rows = q[at + start : at + stop]
            k_rows, v_rows = k[at : at + CELLS], v[at : at + CELLS]
            bias = bias_ref[n, :, start:stop, :]
            left.append(attend_group(q_rows[:, :128], k_rows[:, :128], v_rows[:, :128], bias[:4], 4))
            right.append(attend_group(q_rows[:, 128:], k_rows[:, 128:], v_rows[:, 128:], bias[4:], 2))
        left = jnp.concatenate(left, axis=0).astype(bf16)
        right = jnp.concatenate(right, axis=0).astype(bf16)
        product = dot(left, proj_ref[0:128, :]) + dot(right, proj_ref[128:192, :])
        attended = (get(x_ref, n * 576 + 144, 288, 1, 192) + product).astype(bf16).astype(f32)
        put(a_ref, n * 288, 288, 1, attended)
    for t in range(2):
        for pb in range(2):
            for z in range(WZ):
                for rho in range(12):
                    n, a = divmod(rho, WLAT)
                    line = a_ref[t, pl.ds(n * 288 + pb * LINES + z * WLAT + a, 12, stride=24), :]
                    if rho < 3:
                        at = (z * 3 + rho) * 24 + pb * 12
                        s_ref[t, at : at + 12, :] = line
                        line = jnp.zeros((12, 128), f32)
                        rho += 12
                    w_ref[t, pl.ds(pb * 288 + z * 12 + rho - 3, 12, stride=24), :] = line
    out_ref[...] = get(w_ref, 0, 576, 1, 192).astype(bf16)
    send_ref[...] = get(s_ref, 0, 144, 1, 192).astype(bf16)


def fine_feed_forward_kernel(a_ref, up_ref, down_ref, out_ref):
    for i in range(4):
        rows = slice(i * 144, (i + 1) * 144)
        out_ref[rows, :] = feed_forward(a_ref[rows, :].astype(f32), up_ref, down_ref).astype(bf16)


def coarse_kernel(
    y_ref, got_ref, fine_up_ref, fine_down_ref, merge_ref, bias_ref, qkv_ref, proj_ref, up_ref, down_ref,
    keep_ref, send_ref, w_ref, r_ref, o_ref,
):
    put(r_ref, 0, 144, 1, feed_forward(got_ref[...].astype(f32), fine_up_ref, fine_down_ref))
    put(w_ref, 0, 576, 1, y_ref[...].astype(f32))
    for t in range(2):
        for pb in range(2):
            for z in range(WZ):
                for rho in range(3):
                    at = (z * 3 + rho) * 24 + pb * 12
                    w_ref[t, pl.ds(pb * 288 + z * 12 + 9 + rho, 12, stride=24), :] = r_ref[t, at : at + 12, :]
    parts = [get(w_ref, pb * 288 + pa, CELLS, 2, 192) for pa in range(2) for pb in range(2)]
    mean = sum(jnp.sum(part, axis=-1, keepdims=True) for part in parts) * (1.0 / 768)
    parts = [part - mean for part in parts]
    variance = sum(jnp.sum(part * part, axis=-1, keepdims=True) for part in parts) * (1.0 / 768)
    scale = lax.rsqrt(variance + EPSILON)
    merged = sum(
        dot((part * scale).astype(bf16), merge_ref[i * 192 : (i + 1) * 192, :]) for i, part in enumerate(parts)
    )
    merged = merged.astype(bf16).astype(f32)
    normed = normalise(merged)
    qkv = dot(normed, qkv_ref[...]).astype(bf16)
    product = merged
    for g in range(3):
        q = qkv[:, g * 128 : (g + 1) * 128].astype(f32)
        k = qkv[:, 384 + g * 128 : 384 + (g + 1) * 128]
        v = qkv[:, 768 + g * 128 : 768 + (g + 1) * 128]
        mixed = attend_group(q, k, v, bias_ref[g * 4 : (g + 1) * 4], 4)
        product = product + dot(mixed.astype(bf16), proj_ref[g * 128 : (g + 1) * 128, :])
    attended = product.astype(bf16).astype(f32)
    put(o_ref, 0, CELLS, 1, feed_forward(attended, up_ref, down_ref))
    for z in range(WZ):
        for i in range(3):
            keep_ref[1 - z, i] = get(o_ref, z * WLAT + i, WLON, LINES, 384).astype(bf16)
            send_ref[1 - z, i] = get(o_ref, z * WLAT + 3 + i, WLON, LINES, 384).astype(bf16)


def call(kernel, outs, scratch, operands, flops, smem=0):
    specs = [pl.BlockSpec(memory_space=pltpu.SMEM)] * smem
    specs += [pl.BlockSpec(memory_space=pltpu.VMEM)] * (len(operands) - smem)
    return pl.pallas_call(
        kernel,
        out_shape=[jax.ShapeDtypeStruct(shape, dtype) for shape, dtype in outs],
        in_specs=specs,
        out_specs=[pl.BlockSpec(memory_space=pltpu.VMEM)] * len(outs),
        scratch_shapes=[pltpu.VMEM(shape, dtype) for shape, dtype in scratch],
        compiler_params=pltpu.CompilerParams(vmem_limit_bytes=VMEM_LIMIT),
        cost_estimate=pl.CostEstimate(
            flops=flops,
            bytes_accessed=sum(a.size * a.dtype.itemsize for a in operands),
            transcendentals=0,
        ),
    )(*operands)


def body(
    fields,
    fine_bias,
    fine_qkv,
    fine_proj,
    fine_up,
    fine_down,
    merge_weight,
    coarse_bias,
    coarse_qkv,
    coarse_proj,
    coarse_up,
    coarse_down,
):
    last = (lax.axis_index("lat") == lax.axis_size("lat") - 1).astype(jnp.int32).reshape(1)
    below = from_behind(fields[:, :3], "lat", -1)
    right = from_behind(jnp.concatenate([fields[:, 3:], below], axis=1), "lon", -1)
    bias1, bias2 = call(
        bias_kernel,
        [((2, 6, CELLS, CELLS), f32), ((12, CELLS, CELLS), f32)],
        [((CELLS, CELLS), f32), ((6 * LINES, LINES * 32), f32)],
        [last, fine_bias, coarse_bias],
        3_000_000_000,
        smem=1,
    )
    attended, edge = call(
        fine_attention_kernel,
        [((576, 192), bf16), ((144, 192), bf16)],
        [tiles_of(1152, 192), tiles_of(576, 192), tiles_of(576, 192), tiles_of(144, 192)],
        [fields, below, right, bias1, fine_qkv, fine_proj],
        2_000_000_000,
    )
    got = from_behind(edge, "lat", -1)
    (finished,) = call(
        fine_feed_forward_kernel, [((576, 192), bf16)], [], [attended, fine_up, fine_down], 3_000_000_000
    )
    keep, send = call(
        coarse_kernel,
        [((2, 3, 12, 384), bf16), ((2, 3, 12, 384), bf16)],
        [tiles_of(576, 192), tiles_of(144, 192), tiles_of(CELLS, 384)],
        [finished, got, fine_up, fine_down, merge_weight, bias2, coarse_qkv, coarse_proj, coarse_up, coarse_down],
        4_000_000_000,
    )
    above = from_behind(send, "lat", 1)
    rows = jnp.concatenate([above, keep], axis=1)
    arrived = from_behind(rows[:, :, 6:], "lon", 1)
    return jnp.concatenate([arrived, rows[:, :, :6]], axis=2)


def solution(mesh):
    return jax.shard_map(
        body,
        mesh=mesh,
        in_specs=(
            P(None, "lat", "lon", None),
            P("lat", None, None, None, None),
            P(),
            P(),
            P(),
            P(),
            P(),
            P("lat", None, None, None, None),
            P(),
            P(),
            P(),
            P(),
        ),
        out_specs=P(None, "lat", "lon", None),
        check_vma=False,
    )
```

time: 217 us -> 87.8 us (0.40)
  the two profiles are of different devices: /device:TPU:0 before, /device:TPU:32 now
where the time goes in v1:
time: 87.8 us; the launch traced here: 87.5 us
  starting transfers between devices  39.8 us (45%)
  waiting for transfers between devices  32 us (36%)
  Pallas kernels  11.5 us (13%)
  local copies, waits for them, and re-layouts  3.94 us (4%)
    ppermute x5, starting transfers between devices, from_behind(): lax.ppermute(shard, axis, [(i, (i + by) % peers) for i in range(peers)])  39.8 us
    ppermute x5, waiting for transfers between devices, from_behind(): lax.ppermute(shard, axis, [(i, (i + by) % peers) for i in range(peers)])  32 us
    pallas_call x4, Pallas kernels, call(): pl.pallas_call(kernel, out_shape=[jax.ShapeDtypeStruct(shape, dtype) for...  11.5 us
    unnamed x24, local copies, waits for them, and re-layouts  2.21 us
  transfers between devices with their start and end apart: 5, of which 5 were waited for; matrix products, arithmetic and copies ran while one was open for 2% of the time, Pallas kernels for 5%

profile of v1, /device:TPU:32, one launch (start us, length us, event | category | flops | bytes accessed | tf_op | source)
XLA Modules:
  0.0 87.5 jit_solution(13591909623481742818)
XLA Ops:
  0.0 0.9 %slice.12 = bf16[2,3,24,192]{3,2,1,0:T(8,128)(2,1)S(1)} slice(bf16[2,12,24,192]{3,2,1,0:T(8,128)(2,1)} %own_ref.1), slice={[0:2], [0:3], [0:24], [0:192]} | slice | bytes 110592 | tf_op jit(solution)/shard_map/slice | solution.py:273
  1.0 17.3 %collective-permute-start = (bf16[2,3,24,192]{3,2,1,0:T(8,128)(2,1)S(1)}, bf16[2,3,24,192]{3,2,1,0:T(8,128)(2,1)S(1)}, u32[]{:S(2)}, u32[]{:S(2)}) collective-permute-start(bf16[2,3,24,192]{3,2,1,0:T(8,128)(2,1)S(1)} %slice.12), channel_id=1, source_target_pairs={{0,7},{1,0},{2,1},{3,2},{4,3},{5,4},{6,5},{7,6},{8,15},{9,8},{10,9... | collective-permute-start | bytes 165896 | tf_op jit(solution)/shard_map/ppermute | solution.py:27
  18.2 1.0 %copy.13.fine_ref = f32[2,1,6,23,144]{4,3,2,1,0:T(8,128)S(1)} copy(f32[2,1,6,23,144]{4,1,3,2,0:T(1,128)} %param.13) | data formatting | bytes 317952 | tf_op args[1]
  19.2 1.0 %copy.14.coarse_ref = f32[1,1,12,23,144]{4,3,2,1,0:T(8,128)S(1)} copy(f32[1,1,12,23,144]{4,1,3,2,0:T(1,128)} %param.19) | data formatting | bytes 317952 | tf_op args[7]
  20.2 0.0 copy-done.9
  20.2 0.2 copy.15.down_ref.fine_down_ref
  20.4 4.2 %collective-permute-done.below_ref = bf16[2,3,24,192]{3,2,1,0:T(8,128)(2,1)S(1)} collective-permute-done((bf16[2,3,24,192]{3,2,1,0:T(8,128)(2,1)S(1)}, bf16[2,3,24,192]{3,2,1,0:T(8,128)(2,1)S(1)}, u32[]{:S(2)}, u32[]{:S(2)}) %collective-permute-start) | collective-permute-done | bytes 55328 | tf_op jit(solution)/shard_map/ppermute | solution.py:27
  24.6 0.0 slice-done
  24.6 0.1 pad_maximum_fusion
  24.7 3.4 %collective-permute-start.1 = (bf16[2,12,24,192]{3,2,1,0:T(8,128)(2,1)S(1)}, bf16[2,12,24,192]{3,2,1,0:T(8,128)(2,1)S(1)}, u32[]{:S(2)}, u32[]{:S(2)}) collective-permute-start(bf16[2,12,24,192]{3,2,1,0:T(8,128)(2,1)S(1)} %pad_maximum_fusion), channel_id=1, source_target_pairs={{0,504},{8,0},{16,8},{24,16},{32,24},{40,32},{48,40},{56,48},{64,5... | collective-permute-start | bytes 663560 | tf_op jit(solution)/shard_map/ppermute | solution.py:27
  28.1 0.0 copy-start
  28.1 0.0 copy-start.7
  28.1 0.0 copy-start.8
  28.2 3.5 %shard_map.118 = (f32[2,6,144,144]{3,2,1,0:T(8,128)S(1)}, f32[12,144,144]{2,1,0:T(8,128)S(1)}) custom-call(s32[1]{0:T(128)} %bitcast.last_ref, f32[2,1,6,23,144]{4,3,2,1,0:T(8,128)S(1)} %copy.13.fine_ref, f32[1,1,12,23,144]{4,3,2,1,0:T(8,128)S(1)} %copy.14.coarse_ref), custom_call_target="tpu_custom_call" | custom-call | flops 3000000000 | bytes 317956 | tf_op jit(solution)/shard_map/pallas_call | solution.py:243
  31.6 0.7 collective-permute-done.1.right_ref
  32.4 3.0 %shard_map.119 = (bf16[576,192]{1,0:T(8,128)(2,1)S(1)}, bf16[144,192]{1,0:T(8,128)(2,1)S(1)}) custom-call(bf16[2,12,24,192]{3,2,1,0:T(8,128)(2,1)S(1)} %copy-done, bf16[2,3,24,192]{3,2,1,0:T(8,128)(2,1)S(1)} %collective-permute-done.below_ref, bf16[2,12,24,192]{3,2,1,0:T(8,128)(2,1)S(1)} %collective-permute-done.1.right_ref, ...), custom_call_target="tpu_custom_call" | custom-call | flops 2000000000 | bytes 1787904 | tf_op jit(solution)/shard_map/pallas_call | solution.py:243
  35.4 15.2 %collective-permute-start.2 = (bf16[144,192]{1,0:T(8,128)(2,1)S(1)}, bf16[144,192]{1,0:T(8,128)(2,1)S(1)}, u32[]{:S(2)}, u32[]{:S(2)}) collective-permute-start(bf16[144,192]{1,0:T(8,128)(2,1)S(1)} %get-tuple-element.13), channel_id=1, source_target_pairs={{0,7},{1,0},{2,1},{3,2},{4,3},{5,4},{6,5},{7,6},{8,15},{9,8},{10,9... | collective-permute-start | bytes 165896 | tf_op jit(solution)/shard_map/ppermute | solution.py:27
  50.6 0.0 copy-start.1
  50.6 0.0 copy-start.2
  50.6 0.0 copy-start.3
  50.6 0.0 copy-start.4
  50.7 0.0 copy-start.6
  50.7 1.0 %shard_map.120.y_ref = bf16[576,192]{1,0:T(8,128)(2,1)S(1)} custom-call(bf16[576,192]{1,0:T(8,128)(2,1)S(1)} %get-tuple-element.12.a_ref, bf16[192,768]{1,0:T(8,128)(2,1)S(1)} %copy-done.5, bf16[768,192]{1,0:T(8,128)(2,1)S(1)} %copy.15.down_ref.fine_down_ref), custom_call_target="tpu_custom_call" | custom-call | flops 3000000000 | bytes 811008 | tf_op jit(solution)/shard_map/pallas_call | solution.py:243
  51.7 3.8 %collective-permute-done.2.got_ref = bf16[144,192]{1,0:T(8,128)(2,1)S(1)} collective-permute-done((bf16[144,192]{1,0:T(8,128)(2,1)S(1)}, bf16[144,192]{1,0:T(8,128)(2,1)S(1)}, u32[]{:S(2)}, u32[]{:S(2)}) %collective-permute-start.2) | collective-permute-done | bytes 55328 | tf_op jit(solution)/shard_map/ppermute | solution.py:27
  55.4 0.0 copy-done.3
  55.4 4.0 %shard_map.121 = (bf16[2,3,12,384]{3,2,1,0:T(8,128)(2,1)S(1)}, bf16[2,3,12,384]{3,2,1,0:T(8,128)(2,1)S(1)}) custom-call(bf16[576,192]{1,0:T(8,128)(2,1)S(1)} %shard_map.120.y_ref, bf16[144,192]{1,0:T(8,128)(2,1)S(1)} %collective-permute-done.2.got_ref, bf16[192,768]{1,0:T(8,128)(2,1)S(1)} %copy-done.5, bf16[768,192]{1,0:T(8,128)(2,1)S(1)} %copy.15.down_ref.fine_down_ref, ...), custom_call_target="tpu_custom_call" | custom-call | flops 4000000000 | bytes 5990400 | tf_op jit(solution)/shard_map/pallas_call | solution.py:243
  59.5 1.9 %collective-permute-start.3 = (bf16[2,3,12,384]{3,2,1,0:T(8,128)(2,1)S(1)}, bf16[2,3,12,384]{3,2,1,0:T(8,128)(2,1)S(1)}, u32[]{:S(2)}, u32[]{:S(2)}) collective-permute-start(bf16[2,3,12,384]{3,2,1,0:T(8,128)(2,1)S(1)} %get-tuple-element.15), channel_id=1, source_target_pairs={{0,1},{1,2},{2,3},{3,4},{4,5},{5,6},{6,7},{7,0},{8,9},{9,10},{10,1... | collective-permute-start | bytes 165896 | tf_op jit(solution)/shard_map/ppermute | solution.py:27
  61.4 17.4 %collective-permute-done.3 = bf16[2,3,12,384]{3,2,1,0:T(8,128)(2,1)S(1)} collective-permute-done((bf16[2,3,12,384]{3,2,1,0:T(8,128)(2,1)S(1)}, bf16[2,3,12,384]{3,2,1,0:T(8,128)(2,1)S(1)}, u32[]{:S(2)}, u32[]{:S(2)}) %collective-permute-start.3) | collective-permute-done | bytes 55328 | tf_op jit(solution)/shard_map/ppermute | solution.py:27
  78.9 2.0 %collective-permute-start.4 = (bf16[2,6,6,384]{3,2,1,0:T(8,128)(2,1)S(1)}, bf16[2,6,6,384]{3,2,1,0:T(8,128)(2,1)S(1)}, u32[]{:S(2)}, u32[]{:S(2)}) collective-permute-start(bf16[2,6,6,384]{3,2,1,0:T(8,128)(2,1)S(1)} %get-tuple-element.17), channel_id=1, source_target_pairs={{0,8},{8,16},{16,24},{24,32},{32,40},{40,48},{48,56},{56,64},{64,7... | collective-permute-start | bytes 165896 | tf_op jit(solution)/shard_map/ppermute | solution.py:27
  80.9 5.8 %collective-permute-done.4 = bf16[2,6,6,384]{3,2,1,0:T(8,128)(2,1)S(1)} collective-permute-done((bf16[2,6,6,384]{3,2,1,0:T(8,128)(2,1)S(1)}, bf16[2,6,6,384]{3,2,1,0:T(8,128)(2,1)S(1)}, u32[]{:S(2)}, u32[]{:S(2)}) %collective-permute-start.4) | collective-permute-done | bytes 55328 | tf_op jit(solution)/shard_map/ppermute | solution.py:27
  86.7 0.1 pad_maximum_fusion.1
  86.8 0.7 copy.17
  (14 shorter events, 0.1 us)
Async XLA Ops:
  0.0 24.6 %slice-start = ((bf16[2,12,24,192]{3,2,1,0:T(8,128)(2,1)}), bf16[2,9,24,192]{3,2,1,0:T(8,128)(2,1)S(1)}, s32[]{:S(2)}) async-start(bf16[2,12,24,192]{3,2,1,0:T(8,128)(2,1)} %own_ref.1), calls=%async_computation | async-start | bytes 442368 | tf_op jit(solution)/shard_map/slice | solution.py:274
  0.0 20.2 %copy-start.9 = (bf16[768,192]{0,1:T(8,128)(2,1)S(1)}, bf16[768,192]{0,1:T(8,128)(2,1)}, u32[]{:S(2)}) copy-start(bf16[768,192]{0,1:T(8,128)(2,1)} %param.17) | copy-start | bytes 884740
  1.0 23.7 %collective-permute-start = (bf16[2,3,24,192]{3,2,1,0:T(8,128)(2,1)S(1)}, bf16[2,3,24,192]{3,2,1,0:T(8,128)(2,1)S(1)}, u32[]{:S(2)}, u32[]{:S(2)}) collective-permute-start(bf16[2,3,24,192]{3,2,1,0:T(8,128)(2,1)S(1)} %slice.12), channel_id=1, source_target_pairs={{0,7},{1,0},{2,1},{3,2},{4,3},{5,4},{6,5},{7,6},{8,15},{9,8},{10,9... | collective-permute-start | bytes 165896 | tf_op jit(solution)/shard_map/ppermute | solution.py:27
  24.7 7.7 %collective-permute-start.1 = (bf16[2,12,24,192]{3,2,1,0:T(8,128)(2,1)S(1)}, bf16[2,12,24,192]{3,2,1,0:T(8,128)(2,1)S(1)}, u32[]{:S(2)}, u32[]{:S(2)}) collective-permute-start(bf16[2,12,24,192]{3,2,1,0:T(8,128)(2,1)S(1)} %pad_maximum_fusion), channel_id=1, source_target_pairs={{0,504},{8,0},{16,8},{24,16},{32,24},{40,32},{48,40},{56,48},{64,5... | collective-permute-start | bytes 663560 | tf_op jit(solution)/shard_map/ppermute | solution.py:27
  28.1 4.2 %copy-start = (bf16[2,12,24,192]{3,2,1,0:T(8,128)(2,1)S(1)}, bf16[2,12,24,192]{3,2,1,0:T(8,128)(2,1)}, u32[]{:S(2)}) copy-start(bf16[2,12,24,192]{3,2,1,0:T(8,128)(2,1)} %own_ref.1) | copy-start | bytes 663556
  28.1 4.2 %copy-start.7 = (bf16[192,576]{1,0:T(8,128)(2,1)S(1)}, bf16[192,576]{1,0:T(8,128)(2,1)}, u32[]{:S(2)}) copy-start(bf16[192,576]{1,0:T(8,128)(2,1)} %qkv_ref.2) | copy-start | bytes 663556
  28.1 4.2 %copy-start.8 = (bf16[192,192]{1,0:T(8,128)(2,1)S(1)}, bf16[192,192]{1,0:T(8,128)(2,1)}, u32[]{:S(2)}) copy-start(bf16[192,192]{1,0:T(8,128)(2,1)} %proj_ref.2) | copy-start | bytes 221188
  32.3 18.3 %copy-start.5 = (bf16[192,768]{1,0:T(8,128)(2,1)S(1)}, bf16[192,768]{1,0:T(8,128)(2,1)}, u32[]{:S(2)}) copy-start(bf16[192,768]{1,0:T(8,128)(2,1)} %fine_up_ref.1) | copy-start | bytes 884740
  35.4 20.0 %collective-permute-start.2 = (bf16[144,192]{1,0:T(8,128)(2,1)S(1)}, bf16[144,192]{1,0:T(8,128)(2,1)S(1)}, u32[]{:S(2)}, u32[]{:S(2)}) collective-permute-start(bf16[144,192]{1,0:T(8,128)(2,1)S(1)} %get-tuple-element.13), channel_id=1, source_target_pairs={{0,7},{1,0},{2,1},{3,2},{4,3},{5,4},{6,5},{7,6},{8,15},{9,8},{10,9... | collective-permute-start | bytes 165896 | tf_op jit(solution)/shard_map/ppermute | solution.py:27
  50.6 4.8 %copy-start.1 = (bf16[384,1536]{1,0:T(8,128)(2,1)S(1)}, bf16[384,1536]{1,0:T(8,128)(2,1)}, u32[]{:S(2)}) copy-start(bf16[384,1536]{1,0:T(8,128)(2,1)} %up_ref.3) | copy-start | bytes 3538948
  50.6 4.8 %copy-start.2 = (bf16[1536,384]{1,0:T(8,128)(2,1)S(1)}, bf16[1536,384]{1,0:T(8,128)(2,1)}, u32[]{:S(2)}) copy-start(bf16[1536,384]{1,0:T(8,128)(2,1)} %down_ref.2) | copy-start | bytes 3538948
  50.6 4.8 %copy-start.3 = (bf16[384,1152]{1,0:T(8,128)(2,1)S(1)}, bf16[384,1152]{1,0:T(8,128)(2,1)}, u32[]{:S(2)}) copy-start(bf16[384,1152]{1,0:T(8,128)(2,1)} %qkv_ref.3) | copy-start | bytes 2654212
  50.6 4.8 %copy-start.4 = (bf16[768,384]{1,0:T(8,128)(2,1)S(1)}, bf16[768,384]{1,0:T(8,128)(2,1)}, u32[]{:S(2)}) copy-start(bf16[768,384]{1,0:T(8,128)(2,1)} %merge_ref.1) | copy-start | bytes 1769476
  50.7 4.8 %copy-start.6 = (bf16[384,384]{1,0:T(8,128)(2,1)S(1)}, bf16[384,384]{1,0:T(8,128)(2,1)}, u32[]{:S(2)}) copy-start(bf16[384,384]{1,0:T(8,128)(2,1)} %proj_ref.3) | copy-start | bytes 884740
  59.5 19.4 %collective-permute-start.3 = (bf16[2,3,12,384]{3,2,1,0:T(8,128)(2,1)S(1)}, bf16[2,3,12,384]{3,2,1,0:T(8,128)(2,1)S(1)}, u32[]{:S(2)}, u32[]{:S(2)}) collective-permute-start(bf16[2,3,12,384]{3,2,1,0:T(8,128)(2,1)S(1)} %get-tuple-element.15), channel_id=1, source_target_pairs={{0,1},{1,2},{2,3},{3,4},{4,5},{5,6},{6,7},{7,0},{8,9},{9,10},{10,1... | collective-permute-start | bytes 165896 | tf_op jit(solution)/shard_map/ppermute | solution.py:27
  78.9 7.8 %collective-permute-start.4 = (bf16[2,6,6,384]{3,2,1,0:T(8,128)(2,1)S(1)}, bf16[2,6,6,384]{3,2,1,0:T(8,128)(2,1)S(1)}, u32[]{:S(2)}, u32[]{:S(2)}) collective-permute-start(bf16[2,6,6,384]{3,2,1,0:T(8,128)(2,1)S(1)} %get-tuple-element.17), channel_id=1, source_target_pairs={{0,8},{8,16},{16,24},{24,32},{32,40},{40,48},{48,56},{56,64},{64,7... | collective-permute-start | bytes 165896 | tf_op jit(solution)/shard_map/ppermute | solution.py:27

commit v2 on v1

--- a/solution.py
+++ b/solution.py
@@ -22,9 +22,12 @@
 bf16 = jnp.bfloat16
 
 
-def from_behind(shard, axis, by):
-    peers = lax.axis_size(axis)
-    return lax.ppermute(shard, axis, [(i, (i + by) % peers) for i in range(peers)])
+def from_behind(shard, lon, lat):
+    lons, lats = lax.axis_size("lon"), lax.axis_size("lat")
+    pairs = [
+        (o * lats + a, (o + lon) % lons * lats + (a + lat) % lats) for o in range(lons) for a in range(lats)
+    ]
+    return lax.ppermute(shard, ("lon", "lat"), pairs)
 
 
 def normalise(values):
@@ -150,58 +153,73 @@
     return jnp.concatenate(pieces, axis=-1)[:, :width]
 
 
-def fine_attention_kernel(
-    own_ref, below_ref, right_ref, bias_ref, qkv_ref, proj_ref, out_ref, send_ref, x_ref, a_ref, w_ref, s_ref
-):
+def attend_fine(n, x_ref, bias_ref, qkv_ref, proj_ref):
+    normed = normalise(get(x_ref, 72, 432, 1, 192))
+    q = dot(normed, qkv_ref[:, 0:192]).astype(bf16).astype(f32)
+    k = dot(normed, qkv_ref[:, 192:384]).astype(bf16)
+    v = dot(normed, qkv_ref[:, 384:576]).astype(bf16)
+    left, right = [], []
+    for window, start, stop in ((0, 72, 144), (1, 0, 144), (2, 0, 72)):
+        at = window * CELLS
+        q_rows = q[at + start : at + stop]
+        k_rows, v_rows = k[at : at + CELLS], v[at : at + CELLS]
+        bias = bias_ref[n, :, start:stop, :]
+        left.append(attend_group(q_rows[:, :128], k_rows[:, :128], v_rows[:, :128], bias[:4], 4))
+        right.append(attend_group(q_rows[:, 128:], k_rows[:, 128:], v_rows[:, 128:], bias[4:], 2))
+    left = jnp.concatenate(left, axis=0).astype(bf16)
+    right = jnp.concatenate(right, axis=0).astype(bf16)
+    product = dot(left, proj_ref[0:128, :]) + dot(right, proj_ref[128:192, :])
+    return (get(x_ref, 144, 288, 1, 192) + product).astype(bf16)
+
+
+def first_rows_kernel(own_ref, right_ref, bias_ref, qkv_ref, proj_ref, out_ref, send_ref, x_ref, a_ref, s_ref):
     for z in range(WZ):
-        for rho in range(2 * WLAT):
-            n, a = divmod(rho, WLAT)
-            line = own_ref[1 - z, 3 + rho] if rho < 9 else below_ref[1 - z, rho - 9]
-            put(x_ref, n * 576 + z * WLAT + a, 24, LINES, line.astype(f32))
-            put(x_ref, n * 576 + 288 + z * WLAT + a, 24, LINES, right_ref[1 - z, rho].astype(f32))
-    for n in range(2):
-        normed = normalise(get(x_ref, n * 576 + 72, 432, 1, 192))
-        q = dot(normed, qkv_ref[:, 0:192]).astype(bf16).astype(f32)
-        k = dot(normed, qkv_ref[:, 192:384]).astype(bf16)
-        v = dot(normed, qkv_ref[:, 384:576]).astype(bf16)
-        left, right = [], []
-        for window, start, stop in ((0, 72, 144), (1, 0, 144), (2, 0, 72)):
-            at = window * CELLS
-            q_rows = q[at + start : at + stop]
-            k_rows, v_rows = k[at : at + CELLS], v[at : at + CELLS]
-            bias = bias_ref[n, :, start:stop, :]
-            left.append(attend_group(q_rows[:, :128], k_rows[:, :128], v_rows[:, :128], bias[:4], 4))
-            right.append(attend_group(q_rows[:, 128:], k_rows[:, 128:], v_rows[:, 128:], bias[4:], 2))
-        left = jnp.concatenate(left, axis=0).astype(bf16)
-        right = jnp.concatenate(right, axis=0).astype(bf16)
-        product = dot(left, proj_ref[0:128, :]) + dot(right, proj_ref[128:192, :])
-        attended = (get(x_ref, n * 576 + 144, 288, 1, 192) + product).astype(bf16).astype(f32)
-        put(a_ref, n * 288, 288, 1, attended)
+        for a in range(WLAT):
+            put(x_ref, z * WLAT + a, 24, LINES, own_ref[1 - z, 3 + a].astype(f32))
+            put(x_ref, 288 + z * WLAT + a, 24, LINES, right_ref[1 - z, 3 + a].astype(f32))
+    attended = attend_fine(0, x_ref, bias_ref, qkv_ref, proj_ref)
+    out_ref[...] = attended
+    put(a_ref, 0, 288, 1, attended.astype(f32))
     for t in range(2):
         for pb in range(2):
             for z in range(WZ):
-                for rho in range(12):
+                for a in range(3):
+                    at = (z * 3 + a) * 24 + pb * 12
+                    line = a_ref[t, pl.ds(pb * LINES + z * WLAT + a, 12, stride=24), :]
+                    s_ref[t, at : at + 12, :] = line
+    send_ref[...] = get(s_ref, 0, 144, 1, 192).astype(bf16)
+
+
+def second_rows_kernel(
+    own_ref, right_ref, below_ref, corner_ref, first_ref, bias_ref, qkv_ref, proj_ref, up_ref, down_ref,
+    out_ref, x_ref, a_ref, w_ref,
+):
+    for z in range(WZ):
+        for a in range(WLAT):
+            near = own_ref[1 - z, 9 + a] if a < 3 else below_ref[1 - z, a - 3]
+            far = right_ref[1 - z, 9 + a] if a < 3 else corner_ref[1 - z, a - 3]
+            put(x_ref, z * WLAT + a, 24, LINES, near.astype(f32))
+            put(x_ref, 288 + z * WLAT + a, 24, LINES, far.astype(f32))
+    put(a_ref, 0, 288, 1, first_ref[...].astype(f32))
+    put(a_ref, 288, 288, 1, attend_fine(1, x_ref, bias_ref, qkv_ref, proj_ref).astype(f32))
+    for t in range(2):
+        for pb in range(2):
+            for z in range(WZ):
+                for rho in range(3, 15):
                     n, a = divmod(rho, WLAT)
-                    line = a_ref[t, pl.ds(n * 288 + pb * LINES + z * WLAT + a, 12, stride=24), :]
-                    if rho < 3:
-                        at = (z * 3 + rho) * 24 + pb * 12
-                        s_ref[t, at : at + 12, :] = line
+                    if rho < 12:
+                        line = a_ref[t, pl.ds(n * 288 + pb * LINES + z * WLAT + a, 12, stride=24), :]
+                    else:
                         line = jnp.zeros((12, 128), f32)
-                        rho += 12
                     w_ref[t, pl.ds(pb * 288 + z * 12 + rho - 3, 12, stride=24), :] = line
-    out_ref[...] = get(w_ref, 0, 576, 1, 192).astype(bf16)
-    send_ref[...] = get(s_ref, 0, 144, 1, 192).astype(bf16)
-
-
-def fine_feed_forward_kernel(a_ref, up_ref, down_ref, out_ref):
     for i in range(4):
-        rows = slice(i * 144, (i + 1) * 144)
-        out_ref[rows, :] = feed_forward(a_ref[rows, :].astype(f32), up_ref, down_ref).astype(bf16)
+        x = get(w_ref, i * 144, 144, 1, 192)
+        out_ref[i * 144 : (i + 1) * 144, :] = feed_forward(x, up_ref, down_ref).astype(bf16)
 
 
 def coarse_kernel(
     y_ref, got_ref, fine_up_ref, fine_down_ref, merge_ref, bias_ref, qkv_ref, proj_ref, up_ref, down_ref,
-    keep_ref, send_ref, w_ref, r_ref, o_ref,
+    keep_ref, down_row_ref, right_column_ref, corner_ref, w_ref, r_ref, o_ref,
 ):
     put(r_ref, 0, 144, 1, feed_forward(got_ref[...].astype(f32), fine_up_ref, fine_down_ref))
     put(w_ref, 0, 576, 1, y_ref[...].astype(f32))
@@ -233,8 +251,21 @@
     put(o_ref, 0, CELLS, 1, feed_forward(attended, up_ref, down_ref))
     for z in range(WZ):
         for i in range(3):
-            keep_ref[1 - z, i] = get(o_ref, z * WLAT + i, WLON, LINES, 384).astype(bf16)
-            send_ref[1 - z, i] = get(o_ref, z * WLAT + 3 + i, WLON, LINES, 384).astype(bf16)
+            upper = get(o_ref, z * WLAT + i, WLON, LINES, 384)
+            lower = get(o_ref, z * WLAT + 3 + i, WLON, LINES, 384)
+            keep_ref[1 - z, i] = upper[:6].astype(bf16)
+            right_column_ref[1 - z, i] = upper[6:].astype(bf16)
+            down_row_ref[1 - z, i] = lower[:6].astype(bf16)
+            corner_ref[1 - z, i] = lower[6:].astype(bf16)
+
+
+def assemble_kernel(keep_ref, above_ref, left_ref, corner_ref, out_ref):
+    for z in range(WZ):
+        for i in range(3):
+            upper = [corner_ref[z, i].astype(f32), above_ref[z, i].astype(f32)]
+            lower = [left_ref[z, i].astype(f32), keep_ref[z, i].astype(f32)]
+            out_ref[z, i] = jnp.concatenate(upper, axis=0).astype(bf16)
+            out_ref[z, 3 + i] = jnp.concatenate(lower, axis=0).astype(bf16)
 
 
 def call(kernel, outs, scratch, operands, flops, smem=0):
@@ -270,8 +301,10 @@
     coarse_down,
 ):
     last = (lax.axis_index("lat") == lax.axis_size("lat") - 1).astype(jnp.int32).reshape(1)
-    below = from_behind(fields[:, :3], "lat", -1)
-    right = from_behind(jnp.concatenate([fields[:, 3:], below], axis=1), "lon", -1)
+    right = from_behind(fields, -1, 0)
+    top = fields[:, :3]
+    below = from_behind(top, 0, -1)
+    corner = from_behind(top, -1, -1)
     bias1, bias2 = call(
         bias_kernel,
         [((2, 6, CELLS, CELLS), f32), ((12, CELLS, CELLS), f32)],
@@ -280,28 +313,39 @@
         3_000_000_000,
         smem=1,
     )
-    attended, edge = call(
-        fine_attention_kernel,
-        [((576, 192), bf16), ((144, 192), bf16)],
-        [tiles_of(1152, 192), tiles_of(576, 192), tiles_of(576, 192), tiles_of(144, 192)],
-        [fields, below, right, bias1, fine_qkv, fine_proj],
-        2_000_000_000,
-    )
-    got = from_behind(edge, "lat", -1)
+    first, edge = call(
+        first_rows_kernel,
+        [((288, 192), bf16), ((144, 192), bf16)],
+        [tiles_of(576, 192), tiles_of(288, 192), tiles_of(144, 192)],
+        [fields, right, bias1, fine_qkv, fine_proj],
+        1_000_000_000,
+    )
+    got = from_behind(edge, 0, -1)
     (finished,) = call(
-        fine_feed_forward_kernel, [((576, 192), bf16)], [], [attended, fine_up, fine_down], 3_000_000_000
-    )
-    keep, send = call(
+        second_rows_kernel,
+        [((576, 192), bf16)],
+        [tiles_of(576, 192), tiles_of(576, 192), tiles_of(576, 192)],
+        [fields, right, below, corner, first, bias1, fine_qkv, fine_proj, fine_up, fine_down],
+        3_000_000_000,
+    )
+    quarter = ((2, 3, 6, 384), bf16)
+    keep, down_row, right_column, far_corner = call(
         coarse_kernel,
-        [((2, 3, 12, 384), bf16), ((2, 3, 12, 384), bf16)],
+        [quarter] * 4,
         [tiles_of(576, 192), tiles_of(144, 192), tiles_of(CELLS, 384)],
         [finished, got, fine_up, fine_down, merge_weight, bias2, coarse_qkv, coarse_proj, coarse_up, coarse_down],
         4_000_000_000,
     )
-    above = from_behind(send, "lat", 1)
-    rows = jnp.concatenate([above, keep], axis=1)
-    arrived = from_behind(rows[:, :, 6:], "lon", 1)
-    return jnp.concatenate([arrived, rows[:, :, :6]], axis=2)
+    above = from_behind(down_row, 0, 1)
+    corner = from_behind(far_corner, 1, 1)
+    left = from_behind(right_column, 1, 0)
+    return pl.pallas_call(
+        assemble_kernel,
+        out_shape=jax.ShapeDtypeStruct((2, 6, 12, 384), bf16),
+        grid=(1,),
+        in_specs=[pl.BlockSpec((2, 3, 6, 384), lambda i: (0, 0, 0, 0))] * 4,
+        out_specs=pl.BlockSpec((2, 6, 12, 384), lambda i: (0, 0, 0, 0)),
+    )(keep, above, left, corner)
 
 
 def solution(mesh):

time: 87.8 us -> 77.9 us (0.89)
  the two profiles are of different devices: /device:TPU:32 before, /device:TPU:16 now
where the time goes in v2:
time: 77.9 us; the launch traced here: 77.4 us
  starting transfers between devices  43.9 us (56%)
  Pallas kernels  13.3 us (17%)
  waiting for transfers between devices  13 us (17%)
  local copies, waits for them, and re-layouts  6.92 us (9%)
    ppermute x7, starting transfers between devices, from_behind(): return lax.ppermute(shard, ('lon', 'lat'), pairs)  43.9 us
    ppermute x7, waiting for transfers between devices, from_behind(): return lax.ppermute(shard, ('lon', 'lat'), pairs)  13 us
    pallas_call x4, Pallas kernels, call(): pl.pallas_call(kernel, out_shape=[jax.ShapeDtypeStruct(shape, dtype) for...  11.8 us
    unnamed x29, local copies, waits for them, and re-layouts  4.38 us
    pallas_call x1, local copies, waits for them, and re-layouts, body(): pl.pallas_call(assemble_kernel, out_shape=jax.ShapeDtypeStruct((2, 6, 12,...  1.64 us
  transfers between devices with their start and end apart: 7, of which 2 were waited for; matrix products, arithmetic and copies ran while one was open for 5% of the time, Pallas kernels for 10%

profile of v2, /device:TPU:16, one launch (start us, length us, event | category | flops | bytes accessed | tf_op | source)
XLA Modules:
  0.0 77.4 jit_solution(13893864709511165222)
XLA Ops:
  0.0 14.8 %collective-permute-start = (bf16[2,12,24,192]{3,2,1,0:T(8,128)(2,1)}, bf16[2,12,24,192]{3,2,1,0:T(8,128)(2,1)S(1)}, u32[]{:S(2)}, u32[]{:S(2)}) collective-permute-start(bf16[2,12,24,192]{3,2,1,0:T(8,128)(2,1)} %own_ref.3), channel_id=1, source_target_pairs={{0,504},{1,505},{2,506},{3,507},{4,508},{5,509},{6,510},{7,511},{8... | collective-permute-start | bytes 663560 | tf_op jit(solution)/shard_map/ppermute | solution.py:30
  14.8 0.9 %slice.3 = bf16[2,3,24,192]{3,2,1,0:T(8,128)(2,1)S(1)} slice(bf16[2,12,24,192]{3,2,1,0:T(8,128)(2,1)} %own_ref.3), slice={[0:2], [0:3], [0:24], [0:192]} | slice | bytes 110592 | tf_op jit(solution)/shard_map/slice | solution.py:305
  15.7 2.3 %collective-permute-start.1 = (bf16[2,3,24,192]{3,2,1,0:T(8,128)(2,1)S(1)}, bf16[2,3,24,192]{3,2,1,0:T(8,128)(2,1)S(1)}, u32[]{:S(2)}, u32[]{:S(2)}) collective-permute-start(bf16[2,3,24,192]{3,2,1,0:T(8,128)(2,1)S(1)} %slice.3), channel_id=1, source_target_pairs={{0,7},{1,0},{2,1},{3,2},{4,3},{5,4},{6,5},{7,6},{8,15},{9,8},{10,9... | collective-permute-start | bytes 165896 | tf_op jit(solution)/shard_map/ppermute | solution.py:30
  18.0 2.2 %collective-permute-start.2 = (bf16[2,3,24,192]{3,2,1,0:T(8,128)(2,1)S(1)}, bf16[2,3,24,192]{3,2,1,0:T(8,128)(2,1)S(1)}, u32[]{:S(2)}, u32[]{:S(2)}) collective-permute-start(bf16[2,3,24,192]{3,2,1,0:T(8,128)(2,1)S(1)} %slice.3), channel_id=1, source_target_pairs={{0,511},{1,504},{2,505},{3,506},{4,507},{5,508},{6,509},{7,510},{8... | collective-permute-start | bytes 165896 | tf_op jit(solution)/shard_map/ppermute | solution.py:30
  20.2 1.0 %copy.13.fine_ref = f32[2,1,6,23,144]{4,3,2,1,0:T(8,128)S(1)} copy(f32[2,1,6,23,144]{4,1,3,2,0:T(1,128)} %param.13) | data formatting | bytes 317952 | tf_op args[1]
  21.2 1.0 %copy.14.coarse_ref = f32[1,1,12,23,144]{4,3,2,1,0:T(8,128)S(1)} copy(f32[1,1,12,23,144]{4,1,3,2,0:T(1,128)} %param.19) | data formatting | bytes 317952 | tf_op args[7]
  22.2 1.1 %copy.15.down_ref.fine_down_ref = bf16[768,192]{1,0:T(8,128)(2,1)S(1)} copy(bf16[768,192]{0,1:T(8,128)(2,1)} %param.17) | data formatting | bytes 589824 | tf_op args[5]
  23.4 0.0 copy-start.1
  23.4 0.0 copy-start.8
  23.4 0.0 copy-start.9
  23.4 3.5 %shard_map.118 = (f32[2,6,144,144]{3,2,1,0:T(8,128)S(1)}, f32[12,144,144]{2,1,0:T(8,128)S(1)}) custom-call(s32[1]{0:T(128)} %bitcast.last_ref, f32[2,1,6,23,144]{4,3,2,1,0:T(8,128)S(1)} %copy.13.fine_ref, f32[1,1,12,23,144]{4,3,2,1,0:T(8,128)S(1)} %copy.14.coarse_ref), custom_call_target="tpu_custom_call" | custom-call | flops 3000000000 | bytes 317956 | tf_op jit(solution)/shard_map/pallas_call | solution.py:274
  26.9 0.0 copy-start.6
  26.9 1.7 %shard_map.119 = (bf16[288,192]{1,0:T(8,128)(2,1)S(1)}, bf16[144,192]{1,0:T(8,128)(2,1)S(1)}) custom-call(bf16[2,12,24,192]{3,2,1,0:T(8,128)(2,1)S(1)} %copy-done.1, bf16[2,12,24,192]{3,2,1,0:T(8,128)(2,1)S(1)} %collective-permute-done.right_ref, f32[2,6,144,144]{3,2,1,0:T(8,128)S(1)} %get-tuple-element.13.bias_ref, bf16[192,576]{1,0:T(8,128)(2,1)S(1)} %copy-done.8, ...), custom_call_target="tpu_custom_call" | custom-call | flops 1000000000 | bytes 1732608 | tf_op jit(solution)/shard_map/pallas_call | solution.py:274
  28.6 10.7 %collective-permute-start.3 = (bf16[144,192]{1,0:T(8,128)(2,1)S(1)}, bf16[144,192]{1,0:T(8,128)(2,1)S(1)}, u32[]{:S(2)}, u32[]{:S(2)}) collective-permute-start(bf16[144,192]{1,0:T(8,128)(2,1)S(1)} %get-tuple-element.15), channel_id=1, source_target_pairs={{0,7},{1,0},{2,1},{3,2},{4,3},{5,4},{6,5},{7,6},{8,15},{9,8},{10,9... | collective-permute-start | bytes 165896 | tf_op jit(solution)/shard_map/ppermute | solution.py:30
  39.3 0.0 copy-start.2
  39.3 0.0 copy-start.3
  39.3 0.0 copy-start.4
  39.3 0.0 copy-start.5
  39.3 0.0 copy-start.7
  39.4 2.7 %shard_map.120.y_ref = bf16[576,192]{1,0:T(8,128)(2,1)S(1)} custom-call(bf16[2,12,24,192]{3,2,1,0:T(8,128)(2,1)S(1)} %copy-done.1, bf16[2,12,24,192]{3,2,1,0:T(8,128)(2,1)S(1)} %collective-permute-done.right_ref, bf16[2,3,24,192]{3,2,1,0:T(8,128)(2,1)S(1)} %collective-permute-done.1.below_ref, bf16[2,3,24,192]{3,2,1,0:T(8,128)(2,1)S(1)} %collective-permute-done.2.corner_ref, ...), custom_call_target="tpu_custom_call" | custom-call | flops 3000000000 | bytes 2543616 | tf_op jit(solution)/shard_map/pallas_call | solution.py:274
  42.1 0.0 collective-permute-done.3.got_ref
  42.1 4.0 %shard_map.121 = (bf16[2,3,6,384]{3,2,1,0:T(8,128)(2,1)S(1)}, bf16[2,3,6,384]{3,2,1,0:T(8,128)(2,1)S(1)}, bf16[2,3,6,384]{3,2,1,0:T(8,128)(2,1)S(1)}, bf16[2,3,6,384]{3,2,1,0:T(8,128)(2,1)S(1)}) custom-call(bf16[576,192]{1,0:T(8,128)(2,1)S(1)} %shard_map.120.y_ref, bf16[144,192]{1,0:T(8,128)(2,1)S(1)} %collective-permute-done.3.got_ref, ...), custom_call_target="tpu_custom_call" | custom-call | flops 4000000000 | bytes 5990400 | tf_op jit(solution)/shard_map/pallas_call | solution.py:274
  46.1 0.0 copy-start
  46.2 0.6 copy-done
  46.8 10.0 %collective-permute-start.4 = (bf16[2,3,6,384]{3,2,1,0:T(8,128)(2,1)S(1)}, bf16[2,3,6,384]{3,2,1,0:T(8,128)(2,1)S(1)}, u32[]{:S(2)}, u32[]{:S(2)}) collective-permute-start(bf16[2,3,6,384]{3,2,1,0:T(8,128)(2,1)S(1)} %get-tuple-element.18), channel_id=1, source_target_pairs={{0,1},{1,2},{2,3},{3,4},{4,5},{5,6},{6,7},{7,0},{8,9},{9,10},{10,1... | collective-permute-start | bytes 82952 | tf_op jit(solution)/shard_map/ppermute | solution.py:30
  56.8 1.9 %collective-permute-start.5 = (bf16[2,3,6,384]{3,2,1,0:T(8,128)(2,1)S(1)}, bf16[2,3,6,384]{3,2,1,0:T(8,128)(2,1)S(1)}, u32[]{:S(2)}, u32[]{:S(2)}) collective-permute-start(bf16[2,3,6,384]{3,2,1,0:T(8,128)(2,1)S(1)} %get-tuple-element.19), channel_id=1, source_target_pairs={{0,8},{1,9},{2,10},{3,11},{4,12},{5,13},{6,14},{7,15},{8,16},{9,17... | collective-permute-start | bytes 82952 | tf_op jit(solution)/shard_map/ppermute | solution.py:30
  58.7 1.9 %collective-permute-start.6 = (bf16[2,3,6,384]{3,2,1,0:T(8,128)(2,1)S(1)}, bf16[2,3,6,384]{3,2,1,0:T(8,128)(2,1)S(1)}, u32[]{:S(2)}, u32[]{:S(2)}) collective-permute-start(bf16[2,3,6,384]{3,2,1,0:T(8,128)(2,1)S(1)} %get-tuple-element.20), channel_id=1, source_target_pairs={{0,9},{1,10},{2,11},{3,12},{4,13},{5,14},{6,15},{7,8},{8,17},{9,18... | collective-permute-start | bytes 82952 | tf_op jit(solution)/shard_map/ppermute | solution.py:30
  60.7 10.1 %collective-permute-done.5.left_ref = bf16[2,3,6,384]{3,2,1,0:T(8,128)(2,1)S(1)} collective-permute-done((bf16[2,3,6,384]{3,2,1,0:T(8,128)(2,1)S(1)}, bf16[2,3,6,384]{3,2,1,0:T(8,128)(2,1)S(1)}, u32[]{:S(2)}, u32[]{:S(2)}) %collective-permute-start.5) | collective-permute-done | bytes 27680 | tf_op jit(solution)/shard_map/ppermute | solution.py:30
  70.8 2.8 %collective-permute-done.6.corner_ref = bf16[2,3,6,384]{3,2,1,0:T(8,128)(2,1)S(1)} collective-permute-done((bf16[2,3,6,384]{3,2,1,0:T(8,128)(2,1)S(1)}, bf16[2,3,6,384]{3,2,1,0:T(8,128)(2,1)S(1)}, u32[]{:S(2)}, u32[]{:S(2)}) %collective-permute-start.6) | collective-permute-done | bytes 27680 | tf_op jit(solution)/shard_map/ppermute | solution.py:30
  73.6 0.6 copy-done.12
  74.2 1.5 %shard_map.122 = bf16[2,6,12,384]{3,2,1,0:T(8,128)(2,1)} custom-call(bf16[2,3,6,384]{3,2,1,0:T(8,128)(2,1)} %copy-done, bf16[2,3,6,384]{3,2,1,0:T(8,128)(2,1)} %copy-done.10, bf16[2,3,6,384]{3,2,1,0:T(8,128)(2,1)} %copy-done.11, bf16[2,3,6,384]{3,2,1,0:T(8,128)(2,1)} %copy-done.12), custom_call_target="tpu_custom_call" | custom-call | tf_op jit(solution)/shard_map/pallas_call | solution.py:342
  75.7 1.6 %copy.17 = bf16[2,6,12,384]{3,0,2,1:T(2,128)(2,1)} copy(bf16[2,6,12,384]{3,2,1,0:T(8,128)(2,1)} %shard_map.122) | data formatting | bytes 221184 | tf_op jit(solution)/shard_map/pallas_call | solution.py:342
  (18 shorter events, 0.0 us)
Async XLA Ops:
  0.0 26.9 %collective-permute-start = (bf16[2,12,24,192]{3,2,1,0:T(8,128)(2,1)}, bf16[2,12,24,192]{3,2,1,0:T(8,128)(2,1)S(1)}, u32[]{:S(2)}, u32[]{:S(2)}) collective-permute-start(bf16[2,12,24,192]{3,2,1,0:T(8,128)(2,1)} %own_ref.3), channel_id=1, source_target_pairs={{0,504},{1,505},{2,506},{3,507},{4,508},{5,509},{6,510},{7,511},{8... | collective-permute-start | bytes 663560 | tf_op jit(solution)/shard_map/ppermute | solution.py:30
  15.7 23.6 %collective-permute-start.1 = (bf16[2,3,24,192]{3,2,1,0:T(8,128)(2,1)S(1)}, bf16[2,3,24,192]{3,2,1,0:T(8,128)(2,1)S(1)}, u32[]{:S(2)}, u32[]{:S(2)}) collective-permute-start(bf16[2,3,24,192]{3,2,1,0:T(8,128)(2,1)S(1)} %slice.3), channel_id=1, source_target_pairs={{0,7},{1,0},{2,1},{3,2},{4,3},{5,4},{6,5},{7,6},{8,15},{9,8},{10,9... | collective-permute-start | bytes 165896 | tf_op jit(solution)/shard_map/ppermute | solution.py:30
  18.0 21.2 %collective-permute-start.2 = (bf16[2,3,24,192]{3,2,1,0:T(8,128)(2,1)S(1)}, bf16[2,3,24,192]{3,2,1,0:T(8,128)(2,1)S(1)}, u32[]{:S(2)}, u32[]{:S(2)}) collective-permute-start(bf16[2,3,24,192]{3,2,1,0:T(8,128)(2,1)S(1)} %slice.3), channel_id=1, source_target_pairs={{0,511},{1,504},{2,505},{3,506},{4,507},{5,508},{6,509},{7,510},{8... | collective-permute-start | bytes 165896 | tf_op jit(solution)/shard_map/ppermute | solution.py:30
  23.4 3.5 %copy-start.1 = (bf16[2,12,24,192]{3,2,1,0:T(8,128)(2,1)S(1)}, bf16[2,12,24,192]{3,2,1,0:T(8,128)(2,1)}, u32[]{:S(2)}) copy-start(bf16[2,12,24,192]{3,2,1,0:T(8,128)(2,1)} %own_ref.3) | copy-start | bytes 663556
  23.4 3.5 %copy-start.8 = (bf16[192,576]{1,0:T(8,128)(2,1)S(1)}, bf16[192,576]{1,0:T(8,128)(2,1)}, u32[]{:S(2)}) copy-start(bf16[192,576]{1,0:T(8,128)(2,1)} %qkv_ref.4) | copy-start | bytes 663556
  23.4 3.5 %copy-start.9 = (bf16[192,192]{1,0:T(8,128)(2,1)S(1)}, bf16[192,192]{1,0:T(8,128)(2,1)}, u32[]{:S(2)}) copy-start(bf16[192,192]{1,0:T(8,128)(2,1)} %proj_ref.4) | copy-start | bytes 221188
  26.9 12.4 %copy-start.6 = (bf16[192,768]{1,0:T(8,128)(2,1)S(1)}, bf16[192,768]{1,0:T(8,128)(2,1)}, u32[]{:S(2)}) copy-start(bf16[192,768]{1,0:T(8,128)(2,1)} %fine_up_ref.1) | copy-start | bytes 884740
  28.6 13.5 %collective-permute-start.3 = (bf16[144,192]{1,0:T(8,128)(2,1)S(1)}, bf16[144,192]{1,0:T(8,128)(2,1)S(1)}, u32[]{:S(2)}, u32[]{:S(2)}) collective-permute-start(bf16[144,192]{1,0:T(8,128)(2,1)S(1)} %get-tuple-element.15), channel_id=1, source_target_pairs={{0,7},{1,0},{2,1},{3,2},{4,3},{5,4},{6,5},{7,6},{8,15},{9,8},{10,9... | collective-permute-start | bytes 165896 | tf_op jit(solution)/shard_map/ppermute | solution.py:30
  39.3 2.8 %copy-start.2 = (bf16[384,1536]{1,0:T(8,128)(2,1)S(1)}, bf16[384,1536]{1,0:T(8,128)(2,1)}, u32[]{:S(2)}) copy-start(bf16[384,1536]{1,0:T(8,128)(2,1)} %up_ref.3) | copy-start | bytes 3538948
  39.3 2.8 %copy-start.3 = (bf16[1536,384]{1,0:T(8,128)(2,1)S(1)}, bf16[1536,384]{1,0:T(8,128)(2,1)}, u32[]{:S(2)}) copy-start(bf16[1536,384]{1,0:T(8,128)(2,1)} %down_ref.2) | copy-start | bytes 3538948
  39.3 2.8 %copy-start.4 = (bf16[384,1152]{1,0:T(8,128)(2,1)S(1)}, bf16[384,1152]{1,0:T(8,128)(2,1)}, u32[]{:S(2)}) copy-start(bf16[384,1152]{1,0:T(8,128)(2,1)} %qkv_ref.5) | copy-start | bytes 2654212
  39.3 2.8 %copy-start.5 = (bf16[768,384]{1,0:T(8,128)(2,1)S(1)}, bf16[768,384]{1,0:T(8,128)(2,1)}, u32[]{:S(2)}) copy-start(bf16[768,384]{1,0:T(8,128)(2,1)} %merge_ref.1) | copy-start | bytes 1769476
  39.3 2.8 %copy-start.7 = (bf16[384,384]{1,0:T(8,128)(2,1)S(1)}, bf16[384,384]{1,0:T(8,128)(2,1)}, u32[]{:S(2)}) copy-start(bf16[384,384]{1,0:T(8,128)(2,1)} %proj_ref.5) | copy-start | bytes 884740
  46.1 0.6 copy-start
  46.8 13.9 %collective-permute-start.4 = (bf16[2,3,6,384]{3,2,1,0:T(8,128)(2,1)S(1)}, bf16[2,3,6,384]{3,2,1,0:T(8,128)(2,1)S(1)}, u32[]{:S(2)}, u32[]{:S(2)}) collective-permute-start(bf16[2,3,6,384]{3,2,1,0:T(8,128)(2,1)S(1)} %get-tuple-element.18), channel_id=1, source_target_pairs={{0,1},{1,2},{2,3},{3,4},{4,5},{5,6},{6,7},{7,0},{8,9},{9,10},{10,1... | collective-permute-start | bytes 82952 | tf_op jit(solution)/shard_map/ppermute | solution.py:30
  56.8 14.0 %collective-permute-start.5 = (bf16[2,3,6,384]{3,2,1,0:T(8,128)(2,1)S(1)}, bf16[2,3,6,384]{3,2,1,0:T(8,128)(2,1)S(1)}, u32[]{:S(2)}, u32[]{:S(2)}) collective-permute-start(bf16[2,3,6,384]{3,2,1,0:T(8,128)(2,1)S(1)} %get-tuple-element.19), channel_id=1, source_target_pairs={{0,8},{1,9},{2,10},{3,11},{4,12},{5,13},{6,14},{7,15},{8,16},{9,17... | collective-permute-start | bytes 82952 | tf_op jit(solution)/shard_map/ppermute | solution.py:30
  58.7 14.9 %collective-permute-start.6 = (bf16[2,3,6,384]{3,2,1,0:T(8,128)(2,1)S(1)}, bf16[2,3,6,384]{3,2,1,0:T(8,128)(2,1)S(1)}, u32[]{:S(2)}, u32[]{:S(2)}) collective-permute-start(bf16[2,3,6,384]{3,2,1,0:T(8,128)(2,1)S(1)} %get-tuple-element.20), channel_id=1, source_target_pairs={{0,9},{1,10},{2,11},{3,12},{4,13},{5,14},{6,15},{7,8},{8,17},{9,18... | collective-permute-start | bytes 82952 | tf_op jit(solution)/shard_map/ppermute | solution.py:30
  60.7 13.0 %copy-start.10 = (bf16[2,3,6,384]{3,2,1,0:T(8,128)(2,1)}, bf16[2,3,6,384]{3,2,1,0:T(8,128)(2,1)S(1)}, u32[]{:S(2)}) copy-start(bf16[2,3,6,384]{3,2,1,0:T(8,128)(2,1)S(1)} %collective-permute-done.4.above_ref) | copy-start | bytes 82948
  70.8 2.8 %copy-start.11 = (bf16[2,3,6,384]{3,2,1,0:T(8,128)(2,1)}, bf16[2,3,6,384]{3,2,1,0:T(8,128)(2,1)S(1)}, u32[]{:S(2)}) copy-start(bf16[2,3,6,384]{3,2,1,0:T(8,128)(2,1)S(1)} %collective-permute-done.5.left_ref) | copy-start | bytes 82948
  73.6 0.6 copy-start.12

commit v3 on v2

--- a/solution.py
+++ b/solution.py
@@ -53,6 +53,11 @@
     return (x + dot(hidden, down_ref[...])).astype(bf16).astype(f32)
 
 
+def fine_feed_forward(x, up_ref, down_ref):
+    hidden = gelu(dot(normalise(x), up_ref[...])).astype(bf16)
+    return (x + dot_nt(hidden, down_ref[...])).astype(bf16).astype(f32)
+
+
 def three_parts(x):
     high = x.astype(bf16)
     rest = x - high.astype(f32)
@@ -65,7 +70,7 @@
     return lax.broadcasted_iota(jnp.int32, shape, axis)
 
 
-def bias_kernel(last_ref, fine_ref, coarse_ref, fine_out, coarse_out, stacked, spread_from):
+def expand_bias(tables, outs, stacked, spread_from):
     stacked[...] = jnp.zeros_like(stacked)
     spread_from[...] = jnp.zeros_like(spread_from)
     row = iota((CELLS, CELLS), 0)
@@ -79,8 +84,7 @@
     row, lane = iota((6 * LINES, 384), 0) % LINES, iota((6 * LINES, 384), 1) % LINES
     levels_differ = row // WLAT != lane // WLAT
     rows_differ = (row % WLAT >= WLAT // 2) != (lane % WLAT >= WLAT // 2)
-
-    def expand(table_of, out_of, last):
+    for (table_of, last), out_of in zip(tables, outs, strict=True):
         for head in range(6):
             stacked[head * 24 : head * 24 + SPAN, :] = table_of(head)
         picked = sum(dot_nt(pick, part) for part in three_parts(stacked[...]))
@@ -90,10 +94,7 @@
                     key * LINES : (key + 1) * LINES, head * 24 : (head + 1) * 24
                 ]
         flat = sum(dot(part, spread) for part in three_parts(spread_from[...]))
-        if last is None:
-            apart = levels_differ
-        else:
-            apart = levels_differ | (rows_differ & (last > 0))
+        apart = levels_differ if last is None else levels_differ | (rows_differ & (last > 0))
         flat = jnp.where(apart, MASKED, flat)
         for o in range(WLON):
             start = (WLON - 1 - o) * LINES
@@ -101,23 +102,26 @@
             for head in range(6):
                 out_of(head, o * LINES, piece[head * LINES : (head + 1) * LINES])
 
-    def put_fine(n):
-        def put(head, at, piece):
-            fine_out[n, head, at : at + LINES, :] = piece
-
-        return put
-
-    def put_coarse(base):
-        def put(head, at, piece):
-            coarse_out[base + head, at : at + LINES, :] = piece
-
-        return put
-
+
+def writer(out_ref, base):
+    def write(head, at, piece):
+        out_ref[base + head, at : at + LINES, :] = piece
+
+    return write
+
+
+def reader(table_ref, row, base):
+    return lambda head: table_ref[row, base + head, :, 0, :]
+
+
+def first_bias_kernel(fine_ref, out_ref, stacked, spread_from):
+    expand_bias([(reader(fine_ref, 0, 0), None)], [writer(out_ref, 0)], stacked, spread_from)
+
+
+def other_bias_kernel(last_ref, fine_ref, coarse_ref, after_ref, fine_out, coarse_out, stacked, spread_from):
     last = last_ref[0]
-    expand(lambda head: fine_ref[0, 0, head], put_fine(0), None)
-    expand(lambda head: fine_ref[1, 0, head], put_fine(1), last)
-    expand(lambda head: coarse_ref[0, 0, head], put_coarse(0), last)
-    expand(lambda head: coarse_ref[0, 0, 6 + head], put_coarse(6), last)
+    tables = [(reader(fine_ref, 1, 0), last), (reader(coarse_ref, 0, 0), last), (reader(coarse_ref, 0, 6), last)]
+    expand_bias(tables, [writer(fine_out, 0), writer(coarse_out, 0), writer(coarse_out, 6)], stacked, spread_from)
 
 
 def attend_group(q, k, v, bias, heads):
@@ -153,7 +157,27 @@
     return jnp.concatenate(pieces, axis=-1)[:, :width]
 
 
-def attend_fine(n, x_ref, bias_ref, qkv_ref, proj_ref):
+def pack_lines(first, second):
+    return jnp.concatenate(first + [jnp.concatenate([second[i], second[3 + i]], axis=-1) for i in range(3)], axis=0)
+
+
+def unpack_line(packed, i, size):
+    first = packed[i * size : (i + 1) * size]
+    at = (6 + i % 3) * size
+    second = packed[at : at + size, i // 3 * 64 : i // 3 * 64 + 64]
+    return jnp.concatenate([first, second], axis=-1)
+
+
+def pack_top_kernel(top_ref, below_ref, corner_ref, line_ref):
+    lines = [top_ref[z, a].astype(f32) for z in range(WZ) for a in range(3)]
+    packed = pack_lines([line[:, :128] for line in lines], [line[:, 128:] for line in lines])
+    below_ref[...] = packed.astype(bf16)
+    for i in range(9):
+        line_ref[i * 18 : (i + 1) * 18, :] = packed[i * 24 + 6 : (i + 1) * 24]
+    corner_ref[...] = line_ref[...].astype(bf16)
+
+
+def attend_fine(x_ref, bias_ref, qkv_ref, proj_ref):
     normed = normalise(get(x_ref, 72, 432, 1, 192))
     q = dot(normed, qkv_ref[:, 0:192]).astype(bf16).astype(f32)
     k = dot(normed, qkv_ref[:, 192:384]).astype(bf16)
@@ -163,7 +187,7 @@
         at = window * CELLS
         q_rows = q[at + start : at + stop]
         k_rows, v_rows = k[at : at + CELLS], v[at : at + CELLS]
-        bias = bias_ref[n, :, start:stop, :]
+        bias = bias_ref[:, start:stop, :]
         left.append(attend_group(q_rows[:, :128], k_rows[:, :128], v_rows[:, :128], bias[:4], 4))
         right.append(attend_group(q_rows[:, 128:], k_rows[:, 128:], v_rows[:, 128:], bias[4:], 2))
     left = jnp.concatenate(left, axis=0).astype(bf16)
@@ -172,36 +196,40 @@
     return (get(x_ref, 144, 288, 1, 192) + product).astype(bf16)
 
 
-def first_rows_kernel(own_ref, right_ref, bias_ref, qkv_ref, proj_ref, out_ref, send_ref, x_ref, a_ref, s_ref):
+def first_rows_kernel(left_ref, own_ref, bias_ref, qkv_ref, proj_ref, out_ref, send_ref, x_ref, a_ref):
     for z in range(WZ):
         for a in range(WLAT):
-            put(x_ref, z * WLAT + a, 24, LINES, own_ref[1 - z, 3 + a].astype(f32))
-            put(x_ref, 288 + z * WLAT + a, 24, LINES, right_ref[1 - z, 3 + a].astype(f32))
-    attended = attend_fine(0, x_ref, bias_ref, qkv_ref, proj_ref)
+            put(x_ref, z * WLAT + a, 24, LINES, left_ref[1 - z, 3 + a].astype(f32))
+            put(x_ref, 288 + z * WLAT + a, 24, LINES, own_ref[1 - z, 3 + a].astype(f32))
+    attended = attend_fine(x_ref, bias_ref, qkv_ref, proj_ref)
     out_ref[...] = attended
     put(a_ref, 0, 288, 1, attended.astype(f32))
-    for t in range(2):
-        for pb in range(2):
-            for z in range(WZ):
-                for a in range(3):
-                    at = (z * 3 + a) * 24 + pb * 12
-                    line = a_ref[t, pl.ds(pb * LINES + z * WLAT + a, 12, stride=24), :]
-                    s_ref[t, at : at + 12, :] = line
-    send_ref[...] = get(s_ref, 0, 144, 1, 192).astype(bf16)
+    lines = [
+        jnp.concatenate([a_ref[t, pl.ds(pb * LINES + z * WLAT + a, 12, stride=24), :] for pb in range(2)], axis=0)
+        for t in range(2)
+        for z in range(WZ)
+        for a in range(3)
+    ]
+    send_ref[...] = pack_lines(lines[:6], [line[:, :64] for line in lines[6:]]).astype(bf16)
 
 
 def second_rows_kernel(
-    own_ref, right_ref, below_ref, corner_ref, first_ref, bias_ref, qkv_ref, proj_ref, up_ref, down_ref,
+    left_ref, own_ref, corner_ref, below_ref, first_ref, bias_ref, qkv_ref, proj_ref, up_ref, down_ref,
     out_ref, x_ref, a_ref, w_ref,
 ):
+    below, corner = below_ref[...].astype(f32), corner_ref[...].astype(f32)
     for z in range(WZ):
         for a in range(WLAT):
-            near = own_ref[1 - z, 9 + a] if a < 3 else below_ref[1 - z, a - 3]
-            far = right_ref[1 - z, 9 + a] if a < 3 else corner_ref[1 - z, a - 3]
-            put(x_ref, z * WLAT + a, 24, LINES, near.astype(f32))
-            put(x_ref, 288 + z * WLAT + a, 24, LINES, far.astype(f32))
+            at = z * WLAT + a
+            if a < 3:
+                put(x_ref, at, 24, LINES, left_ref[1 - z, 9 + a].astype(f32))
+                put(x_ref, 288 + at, 24, LINES, own_ref[1 - z, 9 + a].astype(f32))
+            else:
+                line = (1 - z) * 3 + a - 3
+                put(x_ref, 72 + at, 18, LINES, unpack_line(corner, line, 18))
+                put(x_ref, 288 + at, 24, LINES, unpack_line(below, line, 24))
     put(a_ref, 0, 288, 1, first_ref[...].astype(f32))
-    put(a_ref, 288, 288, 1, attend_fine(1, x_ref, bias_ref, qkv_ref, proj_ref).astype(f32))
+    put(a_ref, 288, 288, 1, attend_fine(x_ref, bias_ref, qkv_ref, proj_ref).astype(f32))
     for t in range(2):
         for pb in range(2):
             for z in range(WZ):
@@ -214,14 +242,16 @@
                     w_ref[t, pl.ds(pb * 288 + z * 12 + rho - 3, 12, stride=24), :] = line
     for i in range(4):
         x = get(w_ref, i * 144, 144, 1, 192)
-        out_ref[i * 144 : (i + 1) * 144, :] = feed_forward(x, up_ref, down_ref).astype(bf16)
+        out_ref[i * 144 : (i + 1) * 144, :] = fine_feed_forward(x, up_ref, down_ref).astype(bf16)
 
 
 def coarse_kernel(
     y_ref, got_ref, fine_up_ref, fine_down_ref, merge_ref, bias_ref, qkv_ref, proj_ref, up_ref, down_ref,
-    keep_ref, down_row_ref, right_column_ref, corner_ref, w_ref, r_ref, o_ref,
+    keep_ref, lower_ref, corner_ref, left_ref, w_ref, r_ref, o_ref,
 ):
-    put(r_ref, 0, 144, 1, feed_forward(got_ref[...].astype(f32), fine_up_ref, fine_down_ref))
+    got = got_ref[...].astype(f32)
+    got = jnp.concatenate([unpack_line(got, i, 24) for i in range(6)], axis=0)
+    put(r_ref, 0, 144, 1, fine_feed_forward(got, fine_up_ref, fine_down_ref))
     put(w_ref, 0, 576, 1, y_ref[...].astype(f32))
     for t in range(2):
         for pb in range(2):
@@ -253,19 +283,10 @@
         for i in range(3):
             upper = get(o_ref, z * WLAT + i, WLON, LINES, 384)
             lower = get(o_ref, z * WLAT + 3 + i, WLON, LINES, 384)
-            keep_ref[1 - z, i] = upper[:6].astype(bf16)
-            right_column_ref[1 - z, i] = upper[6:].astype(bf16)
-            down_row_ref[1 - z, i] = lower[:6].astype(bf16)
-            corner_ref[1 - z, i] = lower[6:].astype(bf16)
-
-
-def assemble_kernel(keep_ref, above_ref, left_ref, corner_ref, out_ref):
-    for z in range(WZ):
-        for i in range(3):
-            upper = [corner_ref[z, i].astype(f32), above_ref[z, i].astype(f32)]
-            lower = [left_ref[z, i].astype(f32), keep_ref[z, i].astype(f32)]
-            out_ref[z, i] = jnp.concatenate(upper, axis=0).astype(bf16)
-            out_ref[z, 3 + i] = jnp.concatenate(lower, axis=0).astype(bf16)
+            keep_ref[1 - z, i] = upper[6:].astype(bf16)
+            left_ref[1 - z, i] = upper[:6].astype(bf16)
+            lower_ref[1 - z, i] = lower[6:].astype(bf16)
+            corner_ref[1 - z, i] = lower[:6].astype(bf16)
 
 
 def call(kernel, outs, scratch, operands, flops, smem=0):
@@ -301,51 +322,58 @@
     coarse_down,
 ):
     last = (lax.axis_index("lat") == lax.axis_size("lat") - 1).astype(jnp.int32).reshape(1)
-    right = from_behind(fields, -1, 0)
-    top = fields[:, :3]
-    below = from_behind(top, 0, -1)
-    corner = from_behind(top, -1, -1)
+    fine_tables = fine_bias.transpose(0, 2, 3, 1, 4)
+    coarse_tables = coarse_bias.transpose(0, 2, 3, 1, 4)
+    fine_down = fine_down.T
+    expansion = [((CELLS, CELLS), f32), ((6 * LINES, LINES * 32), f32)]
+    left = from_behind(fields, 1, 0)
+    below, corner = pl.pallas_call(
+        pack_top_kernel,
+        out_shape=[jax.ShapeDtypeStruct((216, 128), bf16), jax.ShapeDtypeStruct((162, 128), bf16)],
+        grid=(1,),
+        in_specs=[pl.BlockSpec((2, 3, 24, 192), lambda i: (0, 0, 0, 0))],
+        out_specs=[pl.BlockSpec(memory_space=pltpu.VMEM)] * 2,
+        scratch_shapes=[pltpu.VMEM((162, 128), f32)],
+    )(fields)
+    below = from_behind(below, 0, -1)
+    corner = from_behind(corner, 1, -1)
+    (bias0,) = call(first_bias_kernel, [((6, CELLS, CELLS), f32)], expansion, [fine_tables], 1_000_000_000)
+    first, edge = call(
+        first_rows_kernel,
+        [((288, 192), bf16), ((216, 128), bf16)],
+        [tiles_of(576, 192), tiles_of(288, 192)],
+        [left, fields, bias0, fine_qkv, fine_proj],
+        1_000_000_000,
+    )
+    got = from_behind(edge, 0, -1)
     bias1, bias2 = call(
-        bias_kernel,
-        [((2, 6, CELLS, CELLS), f32), ((12, CELLS, CELLS), f32)],
-        [((CELLS, CELLS), f32), ((6 * LINES, LINES * 32), f32)],
-        [last, fine_bias, coarse_bias],
+        other_bias_kernel,
+        [((6, CELLS, CELLS), f32), ((12, CELLS, CELLS), f32)],
+        expansion,
+        [last, fine_tables, coarse_tables, first],
         3_000_000_000,
         smem=1,
     )
-    first, edge = call(
-        first_rows_kernel,
-        [((288, 192), bf16), ((144, 192), bf16)],
-        [tiles_of(576, 192), tiles_of(288, 192), tiles_of(144, 192)],
-        [fields, right, bias1, fine_qkv, fine_proj],
-        1_000_000_000,
-    )
-    got = from_behind(edge, 0, -1)
     (finished,) = call(
         second_rows_kernel,
         [((576, 192), bf16)],
         [tiles_of(576, 192), tiles_of(576, 192), tiles_of(576, 192)],
-        [fields, right, below, corner, first, bias1, fine_qkv, fine_proj, fine_up, fine_down],
+        [left, fields, corner, below, first, bias1, fine_qkv, fine_proj, fine_up, fine_down],
         3_000_000_000,
     )
     quarter = ((2, 3, 6, 384), bf16)
-    keep, down_row, right_column, far_corner = call(
+    keep, lower, far_corner, upper_left = call(
         coarse_kernel,
         [quarter] * 4,
         [tiles_of(576, 192), tiles_of(144, 192), tiles_of(CELLS, 384)],
         [finished, got, fine_up, fine_down, merge_weight, bias2, coarse_qkv, coarse_proj, coarse_up, coarse_down],
         4_000_000_000,
     )
-    above = from_behind(down_row, 0, 1)
-    corner = from_behind(far_corner, 1, 1)
-    left = from_behind(right_column, 1, 0)
-    return pl.pallas_call(
-        assemble_kernel,
-        out_shape=jax.ShapeDtypeStruct((2, 6, 12, 384), bf16),
-        grid=(1,),
-        in_specs=[pl.BlockSpec((2, 3, 6, 384), lambda i: (0, 0, 0, 0))] * 4,
-        out_specs=pl.BlockSpec((2, 6, 12, 384), lambda i: (0, 0, 0, 0)),
-    )(keep, above, left, corner)
+    above = from_behind(lower, 0, 1)
+    corner = from_behind(far_corner, -1, 1)
+    right = from_behind(upper_left, -1, 0)
+    rows = [jnp.concatenate([above, corner], axis=2), jnp.concatenate([keep, right], axis=2)]
+    return jnp.concatenate(rows, axis=1)
 
 
 def solution(mesh):

time: 77.9 us -> 64.6 us (0.83)
  the two profiles are of different devices: /device:TPU:16 before, /device:TPU:1 now
where the time goes in v3:
time: 64.6 us; the launch traced here: 64.3 us
  starting transfers between devices  42.7 us (66%)
  Pallas kernels  14.2 us (22%)
  waiting for transfers between devices  5.29 us (8%)
  local copies, waits for them, and re-layouts  1.74 us (3%)
    ppermute x7, starting transfers between devices, from_behind(): return lax.ppermute(shard, ('lon', 'lat'), pairs)  42.7 us
    pallas_call x5, Pallas kernels, call(): pl.pallas_call(kernel, out_shape=[jax.ShapeDtypeStruct(shape, dtype) for...  12.6 us
    ppermute x7, waiting for transfers between devices, from_behind(): return lax.ppermute(shard, ('lon', 'lat'), pairs)  5.29 us
    pallas_call x1, Pallas kernels, body(): pl.pallas_call(pack_top_kernel, out_shape=[jax.ShapeDtypeStruct((216, 128...  1.6 us
  transfers between devices with their start and end apart: 7, of which 1 were waited for; matrix products, arithmetic and copies ran while one was open for 0% of the time, Pallas kernels for 16%

profile of v3, /device:TPU:1, one launch (start us, length us, event | category | flops | bytes accessed | tf_op | source)
XLA Modules:
  0.0 64.3 jit_solution(2915523918074434570)
XLA Ops:
  0.0 4.5 %collective-permute-start = (bf16[2,12,24,192]{3,2,1,0:T(8,128)(2,1)}, bf16[2,12,24,192]{3,2,1,0:T(8,128)(2,1)S(1)}, u32[]{:S(2)}, u32[]{:S(2)}) collective-permute-start(bf16[2,12,24,192]{3,2,1,0:T(8,128)(2,1)} %own_ref.3), channel_id=1, source_target_pairs={{0,8},{1,9},{2,10},{3,11},{4,12},{5,13},{6,14},{7,15},{8,16},{9,17... | collective-permute-start | bytes 663560 | tf_op jit(solution)/shard_map/ppermute | solution.py:30
  4.5 1.6 %shard_map.118 = (bf16[216,128]{1,0:T(8,128)(2,1)}, bf16[162,128]{1,0:T(8,128)(2,1)}) custom-call(bf16[2,12,24,192]{3,2,1,0:T(8,128)(2,1)} %own_ref.3), custom_call_target="tpu_custom_call" | custom-call | tf_op jit(solution)/shard_map/pallas_call | solution.py:330
  6.1 17.6 %collective-permute-start.1 = (bf16[162,128]{1,0:T(8,128)(2,1)}, bf16[162,128]{1,0:T(8,128)(2,1)S(1)}, u32[]{:S(2)}, u32[]{:S(2)}) collective-permute-start(bf16[162,128]{1,0:T(8,128)(2,1)} %get-tuple-element.15), channel_id=1, source_target_pairs={{0,15},{1,8},{2,9},{3,10},{4,11},{5,12},{6,13},{7,14},{8,23},{9,16... | collective-permute-start | bytes 124424 | tf_op jit(solution)/shard_map/ppermute | solution.py:30
  23.7 2.4 %collective-permute-start.2 = (bf16[216,128]{1,0:T(8,128)(2,1)}, bf16[216,128]{1,0:T(8,128)(2,1)S(1)}, u32[]{:S(2)}, u32[]{:S(2)}) collective-permute-start(bf16[216,128]{1,0:T(8,128)(2,1)} %get-tuple-element.16), channel_id=1, source_target_pairs={{0,7},{1,0},{2,1},{3,2},{4,3},{5,4},{6,5},{7,6},{8,15},{9,8},{10,9... | collective-permute-start | bytes 165896 | tf_op jit(solution)/shard_map/ppermute | solution.py:30
  26.1 0.0 copy-start.8
  26.1 0.9 %copy-done.8 = f32[2,1,6,23,144]{4,1,3,2,0:T(1,128)S(1)} copy-done((f32[2,1,6,23,144]{4,1,3,2,0:T(1,128)S(1)}, f32[2,1,6,23,144]{4,1,3,2,0:T(1,128)}, u32[]{:S(2)}) %copy-start.8) | copy-done | bytes 159000
  27.1 1.3 %shard_map.119.bias_ref = f32[6,144,144]{2,1,0:T(8,128)S(1)} custom-call(f32[2,6,23,1,144]{4,3,2,1,0:T(1,128)S(1)} %bitcast.6), custom_call_target="tpu_custom_call" | custom-call | flops 1000000000 | bytes 158976 | tf_op jit(solution)/shard_map/pallas_call | solution.py:295
  28.4 0.0 copy-start.9
  28.4 0.0 collective-permute-done.left_ref
  28.4 1.7 %shard_map.120 = (bf16[288,192]{1,0:T(8,128)(2,1)S(1)}, bf16[216,128]{1,0:T(8,128)(2,1)S(1)}) custom-call(bf16[2,12,24,192]{3,2,1,0:T(8,128)(2,1)S(1)} %collective-permute-done.left_ref, bf16[2,12,24,192]{3,2,1,0:T(8,128)(2,1)S(1)} %copy-done, f32[6,144,144]{2,1,0:T(8,128)S(1)} %shard_map.119.bias_ref, bf16[192,576]{1,0:T(8,128)(2,1)S(1)} %copy-done.10, ...), custom_call_target="tpu_custom_call" | custom-call | flops 1000000000 | bytes 1234944 | tf_op jit(solution)/shard_map/pallas_call | solution.py:295
  30.1 2.2 %collective-permute-start.3 = (bf16[216,128]{1,0:T(8,128)(2,1)S(1)}, bf16[216,128]{1,0:T(8,128)(2,1)S(1)}, u32[]{:S(2)}, u32[]{:S(2)}) collective-permute-start(bf16[216,128]{1,0:T(8,128)(2,1)S(1)} %get-tuple-element.19), channel_id=1, source_target_pairs={{0,7},{1,0},{2,1},{3,2},{4,3},{5,4},{6,5},{7,6},{8,15},{9,8},{10,9... | collective-permute-start | bytes 165896 | tf_op jit(solution)/shard_map/ppermute | solution.py:30
  32.4 0.0 copy-start.5
  32.4 0.0 copy-start.6
  32.4 2.6 %shard_map.121 = (f32[6,144,144]{2,1,0:T(8,128)S(1)}, f32[12,144,144]{2,1,0:T(8,128)S(1)}) custom-call(s32[1]{0:T(128)} %bitcast.1.last_ref, f32[2,6,23,1,144]{4,3,2,1,0:T(1,128)S(1)} %bitcast.7, f32[1,12,23,1,144]{4,3,2,1,0:T(1,128)S(1)} %bitcast.8, bf16[288,192]{1,0:T(8,128)(2,1)S(1)} %get-tuple-element.17.after_ref.first_ref), custom_call_target="tpu_custom_call" | custom-call | flops 3000000000 | bytes 428548 | tf_op jit(solution)/shard_map/pallas_call | solution.py:295
  35.0 0.0 collective-permute-done.1.corner_ref
  35.0 0.0 collective-permute-done.2.below_ref
  35.1 0.0 copy-start.1
  35.1 0.0 copy-start.2
  35.1 0.0 copy-start.3
  35.1 0.0 copy-start.4
  35.1 0.0 copy-start.7
  35.1 2.9 %shard_map.122.y_ref = bf16[576,192]{1,0:T(8,128)(2,1)S(1)} custom-call(bf16[2,12,24,192]{3,2,1,0:T(8,128)(2,1)S(1)} %collective-permute-done.left_ref, bf16[2,12,24,192]{3,2,1,0:T(8,128)(2,1)S(1)} %copy-done, bf16[162,128]{1,0:T(8,128)(2,1)S(1)} %collective-permute-done.1.corner_ref, bf16[216,128]{1,0:T(8,128)(2,1)S(1)} %collective-permute-done.2.below_ref, ...), custom_call_target="tpu_custom_call" | custom-call | flops 3000000000 | bytes 2032128 | tf_op jit(solution)/shard_map/pallas_call | solution.py:295
  38.0 0.0 collective-permute-done.3.got_ref
  38.1 4.1 %shard_map.123 = (bf16[2,3,6,384]{3,2,1,0:T(8,128)(2,1)S(1)}, bf16[2,3,6,384]{3,2,1,0:T(8,128)(2,1)S(1)}, bf16[2,3,6,384]{3,2,1,0:T(8,128)(2,1)S(1)}, bf16[2,3,6,384]{3,2,1,0:T(8,128)(2,1)S(1)}) custom-call(bf16[576,192]{1,0:T(8,128)(2,1)S(1)} %shard_map.122.y_ref, bf16[216,128]{1,0:T(8,128)(2,1)S(1)} %collective-permute-done.3.got_ref, ...), custom_call_target="tpu_custom_call" | custom-call | flops 4000000000 | bytes 5990400 | tf_op jit(solution)/shard_map/pallas_call | solution.py:295
  42.2 3.1 %collective-permute-start.4 = (bf16[2,3,6,384]{3,2,1,0:T(8,128)(2,1)S(1)}, bf16[2,3,6,384]{3,2,1,0:T(8,128)(2,1)S(1)}, u32[]{:S(2)}, u32[]{:S(2)}) collective-permute-start(bf16[2,3,6,384]{3,2,1,0:T(8,128)(2,1)S(1)} %get-tuple-element.21), channel_id=1, source_target_pairs={{0,1},{1,2},{2,3},{3,4},{4,5},{5,6},{6,7},{7,0},{8,9},{9,10},{10,1... | collective-permute-start | bytes 82952 | tf_op jit(solution)/shard_map/ppermute | solution.py:30
  45.3 4.3 %collective-permute-start.5 = (bf16[2,3,6,384]{3,2,1,0:T(8,128)(2,1)S(1)}, bf16[2,3,6,384]{3,2,1,0:T(8,128)(2,1)S(1)}, u32[]{:S(2)}, u32[]{:S(2)}) collective-permute-start(bf16[2,3,6,384]{3,2,1,0:T(8,128)(2,1)S(1)} %get-tuple-element.22), channel_id=1, source_target_pairs={{0,505},{1,506},{2,507},{3,508},{4,509},{5,510},{6,511},{7,504},{8... | collective-permute-start | bytes 82952 | tf_op jit(solution)/shard_map/ppermute | solution.py:30
  49.6 8.6 %collective-permute-start.6 = (bf16[2,3,6,384]{3,2,1,0:T(8,128)(2,1)S(1)}, bf16[2,3,6,384]{3,2,1,0:T(8,128)(2,1)S(1)}, u32[]{:S(2)}, u32[]{:S(2)}) collective-permute-start(bf16[2,3,6,384]{3,2,1,0:T(8,128)(2,1)S(1)} %get-tuple-element.24), channel_id=1, source_target_pairs={{0,504},{1,505},{2,506},{3,507},{4,508},{5,509},{6,510},{7,511},{8... | collective-permute-start | bytes 82952 | tf_op jit(solution)/shard_map/ppermute | solution.py:30
  58.2 0.0 collective-permute-done.4
  58.2 5.3 %collective-permute-done.5 = bf16[2,3,6,384]{3,2,1,0:T(8,128)(2,1)S(1)} collective-permute-done((bf16[2,3,6,384]{3,2,1,0:T(8,128)(2,1)S(1)}, bf16[2,3,6,384]{3,2,1,0:T(8,128)(2,1)S(1)}, u32[]{:S(2)}, u32[]{:S(2)}) %collective-permute-start.5) | collective-permute-done | bytes 27680 | tf_op jit(solution)/shard_map/ppermute | solution.py:30
  63.5 0.0 collective-permute-done.6
  63.5 0.1 maximum_maximum_fusion
  63.6 0.7 %copy.13 = bf16[2,6,12,384]{3,0,2,1:T(2,128)(2,1)} copy(bf16[2,6,12,384]{3,2,1,0:T(8,128)(2,1)S(1)} %maximum_maximum_fusion) | data formatting | bytes 221184 | tf_op jit(solution)/shard_map/concatenate | solution.py:376
  (14 shorter events, 0.0 us)
Async XLA Ops:
  0.0 28.4 %collective-permute-start = (bf16[2,12,24,192]{3,2,1,0:T(8,128)(2,1)}, bf16[2,12,24,192]{3,2,1,0:T(8,128)(2,1)S(1)}, u32[]{:S(2)}, u32[]{:S(2)}) collective-permute-start(bf16[2,12,24,192]{3,2,1,0:T(8,128)(2,1)} %own_ref.3), channel_id=1, source_target_pairs={{0,8},{1,9},{2,10},{3,11},{4,12},{5,13},{6,14},{7,15},{8,16},{9,17... | collective-permute-start | bytes 663560 | tf_op jit(solution)/shard_map/ppermute | solution.py:30
  6.1 28.9 %collective-permute-start.1 = (bf16[162,128]{1,0:T(8,128)(2,1)}, bf16[162,128]{1,0:T(8,128)(2,1)S(1)}, u32[]{:S(2)}, u32[]{:S(2)}) collective-permute-start(bf16[162,128]{1,0:T(8,128)(2,1)} %get-tuple-element.15), channel_id=1, source_target_pairs={{0,15},{1,8},{2,9},{3,10},{4,11},{5,12},{6,13},{7,14},{8,23},{9,16... | collective-permute-start | bytes 124424 | tf_op jit(solution)/shard_map/ppermute | solution.py:30
  23.7 11.3 %collective-permute-start.2 = (bf16[216,128]{1,0:T(8,128)(2,1)}, bf16[216,128]{1,0:T(8,128)(2,1)S(1)}, u32[]{:S(2)}, u32[]{:S(2)}) collective-permute-start(bf16[216,128]{1,0:T(8,128)(2,1)} %get-tuple-element.16), channel_id=1, source_target_pairs={{0,7},{1,0},{2,1},{3,2},{4,3},{5,4},{6,5},{7,6},{8,15},{9,8},{10,9... | collective-permute-start | bytes 165896 | tf_op jit(solution)/shard_map/ppermute | solution.py:30
  26.1 1.0 %copy-start.8 = (f32[2,1,6,23,144]{4,1,3,2,0:T(1,128)S(1)}, f32[2,1,6,23,144]{4,1,3,2,0:T(1,128)}, u32[]{:S(2)}) copy-start(f32[2,1,6,23,144]{4,1,3,2,0:T(1,128)} %param.13) | copy-start | bytes 476932
  27.1 1.3 %copy-start = (bf16[2,12,24,192]{3,2,1,0:T(8,128)(2,1)S(1)}, bf16[2,12,24,192]{3,2,1,0:T(8,128)(2,1)}, u32[]{:S(2)}) copy-start(bf16[2,12,24,192]{3,2,1,0:T(8,128)(2,1)} %own_ref.3) | copy-start | bytes 663556
  27.1 1.3 %copy-start.10 = (bf16[192,576]{1,0:T(8,128)(2,1)S(1)}, bf16[192,576]{1,0:T(8,128)(2,1)}, u32[]{:S(2)}) copy-start(bf16[192,576]{1,0:T(8,128)(2,1)} %qkv_ref.4) | copy-start | bytes 663556
  27.1 1.3 %copy-start.11 = (bf16[192,192]{1,0:T(8,128)(2,1)S(1)}, bf16[192,192]{1,0:T(8,128)(2,1)}, u32[]{:S(2)}) copy-start(bf16[192,192]{1,0:T(8,128)(2,1)} %proj_ref.4) | copy-start | bytes 221188
  28.4 4.0 %copy-start.9 = (f32[1,1,12,23,144]{4,1,3,2,0:T(1,128)S(1)}, f32[1,1,12,23,144]{4,1,3,2,0:T(1,128)}, u32[]{:S(2)}) copy-start(f32[1,1,12,23,144]{4,1,3,2,0:T(1,128)} %param.19) | copy-start | bytes 476932
  30.1 7.9 %collective-permute-start.3 = (bf16[216,128]{1,0:T(8,128)(2,1)S(1)}, bf16[216,128]{1,0:T(8,128)(2,1)S(1)}, u32[]{:S(2)}, u32[]{:S(2)}) collective-permute-start(bf16[216,128]{1,0:T(8,128)(2,1)S(1)} %get-tuple-element.19), channel_id=1, source_target_pairs={{0,7},{1,0},{2,1},{3,2},{4,3},{5,4},{6,5},{7,6},{8,15},{9,8},{10,9... | collective-permute-start | bytes 165896 | tf_op jit(solution)/shard_map/ppermute | solution.py:30
  32.4 2.7 %copy-start.5 = (bf16[192,768]{1,0:T(8,128)(2,1)S(1)}, bf16[192,768]{1,0:T(8,128)(2,1)}, u32[]{:S(2)}) copy-start(bf16[192,768]{1,0:T(8,128)(2,1)} %fine_up_ref.1) | copy-start | bytes 884740
  32.4 2.7 %copy-start.6 = (bf16[768,192]{0,1:T(8,128)(2,1)S(1)}, bf16[768,192]{0,1:T(8,128)(2,1)}, u32[]{:S(2)}) copy-start(bf16[768,192]{0,1:T(8,128)(2,1)} %param.17) | copy-start | bytes 884740
  35.1 3.0 %copy-start.1 = (bf16[384,1536]{1,0:T(8,128)(2,1)S(1)}, bf16[384,1536]{1,0:T(8,128)(2,1)}, u32[]{:S(2)}) copy-start(bf16[384,1536]{1,0:T(8,128)(2,1)} %up_ref.3) | copy-start | bytes 3538948
  35.1 3.0 %copy-start.2 = (bf16[1536,384]{1,0:T(8,128)(2,1)S(1)}, bf16[1536,384]{1,0:T(8,128)(2,1)}, u32[]{:S(2)}) copy-start(bf16[1536,384]{1,0:T(8,128)(2,1)} %down_ref.1) | copy-start | bytes 3538948
  35.1 3.0 %copy-start.3 = (bf16[384,1152]{1,0:T(8,128)(2,1)S(1)}, bf16[384,1152]{1,0:T(8,128)(2,1)}, u32[]{:S(2)}) copy-start(bf16[384,1152]{1,0:T(8,128)(2,1)} %qkv_ref.5) | copy-start | bytes 2654212
  35.1 3.0 %copy-start.4 = (bf16[768,384]{1,0:T(8,128)(2,1)S(1)}, bf16[768,384]{1,0:T(8,128)(2,1)}, u32[]{:S(2)}) copy-start(bf16[768,384]{1,0:T(8,128)(2,1)} %merge_ref.1) | copy-start | bytes 1769476
  35.1 3.0 %copy-start.7 = (bf16[384,384]{1,0:T(8,128)(2,1)S(1)}, bf16[384,384]{1,0:T(8,128)(2,1)}, u32[]{:S(2)}) copy-start(bf16[384,384]{1,0:T(8,128)(2,1)} %proj_ref.5) | copy-start | bytes 884740
  42.2 16.0 %collective-permute-start.4 = (bf16[2,3,6,384]{3,2,1,0:T(8,128)(2,1)S(1)}, bf16[2,3,6,384]{3,2,1,0:T(8,128)(2,1)S(1)}, u32[]{:S(2)}, u32[]{:S(2)}) collective-permute-start(bf16[2,3,6,384]{3,2,1,0:T(8,128)(2,1)S(1)} %get-tuple-element.21), channel_id=1, source_target_pairs={{0,1},{1,2},{2,3},{3,4},{4,5},{5,6},{6,7},{7,0},{8,9},{9,10},{10,1... | collective-permute-start | bytes 82952 | tf_op jit(solution)/shard_map/ppermute | solution.py:30
  45.3 18.2 %collective-permute-start.5 = (bf16[2,3,6,384]{3,2,1,0:T(8,128)(2,1)S(1)}, bf16[2,3,6,384]{3,2,1,0:T(8,128)(2,1)S(1)}, u32[]{:S(2)}, u32[]{:S(2)}) collective-permute-start(bf16[2,3,6,384]{3,2,1,0:T(8,128)(2,1)S(1)} %get-tuple-element.22), channel_id=1, source_target_pairs={{0,505},{1,506},{2,507},{3,508},{4,509},{5,510},{6,511},{7,504},{8... | collective-permute-start | bytes 82952 | tf_op jit(solution)/shard_map/ppermute | solution.py:30
  49.6 13.9 %collective-permute-start.6 = (bf16[2,3,6,384]{3,2,1,0:T(8,128)(2,1)S(1)}, bf16[2,3,6,384]{3,2,1,0:T(8,128)(2,1)S(1)}, u32[]{:S(2)}, u32[]{:S(2)}) collective-permute-start(bf16[2,3,6,384]{3,2,1,0:T(8,128)(2,1)S(1)} %get-tuple-element.24), channel_id=1, source_target_pairs={{0,504},{1,505},{2,506},{3,507},{4,508},{5,509},{6,510},{7,511},{8... | collective-permute-start | bytes 82952 | tf_op jit(solution)/shard_map/ppermute | solution.py:30

commit v4 on v3

--- a/solution.py
+++ b/solution.py
@@ -75,7 +75,8 @@
     spread_from[...] = jnp.zeros_like(spread_from)
     row = iota((CELLS, CELLS), 0)
     key, query = row // LINES, row % LINES
-    column = ((query // WLAT * WZ + key // WLAT) * WLAT + query % WLAT) * WLAT + key % WLAT
+    z_key, z_query = 1 - key // WLAT, 1 - query // WLAT
+    column = ((z_query * WZ + z_key) * WLAT + query % WLAT) * WLAT + key % WLAT
     pick = (iota((CELLS, CELLS), 1) == column).astype(f32).astype(bf16)
     row = iota((LINES * 32, 384), 0)
     lane = iota((LINES * 32, 384), 1)
@@ -114,14 +115,13 @@
     return lambda head: table_ref[row, base + head, :, 0, :]
 
 
-def first_bias_kernel(fine_ref, out_ref, stacked, spread_from):
-    expand_bias([(reader(fine_ref, 0, 0), None)], [writer(out_ref, 0)], stacked, spread_from)
-
-
-def other_bias_kernel(last_ref, fine_ref, coarse_ref, after_ref, fine_out, coarse_out, stacked, spread_from):
-    last = last_ref[0]
+def expand_first(fine_ref, bias0_ref, stacked, spread_from):
+    expand_bias([(reader(fine_ref, 0, 0), None)], [writer(bias0_ref, 0)], stacked, spread_from)
+
+
+def expand_others(last, fine_ref, coarse_ref, bias1_ref, bias2_ref, stacked, spread_from):
     tables = [(reader(fine_ref, 1, 0), last), (reader(coarse_ref, 0, 0), last), (reader(coarse_ref, 0, 6), last)]
-    expand_bias(tables, [writer(fine_out, 0), writer(coarse_out, 0), writer(coarse_out, 6)], stacked, spread_from)
+    expand_bias(tables, [writer(bias1_ref, 0), writer(bias2_ref, 0), writer(bias2_ref, 6)], stacked, spread_from)
 
 
 def attend_group(q, k, v, bias, heads):
@@ -168,13 +168,21 @@
     return jnp.concatenate([first, second], axis=-1)
 
 
-def pack_top_kernel(top_ref, below_ref, corner_ref, line_ref):
-    lines = [top_ref[z, a].astype(f32) for z in range(WZ) for a in range(3)]
+def prepare_kernel(
+    flags_ref, fields_ref, fine_ref, coarse_ref, below_ref, corner_ref, bias0_ref, bias1_ref, bias2_ref,
+    line_ref, stacked, spread_from,
+):
+    lines = [fields_ref[z, a].astype(f32) for z in range(WZ) for a in range(3)]
     packed = pack_lines([line[:, :128] for line in lines], [line[:, 128:] for line in lines])
-    below_ref[...] = packed.astype(bf16)
-    for i in range(9):
-        line_ref[i * 18 : (i + 1) * 18, :] = packed[i * 24 + 6 : (i + 1) * 24]
-    corner_ref[...] = line_ref[...].astype(bf16)
+    for ref, start in ((below_ref, 0), (corner_ref, 6)):
+        for i in range(9):
+            line_ref[i * 18 : (i + 1) * 18, :] = packed[i * 24 + start : i * 24 + start + 18]
+        ref[...] = line_ref[...].astype(bf16)
+    expand_first(fine_ref, bias0_ref, stacked, spread_from)
+
+    @pl.when(flags_ref[1] > 0)
+    def _():
+        expand_others(flags_ref[0], fine_ref, coarse_ref, bias1_ref, bias2_ref, stacked, spread_from)
 
 
 def attend_fine(x_ref, bias_ref, qkv_ref, proj_ref):
@@ -199,67 +207,70 @@
 def first_rows_kernel(left_ref, own_ref, bias_ref, qkv_ref, proj_ref, out_ref, send_ref, x_ref, a_ref):
     for z in range(WZ):
         for a in range(WLAT):
-            put(x_ref, z * WLAT + a, 24, LINES, left_ref[1 - z, 3 + a].astype(f32))
-            put(x_ref, 288 + z * WLAT + a, 24, LINES, own_ref[1 - z, 3 + a].astype(f32))
+            put(x_ref, z * WLAT + a, 24, LINES, left_ref[z, 3 + a].astype(f32))
+            put(x_ref, 288 + z * WLAT + a, 24, LINES, own_ref[z, 3 + a].astype(f32))
     attended = attend_fine(x_ref, bias_ref, qkv_ref, proj_ref)
     out_ref[...] = attended
     put(a_ref, 0, 288, 1, attended.astype(f32))
-    lines = [
-        jnp.concatenate([a_ref[t, pl.ds(pb * LINES + z * WLAT + a, 12, stride=24), :] for pb in range(2)], axis=0)
-        for t in range(2)
-        for z in range(WZ)
-        for a in range(3)
-    ]
+    lines = [a_ref[t, pl.ds(z * WLAT + a, 24, stride=LINES), :] for t in range(2) for z in range(WZ) for a in range(3)]
     send_ref[...] = pack_lines(lines[:6], [line[:, :64] for line in lines[6:]]).astype(bf16)
 
 
 def second_rows_kernel(
-    left_ref, own_ref, corner_ref, below_ref, first_ref, bias_ref, qkv_ref, proj_ref, up_ref, down_ref,
-    out_ref, x_ref, a_ref, w_ref,
+    flags_ref, left_ref, own_ref, corner_ref, below_ref, first_ref, fine_ref, coarse_ref, old1_ref, old2_ref,
+    qkv_ref, proj_ref, up_ref, down_ref, out_ref, bias2_ref, bias1_ref, x_ref, a_ref, w_ref, stacked, spread_from,
 ):
+
+    @pl.when(flags_ref[1] > 0)
+    def _():
+        bias1_ref[...] = old1_ref[...]
+        bias2_ref[...] = old2_ref[...]
+
+    @pl.when(flags_ref[1] == 0)
+    def _():
+        expand_others(flags_ref[0], fine_ref, coarse_ref, bias1_ref, bias2_ref, stacked, spread_from)
+
     below, corner = below_ref[...].astype(f32), corner_ref[...].astype(f32)
     for z in range(WZ):
         for a in range(WLAT):
             at = z * WLAT + a
             if a < 3:
-                put(x_ref, at, 24, LINES, left_ref[1 - z, 9 + a].astype(f32))
-                put(x_ref, 288 + at, 24, LINES, own_ref[1 - z, 9 + a].astype(f32))
+                put(x_ref, at, 24, LINES, left_ref[z, 9 + a].astype(f32))
+                put(x_ref, 288 + at, 24, LINES, own_ref[z, 9 + a].astype(f32))
             else:
-                line = (1 - z) * 3 + a - 3
-                put(x_ref, 72 + at, 18, LINES, unpack_line(corner, line, 18))
-                put(x_ref, 288 + at, 24, LINES, unpack_line(below, line, 24))
+                put(x_ref, 72 + at, 18, LINES, unpack_line(corner, z * 3 + a - 3, 18))
+                put(x_ref, 288 + at, 18, LINES, unpack_line(below, z * 3 + a - 3, 18))
     put(a_ref, 0, 288, 1, first_ref[...].astype(f32))
-    put(a_ref, 288, 288, 1, attend_fine(x_ref, bias_ref, qkv_ref, proj_ref).astype(f32))
+    put(a_ref, 288, 288, 1, attend_fine(x_ref, bias1_ref, qkv_ref, proj_ref).astype(f32))
     for t in range(2):
-        for pb in range(2):
+        for rho in range(3, 12):
             for z in range(WZ):
-                for rho in range(3, 15):
-                    n, a = divmod(rho, WLAT)
-                    if rho < 12:
-                        line = a_ref[t, pl.ds(n * 288 + pb * LINES + z * WLAT + a, 12, stride=24), :]
-                    else:
-                        line = jnp.zeros((12, 128), f32)
-                    w_ref[t, pl.ds(pb * 288 + z * 12 + rho - 3, 12, stride=24), :] = line
-    for i in range(4):
+                at = rho // WLAT * 288 + z * WLAT + rho % WLAT
+                to = ((rho - 3) * WZ + z) * 24
+                w_ref[t, to : to + 24, :] = a_ref[t, pl.ds(at, 24, stride=LINES), :]
+    for i in range(3):
         x = get(w_ref, i * 144, 144, 1, 192)
         out_ref[i * 144 : (i + 1) * 144, :] = fine_feed_forward(x, up_ref, down_ref).astype(bf16)
 
 
 def coarse_kernel(
     y_ref, got_ref, fine_up_ref, fine_down_ref, merge_ref, bias_ref, qkv_ref, proj_ref, up_ref, down_ref,
-    keep_ref, lower_ref, corner_ref, left_ref, w_ref, r_ref, o_ref,
+    keep_ref, lower_ref, corner_ref, left_ref, w_ref, p_ref, o_ref,
 ):
     got = got_ref[...].astype(f32)
-    got = jnp.concatenate([unpack_line(got, i, 24) for i in range(6)], axis=0)
-    put(r_ref, 0, 144, 1, fine_feed_forward(got, fine_up_ref, fine_down_ref))
-    put(w_ref, 0, 576, 1, y_ref[...].astype(f32))
-    for t in range(2):
+    got = jnp.concatenate([unpack_line(got, z * 3 + a, 24) for a in range(3) for z in range(WZ)], axis=0)
+    put(w_ref, 0, 432, 1, y_ref[...].astype(f32))
+    put(w_ref, 432, 144, 1, fine_feed_forward(got, fine_up_ref, fine_down_ref))
+    parts = []
+    for pa in range(2):
         for pb in range(2):
-            for z in range(WZ):
-                for rho in range(3):
-                    at = (z * 3 + rho) * 24 + pb * 12
-                    w_ref[t, pl.ds(pb * 288 + z * 12 + 9 + rho, 12, stride=24), :] = r_ref[t, at : at + 12, :]
-    parts = [get(w_ref, pb * 288 + pa, CELLS, 2, 192) for pa in range(2) for pb in range(2)]
+            for t in range(2):
+                for z in range(WZ):
+                    for i in range(WLAT):
+                        at = ((2 * i + pa) * WZ + z) * 24 + pb
+                        line = w_ref[t, pl.ds(at, WLON, stride=2), :]
+                        p_ref[t, pl.ds(len(parts) * CELLS + z * WLAT + i, WLON, stride=LINES), :] = line
+            parts.append(get(p_ref, len(parts) * CELLS, CELLS, 1, 192))
     mean = sum(jnp.sum(part, axis=-1, keepdims=True) for part in parts) * (1.0 / 768)
     parts = [part - mean for part in parts]
     variance = sum(jnp.sum(part * part, axis=-1, keepdims=True) for part in parts) * (1.0 / 768)
@@ -279,14 +290,10 @@
         product = product + dot(mixed.astype(bf16), proj_ref[g * 128 : (g + 1) * 128, :])
     attended = product.astype(bf16).astype(f32)
     put(o_ref, 0, CELLS, 1, feed_forward(attended, up_ref, down_ref))
-    for z in range(WZ):
-        for i in range(3):
-            upper = get(o_ref, z * WLAT + i, WLON, LINES, 384)
-            lower = get(o_ref, z * WLAT + 3 + i, WLON, LINES, 384)
-            keep_ref[1 - z, i] = upper[6:].astype(bf16)
-            left_ref[1 - z, i] = upper[:6].astype(bf16)
-            lower_ref[1 - z, i] = lower[6:].astype(bf16)
-            corner_ref[1 - z, i] = lower[:6].astype(bf16)
+    for i in range(3):
+        for j in range(WLON):
+            for ref, row in ((left_ref, i), (corner_ref, 3 + i)) if j < 6 else ((keep_ref, i), (lower_ref, 3 + i)):
+                ref[i, j % 6] = get(o_ref, j * LINES + row, WZ, WLAT, 384).astype(bf16)
 
 
 def call(kernel, outs, scratch, operands, flops, smem=0):
@@ -321,23 +328,25 @@
     coarse_up,
     coarse_down,
 ):
-    last = (lax.axis_index("lat") == lax.axis_size("lat") - 1).astype(jnp.int32).reshape(1)
+    lat, lats = lax.axis_index("lat"), lax.axis_size("lat")
+    lon, lons = lax.axis_index("lon"), lax.axis_size("lon")
+    flags = jnp.stack([lat == lats - 1, (lat < lats // 2) & (lon < lons // 2)]).astype(jnp.int32)
     fine_tables = fine_bias.transpose(0, 2, 3, 1, 4)
     coarse_tables = coarse_bias.transpose(0, 2, 3, 1, 4)
     fine_down = fine_down.T
     expansion = [((CELLS, CELLS), f32), ((6 * LINES, LINES * 32), f32)]
+    biases = [((6, CELLS, CELLS), f32), ((12, CELLS, CELLS), f32)]
     left = from_behind(fields, 1, 0)
-    below, corner = pl.pallas_call(
-        pack_top_kernel,
-        out_shape=[jax.ShapeDtypeStruct((216, 128), bf16), jax.ShapeDtypeStruct((162, 128), bf16)],
-        grid=(1,),
-        in_specs=[pl.BlockSpec((2, 3, 24, 192), lambda i: (0, 0, 0, 0))],
-        out_specs=[pl.BlockSpec(memory_space=pltpu.VMEM)] * 2,
-        scratch_shapes=[pltpu.VMEM((162, 128), f32)],
-    )(fields)
+    below, corner, bias0, bias1, bias2 = call(
+        prepare_kernel,
+        [((162, 128), bf16), ((162, 128), bf16), ((6, CELLS, CELLS), f32)] + biases,
+        [((162, 128), f32)] + expansion,
+        [flags, fields, fine_tables, coarse_tables],
+        1_000_000_000,
+        smem=1,
+    )
+    corner = from_behind(corner, 1, -1)
     below = from_behind(below, 0, -1)
-    corner = from_behind(corner, 1, -1)
-    (bias0,) = call(first_bias_kernel, [((6, CELLS, CELLS), f32)], expansion, [fine_tables], 1_000_000_000)
     first, edge = call(
         first_rows_kernel,
         [((288, 192), bf16), ((216, 128), bf16)],
@@ -346,34 +355,28 @@
         1_000_000_000,
     )
     got = from_behind(edge, 0, -1)
-    bias1, bias2 = call(
-        other_bias_kernel,
-        [((6, CELLS, CELLS), f32), ((12, CELLS, CELLS), f32)],
-        expansion,
-        [last, fine_tables, coarse_tables, first],
+    finished, bias2 = call(
+        second_rows_kernel,
+        [((432, 192), bf16), biases[1]],
+        [biases[0], tiles_of(576, 192), tiles_of(576, 192), tiles_of(432, 192)] + expansion,
+        [flags, left, fields, corner, below, first, fine_tables, coarse_tables, bias1, bias2]
+        + [fine_qkv, fine_proj, fine_up, fine_down],
         3_000_000_000,
         smem=1,
     )
-    (finished,) = call(
-        second_rows_kernel,
-        [((576, 192), bf16)],
-        [tiles_of(576, 192), tiles_of(576, 192), tiles_of(576, 192)],
-        [left, fields, corner, below, first, bias1, fine_qkv, fine_proj, fine_up, fine_down],
-        3_000_000_000,
-    )
-    quarter = ((2, 3, 6, 384), bf16)
+    quarter = ((3, 6, WZ, 384), bf16)
     keep, lower, far_corner, upper_left = call(
         coarse_kernel,
         [quarter] * 4,
-        [tiles_of(576, 192), tiles_of(144, 192), tiles_of(CELLS, 384)],
+        [tiles_of(576, 192), tiles_of(576, 192), tiles_of(CELLS, 384)],
         [finished, got, fine_up, fine_down, merge_weight, bias2, coarse_qkv, coarse_proj, coarse_up, coarse_down],
         4_000_000_000,
     )
     above = from_behind(lower, 0, 1)
     corner = from_behind(far_corner, -1, 1)
     right = from_behind(upper_left, -1, 0)
-    rows = [jnp.concatenate([above, corner], axis=2), jnp.concatenate([keep, right], axis=2)]
-    return jnp.concatenate(rows, axis=1)
+    rows = [jnp.concatenate([above, corner], axis=1), jnp.concatenate([keep, right], axis=1)]
+    return jnp.concatenate(rows, axis=0).transpose(2, 0, 1, 3)
 
 
 def solution(mesh):

time: 64.6 us -> 64.7 us (level)
  local copies, waits for them, and re-layouts: 1.74 us -> 2.94 us
  starting transfers between devices: 42.7 us -> 41.6 us
  other arithmetic: 0.05 us -> 0.88 us
    unnamed x24 -> x30, local copies, waits for them, and re-layouts: 1.01 us -> 2.94 us
    pallas_call x1 -> x0, Pallas kernels: 1.6 us -> none  [body(): pl.pallas_call(pack_top_kernel, out_shape=[jax.ShapeDtypeStruct((216, 128...]
    ppermute x7, starting transfers between devices: 42.7 us -> 41.6 us  [from_behind(): return lax.ppermute(shard, ('lon', 'lat'), pairs)]
    pallas_call x5 -> x4, Pallas kernels: 12.6 us -> 13.6 us  [call(): pl.pallas_call(kernel, out_shape=[jax.ShapeDtypeStruct(shape, dtype) for...]
    transpose x0 -> x1, other arithmetic: none -> 0.81 us  [body(): return jnp.concatenate(rows, axis=0).transpose(2, 0, 1, 3)]
    concatenate x1 -> x0, local copies, waits for them, and re-layouts: 0.73 us -> none  [body(): return jnp.concatenate(rows, axis=1)]
  transfers between devices with their start and end apart: 7 -> 7, of which waited for: 1 -> 2; matrix products, arithmetic and copies ran while one was open for 0% -> 0% of each run, Pallas kernels for 16% -> 15%
where the time goes in v4:
time: 64.7 us; the launch traced here: 64.4 us
  starting transfers between devices  41.6 us (64%)
  Pallas kernels  13.6 us (21%)
  waiting for transfers between devices  5.1 us (8%)
  local copies, waits for them, and re-layouts  2.94 us (5%)
  other arithmetic  0.88 us (1%)
    ppermute x7, starting transfers between devices, from_behind(): return lax.ppermute(shard, ('lon', 'lat'), pairs)  41.6 us
    pallas_call x4, Pallas kernels, call(): pl.pallas_call(kernel, out_shape=[jax.ShapeDtypeStruct(shape, dtype) for...  13.6 us
    ppermute x7, waiting for transfers between devices, from_behind(): return lax.ppermute(shard, ('lon', 'lat'), pairs)  5.1 us
    unnamed x30, local copies, waits for them, and re-layouts  2.94 us
  transfers between devices with their start and end apart: 7, of which 2 were waited for; matrix products, arithmetic and copies ran while one was open for 0% of the time, Pallas kernels for 15%

profile of v4, /device:TPU:1, one launch (start us, length us, event | category | flops | bytes accessed | tf_op | source)
XLA Modules:
  0.0 64.4 jit_solution(14382325843496096582)
XLA Ops:
  0.0 4.5 %collective-permute-start = (bf16[2,12,24,192]{3,2,1,0:T(8,128)(2,1)}, bf16[2,12,24,192]{3,2,1,0:T(8,128)(2,1)S(1)}, u32[]{:S(2)}, u32[]{:S(2)}) collective-permute-start(bf16[2,12,24,192]{3,2,1,0:T(8,128)(2,1)} %own_ref.3), channel_id=1, source_target_pairs={{0,8},{1,9},{2,10},{3,11},{4,12},{5,13},{6,14},{7,15},{8,16},{9,17... | collective-permute-start | bytes 663560 | tf_op jit(solution)/shard_map/ppermute | solution.py:30
  4.5 0.1 add_convert_fusion.flags_ref
  4.6 1.0 %copy-done.4 = bf16[2,12,24,192]{3,2,1,0:T(8,128)(2,1)S(1)} copy-done((bf16[2,12,24,192]{3,2,1,0:T(8,128)(2,1)S(1)}, bf16[2,12,24,192]{3,2,1,0:T(8,128)(2,1)}, u32[]{:S(2)}) %copy-start.4) | copy-done | bytes 221208
  5.6 1.0 %copy-done.9 = f32[2,1,6,23,144]{4,1,3,2,0:T(1,128)S(1)} copy-done((f32[2,1,6,23,144]{4,1,3,2,0:T(1,128)S(1)}, f32[2,1,6,23,144]{4,1,3,2,0:T(1,128)}, u32[]{:S(2)}) %copy-start.9) | copy-done | bytes 159000
  6.5 1.0 %copy-done.11 = f32[1,1,12,23,144]{4,1,3,2,0:T(1,128)S(1)} copy-done((f32[1,1,12,23,144]{4,1,3,2,0:T(1,128)S(1)}, f32[1,1,12,23,144]{4,1,3,2,0:T(1,128)}, u32[]{:S(2)}) %copy-start.11) | copy-done | bytes 159000
  7.5 4.3 %shard_map.118 = (bf16[162,128]{1,0:T(8,128)(2,1)S(1)}, bf16[162,128]{1,0:T(8,128)(2,1)S(1)}, f32[6,144,144]{2,1,0:T(8,128)S(1)}, f32[6,144,144]{2,1,0:T(8,128)S(1)}, f32[12,144,144]{2,1,0:T(8,128)S(1)}) custom-call(s32[2]{0:T(128)S(1)} %add_convert_fusion.flags_ref, bf16[2,12,24,192]{3,2,1,0:T(8,128)(2,1)S(1)} %copy-done.4, ...), custom_call_target="tpu_custom_call" | custom-call | flops 1000000000 | bytes 539144 | tf_op jit(solution)/shard_map/pallas_call | solution.py:302
  11.8 15.2 %collective-permute-start.1 = (bf16[162,128]{1,0:T(8,128)(2,1)S(1)}, bf16[162,128]{1,0:T(8,128)(2,1)S(1)}, u32[]{:S(2)}, u32[]{:S(2)}) collective-permute-start(bf16[162,128]{1,0:T(8,128)(2,1)S(1)} %get-tuple-element.18), channel_id=1, source_target_pairs={{0,15},{1,8},{2,9},{3,10},{4,11},{5,12},{6,13},{7,14},{8,23},{9,16... | collective-permute-start | bytes 124424 | tf_op jit(solution)/shard_map/ppermute | solution.py:30
  27.0 2.4 %collective-permute-start.2 = (bf16[162,128]{1,0:T(8,128)(2,1)S(1)}, bf16[162,128]{1,0:T(8,128)(2,1)S(1)}, u32[]{:S(2)}, u32[]{:S(2)}) collective-permute-start(bf16[162,128]{1,0:T(8,128)(2,1)S(1)} %get-tuple-element.19), channel_id=1, source_target_pairs={{0,7},{1,0},{2,1},{3,2},{4,3},{5,4},{6,5},{7,6},{8,15},{9,8},{10,9... | collective-permute-start | bytes 124424 | tf_op jit(solution)/shard_map/ppermute | solution.py:30
  29.3 0.0 collective-permute-done.left_ref
  29.4 0.0 copy-start.6
  29.4 0.0 copy-start.7
  29.4 0.0 copy-start.10
  29.4 0.0 copy-start.12
  29.4 1.7 %shard_map.119 = (bf16[288,192]{1,0:T(8,128)(2,1)S(1)}, bf16[216,128]{1,0:T(8,128)(2,1)S(1)}) custom-call(bf16[2,12,24,192]{3,2,1,0:T(8,128)(2,1)S(1)} %collective-permute-done.left_ref, bf16[2,12,24,192]{3,2,1,0:T(8,128)(2,1)S(1)} %copy-done.5, f32[6,144,144]{2,1,0:T(8,128)S(1)} %get-tuple-element.20.bias_ref, bf16[192,576]{1,0:T(8,128)(2,1)S(1)} %copy-done.13, ...), custom_call_target="tpu_custom_call" | custom-call | flops 1000000000 | bytes 1234944 | tf_op jit(solution)/shard_map/pallas_call | solution.py:302
  31.2 2.2 %collective-permute-start.3 = (bf16[216,128]{1,0:T(8,128)(2,1)S(1)}, bf16[216,128]{1,0:T(8,128)(2,1)S(1)}, u32[]{:S(2)}, u32[]{:S(2)}) collective-permute-start(bf16[216,128]{1,0:T(8,128)(2,1)S(1)} %get-tuple-element.25), channel_id=1, source_target_pairs={{0,7},{1,0},{2,1},{3,2},{4,3},{5,4},{6,5},{7,6},{8,15},{9,8},{10,9... | collective-permute-start | bytes 165896 | tf_op jit(solution)/shard_map/ppermute | solution.py:30
  33.4 0.0 collective-permute-done.1.corner_ref
  33.4 0.0 collective-permute-done.2.below_ref
  33.4 0.0 copy-start
  33.4 0.0 copy-start.1
  33.4 0.0 copy-start.2
  33.5 0.0 copy-start.3
  33.5 0.0 copy-start.8
  33.5 3.4 %shard_map.120 = (bf16[432,192]{1,0:T(8,128)(2,1)S(1)}, f32[12,144,144]{2,1,0:T(8,128)S(1)}) custom-call(s32[2]{0:T(128)S(1)} %add_convert_fusion.flags_ref, bf16[2,12,24,192]{3,2,1,0:T(8,128)(2,1)S(1)} %collective-permute-done.left_ref, bf16[2,12,24,192]{3,2,1,0:T(8,128)(2,1)S(1)} %copy-done.5, bf16[162,128]{1,0:T(8,128)(2,1)S(1)} %collective-permute-done.1.corner_ref, ...), custom_call_target="tpu_custom_call" | custom-call | flops 3000000000 | bytes 3331592 | tf_op jit(solution)/shard_map/pallas_call | solution.py:302
  36.9 1.1 %collective-permute-done.3.got_ref = bf16[216,128]{1,0:T(8,128)(2,1)S(1)} collective-permute-done((bf16[216,128]{1,0:T(8,128)(2,1)S(1)}, bf16[216,128]{1,0:T(8,128)(2,1)S(1)}, u32[]{:S(2)}, u32[]{:S(2)}) %collective-permute-start.3) | collective-permute-done | bytes 55328 | tf_op jit(solution)/shard_map/ppermute | solution.py:30
  38.0 4.2 %shard_map.121 = (bf16[3,6,2,384]{3,2,1,0:T(2,128)(2,1)S(1)}, bf16[3,6,2,384]{3,2,1,0:T(2,128)(2,1)S(1)}, bf16[3,6,2,384]{3,2,1,0:T(2,128)(2,1)S(1)}, bf16[3,6,2,384]{3,2,1,0:T(2,128)(2,1)S(1)}) custom-call(bf16[432,192]{1,0:T(8,128)(2,1)S(1)} %get-tuple-element.24.y_ref, bf16[216,128]{1,0:T(8,128)(2,1)S(1)} %collective-permute-done.3.got_ref, ...), custom_call_target="tpu_custom_call" | custom-call | flops 4000000000 | bytes 5935104 | tf_op jit(solution)/shard_map/pallas_call | solution.py:302
  42.2 2.0 %collective-permute-start.4 = (bf16[3,6,2,384]{3,2,1,0:T(2,128)(2,1)S(1)}, bf16[3,6,2,384]{3,2,1,0:T(2,128)(2,1)S(1)}, u32[]{:S(2)}, u32[]{:S(2)}) collective-permute-start(bf16[3,6,2,384]{3,2,1,0:T(2,128)(2,1)S(1)} %get-tuple-element.27), channel_id=1, source_target_pairs={{0,1},{1,2},{2,3},{3,4},{4,5},{5,6},{6,7},{7,0},{8,9},{9,10},{10,1... | collective-permute-start | bytes 82952 | tf_op jit(solution)/shard_map/ppermute | solution.py:30
  44.2 4.3 %collective-permute-start.5 = (bf16[3,6,2,384]{3,2,1,0:T(2,128)(2,1)S(1)}, bf16[3,6,2,384]{3,2,1,0:T(2,128)(2,1)S(1)}, u32[]{:S(2)}, u32[]{:S(2)}) collective-permute-start(bf16[3,6,2,384]{3,2,1,0:T(2,128)(2,1)S(1)} %get-tuple-element.28), channel_id=1, source_target_pairs={{0,505},{1,506},{2,507},{3,508},{4,509},{5,510},{6,511},{7,504},{8... | collective-permute-start | bytes 82952 | tf_op jit(solution)/shard_map/ppermute | solution.py:30
  48.5 11.1 %collective-permute-start.6 = (bf16[3,6,2,384]{3,2,1,0:T(2,128)(2,1)S(1)}, bf16[3,6,2,384]{3,2,1,0:T(2,128)(2,1)S(1)}, u32[]{:S(2)}, u32[]{:S(2)}) collective-permute-start(bf16[3,6,2,384]{3,2,1,0:T(2,128)(2,1)S(1)} %get-tuple-element.30), channel_id=1, source_target_pairs={{0,504},{1,505},{2,506},{3,507},{4,508},{5,509},{6,510},{7,511},{8... | collective-permute-start | bytes 82952 | tf_op jit(solution)/shard_map/ppermute | solution.py:30
  59.6 0.0 collective-permute-done.4
  59.6 3.9 %collective-permute-done.5 = bf16[3,6,2,384]{3,2,1,0:T(2,128)(2,1)S(1)} collective-permute-done((bf16[3,6,2,384]{3,2,1,0:T(2,128)(2,1)S(1)}, bf16[3,6,2,384]{3,2,1,0:T(2,128)(2,1)S(1)}, u32[]{:S(2)}, u32[]{:S(2)}) %collective-permute-start.5) | collective-permute-done | bytes 27680 | tf_op jit(solution)/shard_map/ppermute | solution.py:30
  63.6 0.0 collective-permute-done.6
  63.6 0.8 %maximum_bitcast_fusion = bf16[2,6,12,384]{3,0,2,1:T(2,128)(2,1)} fusion(bf16[3,6,2,384]{3,2,1,0:T(2,128)(2,1)S(1)} %collective-permute-done.6, bf16[3,6,2,384]{3,2,1,0:T(2,128)(2,1)S(1)} %get-tuple-element.29, bf16[3,6,2,384]{3,2,1,0:T(2,128)(2,1)S(1)} %collective-permute-done.5, bf16[3,6,2,384]{3,2,1,0:T(2,128)(2,1)S(1)} %collective-permute-done.4), kind=kLoop, calls=%fused_computation | loop fusion | flops 165888 | bytes 221184 | tf_op jit(solution)/shard_map/transpose | solution.py:379
  (18 shorter events, 0.0 us)
Async XLA Ops:
  0.0 29.3 %collective-permute-start = (bf16[2,12,24,192]{3,2,1,0:T(8,128)(2,1)}, bf16[2,12,24,192]{3,2,1,0:T(8,128)(2,1)S(1)}, u32[]{:S(2)}, u32[]{:S(2)}) collective-permute-start(bf16[2,12,24,192]{3,2,1,0:T(8,128)(2,1)} %own_ref.3), channel_id=1, source_target_pairs={{0,8},{1,9},{2,10},{3,11},{4,12},{5,13},{6,14},{7,15},{8,16},{9,17... | collective-permute-start | bytes 663560 | tf_op jit(solution)/shard_map/ppermute | solution.py:30
  4.6 1.0 %copy-start.4 = (bf16[2,12,24,192]{3,2,1,0:T(8,128)(2,1)S(1)}, bf16[2,12,24,192]{3,2,1,0:T(8,128)(2,1)}, u32[]{:S(2)}) copy-start(bf16[2,12,24,192]{3,2,1,0:T(8,128)(2,1)} %own_ref.3) | copy-start | bytes 663556
  5.6 1.0 %copy-start.9 = (f32[2,1,6,23,144]{4,1,3,2,0:T(1,128)S(1)}, f32[2,1,6,23,144]{4,1,3,2,0:T(1,128)}, u32[]{:S(2)}) copy-start(f32[2,1,6,23,144]{4,1,3,2,0:T(1,128)} %param.13) | copy-start | bytes 476932
  6.5 1.0 %copy-start.11 = (f32[1,1,12,23,144]{4,1,3,2,0:T(1,128)S(1)}, f32[1,1,12,23,144]{4,1,3,2,0:T(1,128)}, u32[]{:S(2)}) copy-start(f32[1,1,12,23,144]{4,1,3,2,0:T(1,128)} %param.19) | copy-start | bytes 476932
  7.5 21.9 %copy-start.5 = (bf16[2,12,24,192]{3,2,1,0:T(8,128)(2,1)S(1)}, bf16[2,12,24,192]{3,2,1,0:T(8,128)(2,1)}, u32[]{:S(2)}) copy-start(bf16[2,12,24,192]{3,2,1,0:T(8,128)(2,1)} %own_ref.3) | copy-start | bytes 663556
  7.5 21.9 %copy-start.13 = (bf16[192,576]{1,0:T(8,128)(2,1)S(1)}, bf16[192,576]{1,0:T(8,128)(2,1)}, u32[]{:S(2)}) copy-start(bf16[192,576]{1,0:T(8,128)(2,1)} %qkv_ref.4) | copy-start | bytes 663556
  7.5 21.9 %copy-start.14 = (bf16[192,192]{1,0:T(8,128)(2,1)S(1)}, bf16[192,192]{1,0:T(8,128)(2,1)}, u32[]{:S(2)}) copy-start(bf16[192,192]{1,0:T(8,128)(2,1)} %proj_ref.4) | copy-start | bytes 221188
  11.8 21.6 %collective-permute-start.1 = (bf16[162,128]{1,0:T(8,128)(2,1)S(1)}, bf16[162,128]{1,0:T(8,128)(2,1)S(1)}, u32[]{:S(2)}, u32[]{:S(2)}) collective-permute-start(bf16[162,128]{1,0:T(8,128)(2,1)S(1)} %get-tuple-element.18), channel_id=1, source_target_pairs={{0,15},{1,8},{2,9},{3,10},{4,11},{5,12},{6,13},{7,14},{8,23},{9,16... | collective-permute-start | bytes 124424 | tf_op jit(solution)/shard_map/ppermute | solution.py:30
  27.0 6.4 %collective-permute-start.2 = (bf16[162,128]{1,0:T(8,128)(2,1)S(1)}, bf16[162,128]{1,0:T(8,128)(2,1)S(1)}, u32[]{:S(2)}, u32[]{:S(2)}) collective-permute-start(bf16[162,128]{1,0:T(8,128)(2,1)S(1)} %get-tuple-element.19), channel_id=1, source_target_pairs={{0,7},{1,0},{2,1},{3,2},{4,3},{5,4},{6,5},{7,6},{8,15},{9,8},{10,9... | collective-permute-start | bytes 124424 | tf_op jit(solution)/shard_map/ppermute | solution.py:30
  29.4 4.0 %copy-start.6 = (bf16[192,768]{1,0:T(8,128)(2,1)S(1)}, bf16[192,768]{1,0:T(8,128)(2,1)}, u32[]{:S(2)}) copy-start(bf16[192,768]{1,0:T(8,128)(2,1)} %fine_up_ref.1) | copy-start | bytes 884740
  29.4 4.0 %copy-start.7 = (bf16[768,192]{0,1:T(8,128)(2,1)S(1)}, bf16[768,192]{0,1:T(8,128)(2,1)}, u32[]{:S(2)}) copy-start(bf16[768,192]{0,1:T(8,128)(2,1)} %param.17) | copy-start | bytes 884740
  29.4 4.0 %copy-start.10 = (f32[2,1,6,23,144]{4,1,3,2,0:T(1,128)S(1)}, f32[2,1,6,23,144]{4,1,3,2,0:T(1,128)}, u32[]{:S(2)}) copy-start(f32[2,1,6,23,144]{4,1,3,2,0:T(1,128)} %param.13) | copy-start | bytes 476932
  29.4 4.0 %copy-start.12 = (f32[1,1,12,23,144]{4,1,3,2,0:T(1,128)S(1)}, f32[1,1,12,23,144]{4,1,3,2,0:T(1,128)}, u32[]{:S(2)}) copy-start(f32[1,1,12,23,144]{4,1,3,2,0:T(1,128)} %param.19) | copy-start | bytes 476932
  31.2 6.8 %collective-permute-start.3 = (bf16[216,128]{1,0:T(8,128)(2,1)S(1)}, bf16[216,128]{1,0:T(8,128)(2,1)S(1)}, u32[]{:S(2)}, u32[]{:S(2)}) collective-permute-start(bf16[216,128]{1,0:T(8,128)(2,1)S(1)} %get-tuple-element.25), channel_id=1, source_target_pairs={{0,7},{1,0},{2,1},{3,2},{4,3},{5,4},{6,5},{7,6},{8,15},{9,8},{10,9... | collective-permute-start | bytes 165896 | tf_op jit(solution)/shard_map/ppermute | solution.py:30
  33.4 4.6 %copy-start = (bf16[384,1536]{1,0:T(8,128)(2,1)S(1)}, bf16[384,1536]{1,0:T(8,128)(2,1)}, u32[]{:S(2)}) copy-start(bf16[384,1536]{1,0:T(8,128)(2,1)} %up_ref.3) | copy-start | bytes 3538948
  33.4 4.6 %copy-start.1 = (bf16[1536,384]{1,0:T(8,128)(2,1)S(1)}, bf16[1536,384]{1,0:T(8,128)(2,1)}, u32[]{:S(2)}) copy-start(bf16[1536,384]{1,0:T(8,128)(2,1)} %down_ref.1) | copy-start | bytes 3538948
  33.4 4.6 %copy-start.2 = (bf16[384,1152]{1,0:T(8,128)(2,1)S(1)}, bf16[384,1152]{1,0:T(8,128)(2,1)}, u32[]{:S(2)}) copy-start(bf16[384,1152]{1,0:T(8,128)(2,1)} %qkv_ref.5) | copy-start | bytes 2654212
  33.5 4.6 %copy-start.3 = (bf16[768,384]{1,0:T(8,128)(2,1)S(1)}, bf16[768,384]{1,0:T(8,128)(2,1)}, u32[]{:S(2)}) copy-start(bf16[768,384]{1,0:T(8,128)(2,1)} %merge_ref.1) | copy-start | bytes 1769476
  33.5 4.6 %copy-start.8 = (bf16[384,384]{1,0:T(8,128)(2,1)S(1)}, bf16[384,384]{1,0:T(8,128)(2,1)}, u32[]{:S(2)}) copy-start(bf16[384,384]{1,0:T(8,128)(2,1)} %proj_ref.5) | copy-start | bytes 884740
  42.2 17.4 %collective-permute-start.4 = (bf16[3,6,2,384]{3,2,1,0:T(2,128)(2,1)S(1)}, bf16[3,6,2,384]{3,2,1,0:T(2,128)(2,1)S(1)}, u32[]{:S(2)}, u32[]{:S(2)}) collective-permute-start(bf16[3,6,2,384]{3,2,1,0:T(2,128)(2,1)S(1)} %get-tuple-element.27), channel_id=1, source_target_pairs={{0,1},{1,2},{2,3},{3,4},{4,5},{5,6},{6,7},{7,0},{8,9},{9,10},{10,1... | collective-permute-start | bytes 82952 | tf_op jit(solution)/shard_map/ppermute | solution.py:30
  44.2 19.3 %collective-permute-start.5 = (bf16[3,6,2,384]{3,2,1,0:T(2,128)(2,1)S(1)}, bf16[3,6,2,384]{3,2,1,0:T(2,128)(2,1)S(1)}, u32[]{:S(2)}, u32[]{:S(2)}) collective-permute-start(bf16[3,6,2,384]{3,2,1,0:T(2,128)(2,1)S(1)} %get-tuple-element.28), channel_id=1, source_target_pairs={{0,505},{1,506},{2,507},{3,508},{4,509},{5,510},{6,511},{7,504},{8... | collective-permute-start | bytes 82952 | tf_op jit(solution)/shard_map/ppermute | solution.py:30
  48.5 15.0 %collective-permute-start.6 = (bf16[3,6,2,384]{3,2,1,0:T(2,128)(2,1)S(1)}, bf16[3,6,2,384]{3,2,1,0:T(2,128)(2,1)S(1)}, u32[]{:S(2)}, u32[]{:S(2)}) collective-permute-start(bf16[3,6,2,384]{3,2,1,0:T(2,128)(2,1)S(1)} %get-tuple-element.30), channel_id=1, source_target_pairs={{0,504},{1,505},{2,506},{3,507},{4,508},{5,509},{6,510},{7,511},{8... | collective-permute-start | bytes 82952 | tf_op jit(solution)/shard_map/ppermute | solution.py:30

commit v5 on v4

--- a/solution.py
+++ b/solution.py
@@ -115,15 +115,6 @@
     return lambda head: table_ref[row, base + head, :, 0, :]
 
 
-def expand_first(fine_ref, bias0_ref, stacked, spread_from):
-    expand_bias([(reader(fine_ref, 0, 0), None)], [writer(bias0_ref, 0)], stacked, spread_from)
-
-
-def expand_others(last, fine_ref, coarse_ref, bias1_ref, bias2_ref, stacked, spread_from):
-    tables = [(reader(fine_ref, 1, 0), last), (reader(coarse_ref, 0, 0), last), (reader(coarse_ref, 0, 6), last)]
-    expand_bias(tables, [writer(bias1_ref, 0), writer(bias2_ref, 0), writer(bias2_ref, 6)], stacked, spread_from)
-
-
 def attend_group(q, k, v, bias, heads):
     queries, width = q.shape
     of_head = iota((queries, width), 1) // HD
@@ -168,21 +159,46 @@
     return jnp.concatenate([first, second], axis=-1)
 
 
+def expand_all(last, fine_ref, coarse_ref, bias0_ref, bias1_ref, bias2_ref, stacked, spread_from):
+    tables = [
+        (reader(fine_ref, 0, 0), None),
+        (reader(fine_ref, 1, 0), last),
+        (reader(coarse_ref, 0, 0), last),
+        (reader(coarse_ref, 0, 6), last),
+    ]
+    outs = [writer(bias0_ref, 0), writer(bias1_ref, 0), writer(bias2_ref, 0), writer(bias2_ref, 6)]
+    expand_bias(tables, outs, stacked, spread_from)
+
+
 def prepare_kernel(
-    flags_ref, fields_ref, fine_ref, coarse_ref, below_ref, corner_ref, bias0_ref, bias1_ref, bias2_ref,
-    line_ref, stacked, spread_from,
+    flags_ref, fields_hbm, fine_hbm, coarse_hbm, qkv_hbm, proj_hbm, below_ref, corner_ref, own_ref, fine_ref,
+    coarse_ref, qkv_ref, proj_ref, bias0_ref, bias1_ref, bias2_ref, line_ref, stacked, spread_from, sems,
 ):
-    lines = [fields_ref[z, a].astype(f32) for z in range(WZ) for a in range(3)]
+    moves = [
+        (fields_hbm.at[:, 0:3], own_ref.at[:, 0:3]),
+        (fine_hbm, fine_ref),
+        (coarse_hbm, coarse_ref),
+        (fields_hbm.at[:, 3:12], own_ref.at[:, 3:12]),
+        (qkv_hbm, qkv_ref),
+        (proj_hbm, proj_ref),
+    ]
+    copies = [pltpu.make_async_copy(source, to, sems.at[i]) for i, (source, to) in enumerate(moves)]
+    for copy in copies:
+        copy.start()
+    copies[0].wait()
+    lines = [own_ref[z, a].astype(f32) for z in range(WZ) for a in range(3)]
     packed = pack_lines([line[:, :128] for line in lines], [line[:, 128:] for line in lines])
     for ref, start in ((below_ref, 0), (corner_ref, 6)):
         for i in range(9):
             line_ref[i * 18 : (i + 1) * 18, :] = packed[i * 24 + start : i * 24 + start + 18]
         ref[...] = line_ref[...].astype(bf16)
-    expand_first(fine_ref, bias0_ref, stacked, spread_from)
+
+    for copy in copies[1:]:
+        copy.wait()
 
     @pl.when(flags_ref[1] > 0)
     def _():
-        expand_others(flags_ref[0], fine_ref, coarse_ref, bias1_ref, bias2_ref, stacked, spread_from)
+        expand_all(flags_ref[0], fine_ref, coarse_ref, bias0_ref, bias1_ref, bias2_ref, stacked, spread_from)
 
 
 def attend_fine(x_ref, bias_ref, qkv_ref, proj_ref):
@@ -204,12 +220,25 @@
     return (get(x_ref, 144, 288, 1, 192) + product).astype(bf16)
 
 
-def first_rows_kernel(left_ref, own_ref, bias_ref, qkv_ref, proj_ref, out_ref, send_ref, x_ref, a_ref):
+def first_rows_kernel(
+    flags_ref, left_ref, own_ref, fine_ref, coarse_ref, old0_ref, old1_ref, old2_ref, qkv_ref, proj_ref,
+    out_ref, send_ref, bias1_ref, bias2_ref, bias0_ref, x_ref, a_ref, stacked, spread_from,
+):
+    @pl.when(flags_ref[1] > 0)
+    def _():
+        bias0_ref[...] = old0_ref[...]
+        bias1_ref[...] = old1_ref[...]
+        bias2_ref[...] = old2_ref[...]
+
+    @pl.when(flags_ref[1] == 0)
+    def _():
+        expand_all(flags_ref[0], fine_ref, coarse_ref, bias0_ref, bias1_ref, bias2_ref, stacked, spread_from)
+
     for z in range(WZ):
         for a in range(WLAT):
             put(x_ref, z * WLAT + a, 24, LINES, left_ref[z, 3 + a].astype(f32))
             put(x_ref, 288 + z * WLAT + a, 24, LINES, own_ref[z, 3 + a].astype(f32))
-    attended = attend_fine(x_ref, bias_ref, qkv_ref, proj_ref)
+    attended = attend_fine(x_ref, bias0_ref, qkv_ref, proj_ref)
     out_ref[...] = attended
     put(a_ref, 0, 288, 1, attended.astype(f32))
     lines = [a_ref[t, pl.ds(z * WLAT + a, 24, stride=LINES), :] for t in range(2) for z in range(WZ) for a in range(3)]
@@ -217,19 +246,9 @@
 
 
 def second_rows_kernel(
-    flags_ref, left_ref, own_ref, corner_ref, below_ref, first_ref, fine_ref, coarse_ref, old1_ref, old2_ref,
-    qkv_ref, proj_ref, up_ref, down_ref, out_ref, bias2_ref, bias1_ref, x_ref, a_ref, w_ref, stacked, spread_from,
+    left_ref, own_ref, corner_ref, below_ref, first_ref, bias1_ref, qkv_ref, proj_ref, up_ref, down_ref,
+    out_ref, x_ref, a_ref, w_ref,
 ):
-
-    @pl.when(flags_ref[1] > 0)
-    def _():
-        bias1_ref[...] = old1_ref[...]
-        bias2_ref[...] = old2_ref[...]
-
-    @pl.when(flags_ref[1] == 0)
-    def _():
-        expand_others(flags_ref[0], fine_ref, coarse_ref, bias1_ref, bias2_ref, stacked, spread_from)
-
     below, corner = below_ref[...].astype(f32), corner_ref[...].astype(f32)
     for z in range(WZ):
         for a in range(WLAT):
@@ -337,32 +356,37 @@
     expansion = [((CELLS, CELLS), f32), ((6 * LINES, LINES * 32), f32)]
     biases = [((6, CELLS, CELLS), f32), ((12, CELLS, CELLS), f32)]
     left = from_behind(fields, 1, 0)
-    below, corner, bias0, bias1, bias2 = call(
+    sources = [fields, fine_tables, coarse_tables, fine_qkv, fine_proj]
+    hbm, vmem, smem = (pl.BlockSpec(memory_space=space) for space in (pltpu.HBM, pltpu.VMEM, pltpu.SMEM))
+    below, corner, own, fine_tables, coarse_tables, fine_qkv, fine_proj, bias0, bias1, bias2 = pl.pallas_call(
         prepare_kernel,
-        [((162, 128), bf16), ((162, 128), bf16), ((6, CELLS, CELLS), f32)] + biases,
-        [((162, 128), f32)] + expansion,
-        [flags, fields, fine_tables, coarse_tables],
+        out_shape=[jax.ShapeDtypeStruct((162, 128), bf16)] * 2
+        + [jax.ShapeDtypeStruct(source.shape, source.dtype) for source in sources]
+        + [jax.ShapeDtypeStruct(shape, dtype) for shape, dtype in [((6, CELLS, CELLS), f32)] + biases],
+        in_specs=[smem] + [hbm] * 5,
+        out_specs=[vmem] * 10,
+        scratch_shapes=[pltpu.VMEM((162, 128), f32)]
+        + [pltpu.VMEM(shape, dtype) for shape, dtype in expansion]
+        + [pltpu.SemaphoreType.DMA((6,))],
+        compiler_params=pltpu.CompilerParams(vmem_limit_bytes=VMEM_LIMIT),
+    )(flags, *(pltpu.with_memory_space_constraint(source, pltpu.HBM) for source in sources))
+    corner = from_behind(corner, 1, -1)
+    below = from_behind(below, 0, -1)
+    first, edge, bias1, bias2 = call(
+        first_rows_kernel,
+        [((288, 192), bf16), ((216, 128), bf16)] + biases,
+        [((6, CELLS, CELLS), f32), tiles_of(576, 192), tiles_of(288, 192)] + expansion,
+        [flags, left, own, fine_tables, coarse_tables, bias0, bias1, bias2, fine_qkv, fine_proj],
         1_000_000_000,
         smem=1,
     )
-    corner = from_behind(corner, 1, -1)
-    below = from_behind(below, 0, -1)
-    first, edge = call(
-        first_rows_kernel,
-        [((288, 192), bf16), ((216, 128), bf16)],
-        [tiles_of(576, 192), tiles_of(288, 192)],
-        [left, fields, bias0, fine_qkv, fine_proj],
-        1_000_000_000,
-    )
     got = from_behind(edge, 0, -1)
-    finished, bias2 = call(
+    (finished,) = call(
         second_rows_kernel,
-        [((432, 192), bf16), biases[1]],
-        [biases[0], tiles_of(576, 192), tiles_of(576, 192), tiles_of(432, 192)] + expansion,
-        [flags, left, fields, corner, below, first, fine_tables, coarse_tables, bias1, bias2]
-        + [fine_qkv, fine_proj, fine_up, fine_down],
+        [((432, 192), bf16)],
+        [tiles_of(576, 192), tiles_of(576, 192), tiles_of(432, 192)],
+        [left, own, corner, below, first, bias1, fine_qkv, fine_proj, fine_up, fine_down],
         3_000_000_000,
-        smem=1,
     )
     quarter = ((3, 6, WZ, 384), bf16)
     keep, lower, far_corner, upper_left = call(

time: 64.7 us -> 63.7 us (0.985)
  local copies, waits for them, and re-layouts: 2.94 us -> 0.04 us
  starting transfers between devices: 41.6 us -> 42.6 us
  Pallas kernels: 13.6 us -> 14.5 us
    pallas_call x0 -> x1, Pallas kernels: none -> 5.39 us  [body(): pl.pallas_call(prepare_kernel, out_shape=[jax.ShapeDtypeStruct((162, 128)...]
    pallas_call x4 -> x3, Pallas kernels: 13.6 us -> 9.14 us  [call(): pl.pallas_call(kernel, out_shape=[jax.ShapeDtypeStruct(shape, dtype) for...]
    unnamed x30 -> x14, local copies, waits for them, and re-layouts: 2.94 us -> 0.04 us
    ppermute x7, starting transfers between devices: 41.6 us -> 42.6 us  [from_behind(): return lax.ppermute(shard, ('lon', 'lat'), pairs)]
  transfers between devices with their start and end apart: 7 -> 7, of which waited for: 2 -> 1; matrix products, arithmetic and copies ran while one was open for 0% -> 0% of each run, Pallas kernels for 15% -> 16%
where the time goes in v5:
time: 63.7 us; the launch traced here: 63.4 us
  starting transfers between devices  42.6 us (67%)
  Pallas kernels  14.5 us (23%)
  waiting for transfers between devices  5.08 us (8%)
  other arithmetic  0.88 us (1%)
    ppermute x7, starting transfers between devices, from_behind(): return lax.ppermute(shard, ('lon', 'lat'), pairs)  42.6 us
    pallas_call x3, Pallas kernels, call(): pl.pallas_call(kernel, out_shape=[jax.ShapeDtypeStruct(shape, dtype) for...  9.14 us
    pallas_call x1, Pallas kernels, body(): pl.pallas_call(prepare_kernel, out_shape=[jax.ShapeDtypeStruct((162, 128)...  5.39 us
    ppermute x7, waiting for transfers between devices, from_behind(): return lax.ppermute(shard, ('lon', 'lat'), pairs)  5.08 us
  transfers between devices with their start and end apart: 7, of which 1 were waited for; matrix products, arithmetic and copies ran while one was open for 0% of the time, Pallas kernels for 16%

profile of v5, /device:TPU:1, one launch (start us, length us, event | category | flops | bytes accessed | tf_op | source)
XLA Modules:
  0.0 63.4 jit_solution(8000920065553130770)
XLA Ops:
  0.0 4.5 %collective-permute-start = (bf16[2,12,24,192]{3,2,1,0:T(8,128)(2,1)}, bf16[2,12,24,192]{3,2,1,0:T(8,128)(2,1)S(1)}, u32[]{:S(2)}, u32[]{:S(2)}) collective-permute-start(bf16[2,12,24,192]{3,2,1,0:T(8,128)(2,1)} %fields_hbm.1), channel_id=1, source_target_pairs={{0,8},{1,9},{2,10},{3,11},{4,12},{5,13},{6,14},{7,15},{8,16},{9,17... | collective-permute-start | bytes 663560 | tf_op jit(solution)/shard_map/ppermute | solution.py:30
  4.5 0.1 add_convert_fusion.flags_ref
  4.6 5.4 %shard_map.118 = (bf16[162,128]{1,0:T(8,128)(2,1)S(1)}, bf16[162,128]{1,0:T(8,128)(2,1)S(1)}, bf16[2,12,24,192]{3,2,1,0:T(8,128)(2,1)S(1)}, f32[2,6,23,1,144]{4,...) custom-call(s32[2]{0:T(128)S(1)} %add_convert_fusion.flags_ref, ...), custom_call_target="tpu_custom_call" | custom-call | tf_op jit(solution)/shard_map/pallas_call | solution.py:361
  10.0 14.1 %collective-permute-start.1 = (bf16[162,128]{1,0:T(8,128)(2,1)S(1)}, bf16[162,128]{1,0:T(8,128)(2,1)S(1)}, u32[]{:S(2)}, u32[]{:S(2)}) collective-permute-start(bf16[162,128]{1,0:T(8,128)(2,1)S(1)} %get-tuple-element.24), channel_id=1, source_target_pairs={{0,15},{1,8},{2,9},{3,10},{4,11},{5,12},{6,13},{7,14},{8,23},{9,16... | collective-permute-start | bytes 124424 | tf_op jit(solution)/shard_map/ppermute | solution.py:30
  24.1 2.4 %collective-permute-start.2 = (bf16[162,128]{1,0:T(8,128)(2,1)S(1)}, bf16[162,128]{1,0:T(8,128)(2,1)S(1)}, u32[]{:S(2)}, u32[]{:S(2)}) collective-permute-start(bf16[162,128]{1,0:T(8,128)(2,1)S(1)} %get-tuple-element.25), channel_id=1, source_target_pairs={{0,7},{1,0},{2,1},{3,2},{4,3},{5,4},{6,5},{7,6},{8,15},{9,8},{10,9... | collective-permute-start | bytes 124424 | tf_op jit(solution)/shard_map/ppermute | solution.py:30
  26.4 0.0 collective-permute-done.left_ref
  26.5 0.0 copy-start.4
  26.5 0.0 copy-start.5
  26.5 2.5 %shard_map.119 = (bf16[288,192]{1,0:T(8,128)(2,1)S(1)}, bf16[216,128]{1,0:T(8,128)(2,1)S(1)}, f32[6,144,144]{2,1,0:T(8,128)S(1)}, f32[12,144,144]{2,1,0:T(8,128)S(1)}) custom-call(s32[2]{0:T(128)S(1)} %add_convert_fusion.flags_ref, bf16[2,12,24,192]{3,2,1,0:T(8,128)(2,1)S(1)} %collective-permute-done.left_ref, ...), custom_call_target="tpu_custom_call" | custom-call | flops 1000000000 | bytes 3045896 | tf_op jit(solution)/shard_map/pallas_call | solution.py:321
  29.0 5.7 %collective-permute-start.3 = (bf16[216,128]{1,0:T(8,128)(2,1)S(1)}, bf16[216,128]{1,0:T(8,128)(2,1)S(1)}, u32[]{:S(2)}, u32[]{:S(2)}) collective-permute-start(bf16[216,128]{1,0:T(8,128)(2,1)S(1)} %get-tuple-element.35), channel_id=1, source_target_pairs={{0,7},{1,0},{2,1},{3,2},{4,3},{5,4},{6,5},{7,6},{8,15},{9,8},{10,9... | collective-permute-start | bytes 165896 | tf_op jit(solution)/shard_map/ppermute | solution.py:30
  34.7 0.0 collective-permute-done.1.corner_ref
  34.7 0.0 collective-permute-done.2.below_ref
  34.7 0.0 copy-done.4
  34.7 0.0 copy-done.5
  34.7 0.0 copy-start
  34.7 0.0 copy-start.1
  34.8 0.0 copy-start.2
  34.8 0.0 copy-start.3
  34.8 0.0 copy-start.6
  34.8 2.5 %shard_map.120.y_ref = bf16[432,192]{1,0:T(8,128)(2,1)S(1)} custom-call(bf16[2,12,24,192]{3,2,1,0:T(8,128)(2,1)S(1)} %collective-permute-done.left_ref, bf16[2,12,24,192]{3,2,1,0:T(8,128)(2,1)S(1)} %get-tuple-element.23.own_ref, bf16[162,128]{1,0:T(8,128)(2,1)S(1)} %collective-permute-done.1.corner_ref, ...), custom_call_target="tpu_custom_call" | custom-call | flops 3000000000 | bytes 2018304 | tf_op jit(solution)/shard_map/pallas_call | solution.py:321
  37.3 0.0 collective-permute-done.3.got_ref
  37.3 0.0 copy-done
  37.3 0.0 copy-done.1
  37.3 0.0 copy-done.2
  37.3 4.2 %shard_map.121 = (bf16[3,6,2,384]{3,2,1,0:T(2,128)(2,1)S(1)}, bf16[3,6,2,384]{3,2,1,0:T(2,128)(2,1)S(1)}, bf16[3,6,2,384]{3,2,1,0:T(2,128)(2,1)S(1)}, bf16[3,6,2,384]{3,2,1,0:T(2,128)(2,1)S(1)}) custom-call(bf16[432,192]{1,0:T(8,128)(2,1)S(1)} %shard_map.120.y_ref, bf16[216,128]{1,0:T(8,128)(2,1)S(1)} %collective-permute-done.3.got_ref, ...), custom_call_target="tpu_custom_call" | custom-call | flops 4000000000 | bytes 5935104 | tf_op jit(solution)/shard_map/pallas_call | solution.py:321
  41.5 1.9 %collective-permute-start.4 = (bf16[3,6,2,384]{3,2,1,0:T(2,128)(2,1)S(1)}, bf16[3,6,2,384]{3,2,1,0:T(2,128)(2,1)S(1)}, u32[]{:S(2)}, u32[]{:S(2)}) collective-permute-start(bf16[3,6,2,384]{3,2,1,0:T(2,128)(2,1)S(1)} %get-tuple-element.37), channel_id=1, source_target_pairs={{0,1},{1,2},{2,3},{3,4},{4,5},{5,6},{6,7},{7,0},{8,9},{9,10},{10,1... | collective-permute-start | bytes 82952 | tf_op jit(solution)/shard_map/ppermute | solution.py:30
  43.4 2.2 %collective-permute-start.5 = (bf16[3,6,2,384]{3,2,1,0:T(2,128)(2,1)S(1)}, bf16[3,6,2,384]{3,2,1,0:T(2,128)(2,1)S(1)}, u32[]{:S(2)}, u32[]{:S(2)}) collective-permute-start(bf16[3,6,2,384]{3,2,1,0:T(2,128)(2,1)S(1)} %get-tuple-element.38), channel_id=1, source_target_pairs={{0,505},{1,506},{2,507},{3,508},{4,509},{5,510},{6,511},{7,504},{8... | collective-permute-start | bytes 82952 | tf_op jit(solution)/shard_map/ppermute | solution.py:30
  45.6 11.9 %collective-permute-start.6 = (bf16[3,6,2,384]{3,2,1,0:T(2,128)(2,1)S(1)}, bf16[3,6,2,384]{3,2,1,0:T(2,128)(2,1)S(1)}, u32[]{:S(2)}, u32[]{:S(2)}) collective-permute-start(bf16[3,6,2,384]{3,2,1,0:T(2,128)(2,1)S(1)} %get-tuple-element.40), channel_id=1, source_target_pairs={{0,504},{1,505},{2,506},{3,507},{4,508},{5,509},{6,510},{7,511},{8... | collective-permute-start | bytes 82952 | tf_op jit(solution)/shard_map/ppermute | solution.py:30
  57.5 0.0 collective-permute-done.4
  57.5 5.1 %collective-permute-done.5 = bf16[3,6,2,384]{3,2,1,0:T(2,128)(2,1)S(1)} collective-permute-done((bf16[3,6,2,384]{3,2,1,0:T(2,128)(2,1)S(1)}, bf16[3,6,2,384]{3,2,1,0:T(2,128)(2,1)S(1)}, u32[]{:S(2)}, u32[]{:S(2)}) %collective-permute-start.5) | collective-permute-done | bytes 27680 | tf_op jit(solution)/shard_map/ppermute | solution.py:30
  62.6 0.0 collective-permute-done.6
  62.6 0.8 %maximum_bitcast_fusion = bf16[2,6,12,384]{3,0,2,1:T(2,128)(2,1)} fusion(bf16[3,6,2,384]{3,2,1,0:T(2,128)(2,1)S(1)} %collective-permute-done.6, bf16[3,6,2,384]{3,2,1,0:T(2,128)(2,1)S(1)} %get-tuple-element.39, bf16[3,6,2,384]{3,2,1,0:T(2,128)(2,1)S(1)} %collective-permute-done.5, bf16[3,6,2,384]{3,2,1,0:T(2,128)(2,1)S(1)} %collective-permute-done.4), kind=kLoop, calls=%fused_computation | loop fusion | flops 165888 | bytes 221184 | tf_op jit(solution)/shard_map/transpose | solution.py:403
  (2 shorter events, 0.0 us)
Async XLA Ops:
  0.0 26.4 %collective-permute-start = (bf16[2,12,24,192]{3,2,1,0:T(8,128)(2,1)}, bf16[2,12,24,192]{3,2,1,0:T(8,128)(2,1)S(1)}, u32[]{:S(2)}, u32[]{:S(2)}) collective-permute-start(bf16[2,12,24,192]{3,2,1,0:T(8,128)(2,1)} %fields_hbm.1), channel_id=1, source_target_pairs={{0,8},{1,9},{2,10},{3,11},{4,12},{5,13},{6,14},{7,15},{8,16},{9,17... | collective-permute-start | bytes 663560 | tf_op jit(solution)/shard_map/ppermute | solution.py:30
  10.0 24.7 %collective-permute-start.1 = (bf16[162,128]{1,0:T(8,128)(2,1)S(1)}, bf16[162,128]{1,0:T(8,128)(2,1)S(1)}, u32[]{:S(2)}, u32[]{:S(2)}) collective-permute-start(bf16[162,128]{1,0:T(8,128)(2,1)S(1)} %get-tuple-element.24), channel_id=1, source_target_pairs={{0,15},{1,8},{2,9},{3,10},{4,11},{5,12},{6,13},{7,14},{8,23},{9,16... | collective-permute-start | bytes 124424 | tf_op jit(solution)/shard_map/ppermute | solution.py:30
  24.1 10.6 %collective-permute-start.2 = (bf16[162,128]{1,0:T(8,128)(2,1)S(1)}, bf16[162,128]{1,0:T(8,128)(2,1)S(1)}, u32[]{:S(2)}, u32[]{:S(2)}) collective-permute-start(bf16[162,128]{1,0:T(8,128)(2,1)S(1)} %get-tuple-element.25), channel_id=1, source_target_pairs={{0,7},{1,0},{2,1},{3,2},{4,3},{5,4},{6,5},{7,6},{8,15},{9,8},{10,9... | collective-permute-start | bytes 124424 | tf_op jit(solution)/shard_map/ppermute | solution.py:30
  26.5 8.3 %copy-start.4 = (bf16[192,768]{1,0:T(8,128)(2,1)S(1)}, bf16[192,768]{1,0:T(8,128)(2,1)}, u32[]{:S(2)}) copy-start(bf16[192,768]{1,0:T(8,128)(2,1)} %fine_up_ref.1) | copy-start | bytes 884740
  26.5 8.3 %copy-start.5 = (bf16[768,192]{0,1:T(8,128)(2,1)S(1)}, bf16[768,192]{0,1:T(8,128)(2,1)}, u32[]{:S(2)}) copy-start(bf16[768,192]{0,1:T(8,128)(2,1)} %param.17) | copy-start | bytes 884740
  29.0 8.3 %collective-permute-start.3 = (bf16[216,128]{1,0:T(8,128)(2,1)S(1)}, bf16[216,128]{1,0:T(8,128)(2,1)S(1)}, u32[]{:S(2)}, u32[]{:S(2)}) collective-permute-start(bf16[216,128]{1,0:T(8,128)(2,1)S(1)} %get-tuple-element.35), channel_id=1, source_target_pairs={{0,7},{1,0},{2,1},{3,2},{4,3},{5,4},{6,5},{7,6},{8,15},{9,8},{10,9... | collective-permute-start | bytes 165896 | tf_op jit(solution)/shard_map/ppermute | solution.py:30
  34.7 2.5 %copy-start = (bf16[384,1536]{1,0:T(8,128)(2,1)S(1)}, bf16[384,1536]{1,0:T(8,128)(2,1)}, u32[]{:S(2)}) copy-start(bf16[384,1536]{1,0:T(8,128)(2,1)} %up_ref.3) | copy-start | bytes 3538948
  34.7 2.5 %copy-start.1 = (bf16[1536,384]{1,0:T(8,128)(2,1)S(1)}, bf16[1536,384]{1,0:T(8,128)(2,1)}, u32[]{:S(2)}) copy-start(bf16[1536,384]{1,0:T(8,128)(2,1)} %down_ref.1) | copy-start | bytes 3538948
  34.8 2.5 %copy-start.2 = (bf16[384,1152]{1,0:T(8,128)(2,1)S(1)}, bf16[384,1152]{1,0:T(8,128)(2,1)}, u32[]{:S(2)}) copy-start(bf16[384,1152]{1,0:T(8,128)(2,1)} %qkv_ref.1) | copy-start | bytes 2654212
  34.8 2.5 %copy-start.3 = (bf16[768,384]{1,0:T(8,128)(2,1)S(1)}, bf16[768,384]{1,0:T(8,128)(2,1)}, u32[]{:S(2)}) copy-start(bf16[768,384]{1,0:T(8,128)(2,1)} %merge_ref.1) | copy-start | bytes 1769476
  34.8 2.5 %copy-start.6 = (bf16[384,384]{1,0:T(8,128)(2,1)S(1)}, bf16[384,384]{1,0:T(8,128)(2,1)}, u32[]{:S(2)}) copy-start(bf16[384,384]{1,0:T(8,128)(2,1)} %proj_ref.1) | copy-start | bytes 884740
  41.5 16.0 %collective-permute-start.4 = (bf16[3,6,2,384]{3,2,1,0:T(2,128)(2,1)S(1)}, bf16[3,6,2,384]{3,2,1,0:T(2,128)(2,1)S(1)}, u32[]{:S(2)}, u32[]{:S(2)}) collective-permute-start(bf16[3,6,2,384]{3,2,1,0:T(2,128)(2,1)S(1)} %get-tuple-element.37), channel_id=1, source_target_pairs={{0,1},{1,2},{2,3},{3,4},{4,5},{5,6},{6,7},{7,0},{8,9},{9,10},{10,1... | collective-permute-start | bytes 82952 | tf_op jit(solution)/shard_map/ppermute | solution.py:30
  43.4 19.2 %collective-permute-start.5 = (bf16[3,6,2,384]{3,2,1,0:T(2,128)(2,1)S(1)}, bf16[3,6,2,384]{3,2,1,0:T(2,128)(2,1)S(1)}, u32[]{:S(2)}, u32[]{:S(2)}) collective-permute-start(bf16[3,6,2,384]{3,2,1,0:T(2,128)(2,1)S(1)} %get-tuple-element.38), channel_id=1, source_target_pairs={{0,505},{1,506},{2,507},{3,508},{4,509},{5,510},{6,511},{7,504},{8... | collective-permute-start | bytes 82952 | tf_op jit(solution)/shard_map/ppermute | solution.py:30
  45.6 17.0 %collective-permute-start.6 = (bf16[3,6,2,384]{3,2,1,0:T(2,128)(2,1)S(1)}, bf16[3,6,2,384]{3,2,1,0:T(2,128)(2,1)S(1)}, u32[]{:S(2)}, u32[]{:S(2)}) collective-permute-start(bf16[3,6,2,384]{3,2,1,0:T(2,128)(2,1)S(1)} %get-tuple-element.40), channel_id=1, source_target_pairs={{0,504},{1,505},{2,506},{3,507},{4,508},{5,509},{6,510},{7,511},{8... | collective-permute-start | bytes 82952 | tf_op jit(solution)/shard_map/ppermute | solution.py:30

commit v6 on v5

--- a/solution.py
+++ b/solution.py
@@ -72,28 +72,33 @@
 
 def expand_bias(tables, outs, stacked, spread_from):
     stacked[...] = jnp.zeros_like(stacked)
-    spread_from[...] = jnp.zeros_like(spread_from)
-    row = iota((CELLS, CELLS), 0)
-    key, query = row // LINES, row % LINES
+    row = iota((LINES * 16, CELLS), 0)
+    key, query = row // 16, row % 16
     z_key, z_query = 1 - key // WLAT, 1 - query // WLAT
     column = ((z_query * WZ + z_key) * WLAT + query % WLAT) * WLAT + key % WLAT
-    pick = (iota((CELLS, CELLS), 1) == column).astype(f32).astype(bf16)
+    pick = ((iota((LINES * 16, CELLS), 1) == column) & (query < LINES)).astype(f32).astype(bf16)
     row = iota((LINES * 32, 384), 0)
     lane = iota((LINES * 32, 384), 1)
     spread = (lane == (SPAN - 1 - row % 32) * LINES + row // 32) & (row % 32 < SPAN)
     spread = spread.astype(f32).astype(bf16)
-    row, lane = iota((6 * LINES, 384), 0) % LINES, iota((6 * LINES, 384), 1) % LINES
+    row, lane = iota((6 * 16, 384), 0) % 16, iota((6 * 16, 384), 1) % LINES
     levels_differ = row // WLAT != lane // WLAT
     rows_differ = (row % WLAT >= WLAT // 2) != (lane % WLAT >= WLAT // 2)
+    slot = iota((16, 128), 1) // 32
     for (table_of, last), out_of in zip(tables, outs, strict=True):
         for head in range(6):
-            stacked[head * 24 : head * 24 + SPAN, :] = table_of(head)
+            stacked[head * 32 : head * 32 + SPAN, :] = table_of(head)
         picked = sum(dot_nt(pick, part) for part in three_parts(stacked[...]))
+        picked = [picked[:, :128], jnp.concatenate([picked[:, 128:], jnp.zeros((LINES * 16, 64), f32)], axis=-1)]
+        rolled = [[half] + [pltpu.roll(half, 32 * r, 1) for r in range(1, 4)] for half in picked]
         for head in range(6):
-            for key in range(LINES):
-                spread_from[head * LINES : (head + 1) * LINES, key * 32 : key * 32 + 24] = picked[
-                    key * LINES : (key + 1) * LINES, head * 24 : (head + 1) * 24
-                ]
+            for group in range(3):
+                block = None
+                for at in range(4):
+                    key = group * 4 + at
+                    piece = rolled[head // 4][(at - head) % 4][key * 16 : (key + 1) * 16]
+                    block = piece if block is None else jnp.where(slot == at, piece, block)
+                spread_from[head * 16 : (head + 1) * 16, group * 128 : (group + 1) * 128] = block
         flat = sum(dot(part, spread) for part in three_parts(spread_from[...]))
         apart = levels_differ if last is None else levels_differ | (rows_differ & (last > 0))
         flat = jnp.where(apart, MASKED, flat)
@@ -101,7 +106,7 @@
             start = (WLON - 1 - o) * LINES
             piece = flat[:, start : start + CELLS]
             for head in range(6):
-                out_of(head, o * LINES, piece[head * LINES : (head + 1) * LINES])
+                out_of(head, o * LINES, piece[head * 16 : head * 16 + LINES])
 
 
 def writer(out_ref, base):
@@ -159,15 +164,13 @@
     return jnp.concatenate([first, second], axis=-1)
 
 
-def expand_all(last, fine_ref, coarse_ref, bias0_ref, bias1_ref, bias2_ref, stacked, spread_from):
-    tables = [
-        (reader(fine_ref, 0, 0), None),
-        (reader(fine_ref, 1, 0), last),
-        (reader(coarse_ref, 0, 0), last),
-        (reader(coarse_ref, 0, 6), last),
-    ]
-    outs = [writer(bias0_ref, 0), writer(bias1_ref, 0), writer(bias2_ref, 0), writer(bias2_ref, 6)]
-    expand_bias(tables, outs, stacked, spread_from)
+def expand_first(fine_ref, bias0_ref, stacked, spread_from):
+    expand_bias([(reader(fine_ref, 0, 0), None)], [writer(bias0_ref, 0)], stacked, spread_from)
+
+
+def expand_others(last, fine_ref, coarse_ref, bias1_ref, bias2_ref, stacked, spread_from):
+    tables = [(reader(fine_ref, 1, 0), last), (reader(coarse_ref, 0, 0), last), (reader(coarse_ref, 0, 6), last)]
+    expand_bias(tables, [writer(bias1_ref, 0), writer(bias2_ref, 0), writer(bias2_ref, 6)], stacked, spread_from)
 
 
 def prepare_kernel(
@@ -198,10 +201,17 @@
 
     @pl.when(flags_ref[1] > 0)
     def _():
-        expand_all(flags_ref[0], fine_ref, coarse_ref, bias0_ref, bias1_ref, bias2_ref, stacked, spread_from)
-
-
-def attend_fine(x_ref, bias_ref, qkv_ref, proj_ref):
+        expand_first(fine_ref, bias0_ref, stacked, spread_from)
+        expand_others(flags_ref[0], fine_ref, coarse_ref, bias1_ref, bias2_ref, stacked, spread_from)
+
+
+def other_bias_kernel(flags_ref, fine_ref, coarse_ref, after_ref, bias1_ref, bias2_ref, stacked, spread_from):
+    @pl.when(flags_ref[1] == 0)
+    def _():
+        expand_others(flags_ref[0], fine_ref, coarse_ref, bias1_ref, bias2_ref, stacked, spread_from)
+
+
+def attend_fine(x_ref, bias, qkv_ref, proj_ref):
     normed = normalise(get(x_ref, 72, 432, 1, 192))
     q = dot(normed, qkv_ref[:, 0:192]).astype(bf16).astype(f32)
     k = dot(normed, qkv_ref[:, 192:384]).astype(bf16)
@@ -211,34 +221,33 @@
         at = window * CELLS
         q_rows = q[at + start : at + stop]
         k_rows, v_rows = k[at : at + CELLS], v[at : at + CELLS]
-        bias = bias_ref[:, start:stop, :]
-        left.append(attend_group(q_rows[:, :128], k_rows[:, :128], v_rows[:, :128], bias[:4], 4))
-        right.append(attend_group(q_rows[:, 128:], k_rows[:, 128:], v_rows[:, 128:], bias[4:], 2))
+        left.append(attend_group(q_rows[:, :128], k_rows[:, :128], v_rows[:, :128], bias(0, 4, start, stop), 4))
+        right.append(attend_group(q_rows[:, 128:], k_rows[:, 128:], v_rows[:, 128:], bias(4, 6, start, stop), 2))
     left = jnp.concatenate(left, axis=0).astype(bf16)
     right = jnp.concatenate(right, axis=0).astype(bf16)
     product = dot(left, proj_ref[0:128, :]) + dot(right, proj_ref[128:192, :])
     return (get(x_ref, 144, 288, 1, 192) + product).astype(bf16)
 
 
+def early_or_late(flags_ref, early_ref, late_ref):
+    return lambda head, last, start, stop: jnp.where(
+        flags_ref[1] > 0, early_ref[head:last, start:stop, :], late_ref[head:last, start:stop, :]
+    )
+
+
 def first_rows_kernel(
-    flags_ref, left_ref, own_ref, fine_ref, coarse_ref, old0_ref, old1_ref, old2_ref, qkv_ref, proj_ref,
-    out_ref, send_ref, bias1_ref, bias2_ref, bias0_ref, x_ref, a_ref, stacked, spread_from,
+    flags_ref, left_ref, own_ref, fine_ref, early0_ref, qkv_ref, proj_ref,
+    out_ref, send_ref, late0_ref, x_ref, a_ref, stacked, spread_from,
 ):
-    @pl.when(flags_ref[1] > 0)
-    def _():
-        bias0_ref[...] = old0_ref[...]
-        bias1_ref[...] = old1_ref[...]
-        bias2_ref[...] = old2_ref[...]
-
     @pl.when(flags_ref[1] == 0)
     def _():
-        expand_all(flags_ref[0], fine_ref, coarse_ref, bias0_ref, bias1_ref, bias2_ref, stacked, spread_from)
+        expand_first(fine_ref, late0_ref, stacked, spread_from)
 
     for z in range(WZ):
         for a in range(WLAT):
             put(x_ref, z * WLAT + a, 24, LINES, left_ref[z, 3 + a].astype(f32))
             put(x_ref, 288 + z * WLAT + a, 24, LINES, own_ref[z, 3 + a].astype(f32))
-    attended = attend_fine(x_ref, bias0_ref, qkv_ref, proj_ref)
+    attended = attend_fine(x_ref, early_or_late(flags_ref, early0_ref, late0_ref), qkv_ref, proj_ref)
     out_ref[...] = attended
     put(a_ref, 0, 288, 1, attended.astype(f32))
     lines = [a_ref[t, pl.ds(z * WLAT + a, 24, stride=LINES), :] for t in range(2) for z in range(WZ) for a in range(3)]
@@ -246,8 +255,8 @@
 
 
 def second_rows_kernel(
-    left_ref, own_ref, corner_ref, below_ref, first_ref, bias1_ref, qkv_ref, proj_ref, up_ref, down_ref,
-    out_ref, x_ref, a_ref, w_ref,
+    flags_ref, left_ref, own_ref, corner_ref, below_ref, first_ref, early1_ref, late1_ref, qkv_ref, proj_ref, up_ref,
+    down_ref, out_ref, x_ref, a_ref, w_ref,
 ):
     below, corner = below_ref[...].astype(f32), corner_ref[...].astype(f32)
     for z in range(WZ):
@@ -260,7 +269,8 @@
                 put(x_ref, 72 + at, 18, LINES, unpack_line(corner, z * 3 + a - 3, 18))
                 put(x_ref, 288 + at, 18, LINES, unpack_line(below, z * 3 + a - 3, 18))
     put(a_ref, 0, 288, 1, first_ref[...].astype(f32))
-    put(a_ref, 288, 288, 1, attend_fine(x_ref, bias1_ref, qkv_ref, proj_ref).astype(f32))
+    bias = early_or_late(flags_ref, early1_ref, late1_ref)
+    put(a_ref, 288, 288, 1, attend_fine(x_ref, bias, qkv_ref, proj_ref).astype(f32))
     for t in range(2):
         for rho in range(3, 12):
             for z in range(WZ):
@@ -273,7 +283,7 @@
 
 
 def coarse_kernel(
-    y_ref, got_ref, fine_up_ref, fine_down_ref, merge_ref, bias_ref, qkv_ref, proj_ref, up_ref, down_ref,
+    flags_ref, y_ref, got_ref, fine_up_ref, fine_down_ref, merge_ref, early2_ref, late2_ref, qkv_ref, proj_ref, up_ref, down_ref,
     keep_ref, lower_ref, corner_ref, left_ref, w_ref, p_ref, o_ref,
 ):
     got = got_ref[...].astype(f32)
@@ -301,11 +311,12 @@
     normed = normalise(merged)
     qkv = dot(normed, qkv_ref[...]).astype(bf16)
     product = merged
+    bias = early_or_late(flags_ref, early2_ref, late2_ref)
     for g in range(3):
         q = qkv[:, g * 128 : (g + 1) * 128].astype(f32)
         k = qkv[:, 384 + g * 128 : 384 + (g + 1) * 128]
         v = qkv[:, 768 + g * 128 : 768 + (g + 1) * 128]
-        mixed = attend_group(q, k, v, bias_ref[g * 4 : (g + 1) * 4], 4)
+        mixed = attend_group(q, k, v, bias(g * 4, (g + 1) * 4, 0, CELLS), 4)
         product = product + dot(mixed.astype(bf16), proj_ref[g * 128 : (g + 1) * 128, :])
     attended = product.astype(bf16).astype(f32)
     put(o_ref, 0, CELLS, 1, feed_forward(attended, up_ref, down_ref))
@@ -353,7 +364,7 @@
     fine_tables = fine_bias.transpose(0, 2, 3, 1, 4)
     coarse_tables = coarse_bias.transpose(0, 2, 3, 1, 4)
     fine_down = fine_down.T
-    expansion = [((CELLS, CELLS), f32), ((6 * LINES, LINES * 32), f32)]
+    expansion = [((6 * 32, CELLS), f32), ((6 * 16, LINES * 32), f32)]
     biases = [((6, CELLS, CELLS), f32), ((12, CELLS, CELLS), f32)]
     left = from_behind(fields, 1, 0)
     sources = [fields, fine_tables, coarse_tables, fine_qkv, fine_proj]
@@ -372,29 +383,35 @@
     )(flags, *(pltpu.with_memory_space_constraint(source, pltpu.HBM) for source in sources))
     corner = from_behind(corner, 1, -1)
     below = from_behind(below, 0, -1)
-    first, edge, bias1, bias2 = call(
+    first, edge = call(
         first_rows_kernel,
-        [((288, 192), bf16), ((216, 128), bf16)] + biases,
+        [((288, 192), bf16), ((216, 128), bf16)],
         [((6, CELLS, CELLS), f32), tiles_of(576, 192), tiles_of(288, 192)] + expansion,
-        [flags, left, own, fine_tables, coarse_tables, bias0, bias1, bias2, fine_qkv, fine_proj],
+        [flags, left, own, fine_tables, bias0, fine_qkv, fine_proj],
         1_000_000_000,
         smem=1,
     )
     got = from_behind(edge, 0, -1)
+    late1, late2 = call(
+        other_bias_kernel, biases, expansion, [flags, fine_tables, coarse_tables, first], 2_000_000_000, smem=1
+    )
     (finished,) = call(
         second_rows_kernel,
         [((432, 192), bf16)],
         [tiles_of(576, 192), tiles_of(576, 192), tiles_of(432, 192)],
-        [left, own, corner, below, first, bias1, fine_qkv, fine_proj, fine_up, fine_down],
+        [flags, left, own, corner, below, first, bias1, late1, fine_qkv, fine_proj, fine_up, fine_down],
         3_000_000_000,
+        smem=1,
     )
     quarter = ((3, 6, WZ, 384), bf16)
     keep, lower, far_corner, upper_left = call(
         coarse_kernel,
         [quarter] * 4,
         [tiles_of(576, 192), tiles_of(576, 192), tiles_of(CELLS, 384)],
-        [finished, got, fine_up, fine_down, merge_weight, bias2, coarse_qkv, coarse_proj, coarse_up, coarse_down],
+        [flags, finished, got, fine_up, fine_down, merge_weight, bias2, late2]
+        + [coarse_qkv, coarse_proj, coarse_up, coarse_down],
         4_000_000_000,
+        smem=1,
     )
     above = from_behind(lower, 0, 1)
     corner = from_behind(far_corner, -1, 1)

time: 63.7 us -> 63.6 us (level)
  the two profiles are of different devices: /device:TPU:1 before, /device:TPU:511 now
where the time goes in v6:
time: 63.6 us; the launch traced here: 63.3 us
  starting transfers between devices  25.6 us (40%)
  waiting for transfers between devices  20.1 us (32%)
  Pallas kernels  16.4 us (26%)
  other arithmetic  0.88 us (1%)
    ppermute x7, starting transfers between devices, from_behind(): return lax.ppermute(shard, ('lon', 'lat'), pairs)  25.6 us
    ppermute x7, waiting for transfers between devices, from_behind(): return lax.ppermute(shard, ('lon', 'lat'), pairs)  20.1 us
    pallas_call x4, Pallas kernels, call(): pl.pallas_call(kernel, out_shape=[jax.ShapeDtypeStruct(shape, dtype) for...  14.6 us
    pallas_call x1, Pallas kernels, body(): pl.pallas_call(prepare_kernel, out_shape=[jax.ShapeDtypeStruct((162, 128)...  1.84 us
  transfers between devices with their start and end apart: 7, of which 4 were waited for; matrix products, arithmetic and copies ran while one was open for 0% of the time, Pallas kernels for 18%

profile of v6, /device:TPU:511, one launch (start us, length us, event | category | flops | bytes accessed | tf_op | source)
XLA Modules:
  0.0 63.3 jit_solution(13146740670345469851)
XLA Ops:
  0.0 7.0 %collective-permute-start = (bf16[2,12,24,192]{3,2,1,0:T(8,128)(2,1)}, bf16[2,12,24,192]{3,2,1,0:T(8,128)(2,1)S(1)}, u32[]{:S(2)}, u32[]{:S(2)}) collective-permute-start(bf16[2,12,24,192]{3,2,1,0:T(8,128)(2,1)} %fields_hbm.1), channel_id=1, source_target_pairs={{0,8},{1,9},{2,10},{3,11},{4,12},{5,13},{6,14},{7,15},{8,16},{9,17... | collective-permute-start | bytes 663560 | tf_op jit(solution)/shard_map/ppermute | solution.py:30
  7.0 0.1 add_convert_fusion.flags_ref
  7.1 1.8 %shard_map.118 = (bf16[162,128]{1,0:T(8,128)(2,1)S(1)}, bf16[162,128]{1,0:T(8,128)(2,1)S(1)}, bf16[2,12,24,192]{3,2,1,0:T(8,128)(2,1)S(1)}, f32[2,6,23,1,144]{4,...) custom-call(s32[2]{0:T(128)S(1)} %add_convert_fusion.flags_ref, ...), custom_call_target="tpu_custom_call" | custom-call | tf_op jit(solution)/shard_map/pallas_call | solution.py:372
  8.9 2.1 %collective-permute-start.1 = (bf16[162,128]{1,0:T(8,128)(2,1)S(1)}, bf16[162,128]{1,0:T(8,128)(2,1)S(1)}, u32[]{:S(2)}, u32[]{:S(2)}) collective-permute-start(bf16[162,128]{1,0:T(8,128)(2,1)S(1)} %get-tuple-element.24), channel_id=1, source_target_pairs={{0,15},{1,8},{2,9},{3,10},{4,11},{5,12},{6,13},{7,14},{8,23},{9,16... | collective-permute-start | bytes 124424 | tf_op jit(solution)/shard_map/ppermute | solution.py:30
  11.0 2.2 %collective-permute-start.2 = (bf16[162,128]{1,0:T(8,128)(2,1)S(1)}, bf16[162,128]{1,0:T(8,128)(2,1)S(1)}, u32[]{:S(2)}, u32[]{:S(2)}) collective-permute-start(bf16[162,128]{1,0:T(8,128)(2,1)S(1)} %get-tuple-element.25), channel_id=1, source_target_pairs={{0,7},{1,0},{2,1},{3,2},{4,3},{5,4},{6,5},{7,6},{8,15},{9,8},{10,9... | collective-permute-start | bytes 124424 | tf_op jit(solution)/shard_map/ppermute | solution.py:30
  13.2 0.0 collective-permute-done.left_ref
  13.2 3.5 %shard_map.119 = (bf16[288,192]{1,0:T(8,128)(2,1)S(1)}, bf16[216,128]{1,0:T(8,128)(2,1)S(1)}) custom-call(s32[2]{0:T(128)S(1)} %add_convert_fusion.flags_ref, bf16[2,12,24,192]{3,2,1,0:T(8,128)(2,1)S(1)} %collective-permute-done.left_ref, bf16[2,12,24,192]{3,2,1,0:T(8,128)(2,1)S(1)} %get-tuple-element.23.own_ref, ...), custom_call_target="tpu_custom_call" | custom-call | flops 1000000000 | bytes 1393928 | tf_op jit(solution)/shard_map/pallas_call | solution.py:332
  16.7 2.1 %collective-permute-start.3 = (bf16[216,128]{1,0:T(8,128)(2,1)S(1)}, bf16[216,128]{1,0:T(8,128)(2,1)S(1)}, u32[]{:S(2)}, u32[]{:S(2)}) collective-permute-start(bf16[216,128]{1,0:T(8,128)(2,1)S(1)} %get-tuple-element.34), channel_id=1, source_target_pairs={{0,7},{1,0},{2,1},{3,2},{4,3},{5,4},{6,5},{7,6},{8,15},{9,8},{10,9... | collective-permute-start | bytes 165896 | tf_op jit(solution)/shard_map/ppermute | solution.py:30
  18.8 0.0 copy-start.4
  18.8 0.0 copy-start.5
  18.8 3.2 %shard_map.120 = (f32[6,144,144]{2,1,0:T(8,128)S(1)}, f32[12,144,144]{2,1,0:T(8,128)S(1)}) custom-call(s32[2]{0:T(128)S(1)} %add_convert_fusion.flags_ref, f32[2,6,23,1,144]{4,3,2,1,0:T(1,128)S(1)} %get-tuple-element.26.fine_ref, f32[1,12,23,1,144]{4,3,2,1,0:T(1,128)S(1)} %get-tuple-element.32.coarse_ref, ...), custom_call_target="tpu_custom_call" | custom-call | flops 2000000000 | bytes 428552 | tf_op jit(solution)/shard_map/pallas_call | solution.py:332
  22.1 7.7 %collective-permute-done.1.corner_ref = bf16[162,128]{1,0:T(8,128)(2,1)S(1)} collective-permute-done((bf16[162,128]{1,0:T(8,128)(2,1)S(1)}, bf16[162,128]{1,0:T(8,128)(2,1)S(1)}, u32[]{:S(2)}, u32[]{:S(2)}) %collective-permute-start.1) | collective-permute-done | bytes 41504 | tf_op jit(solution)/shard_map/ppermute | solution.py:30
  29.8 0.5 collective-permute-done.2.below_ref
  30.2 0.0 copy-done.4
  30.2 0.0 copy-done.5
  30.3 0.0 copy-start.2
  30.3 0.0 copy-start.3
  30.3 0.0 copy-start.6
  30.3 3.1 %shard_map.121.y_ref = bf16[432,192]{1,0:T(8,128)(2,1)S(1)} custom-call(s32[2]{0:T(128)S(1)} %add_convert_fusion.flags_ref, bf16[2,12,24,192]{3,2,1,0:T(8,128)(2,1)S(1)} %collective-permute-done.left_ref, bf16[2,12,24,192]{3,2,1,0:T(8,128)(2,1)S(1)} %get-tuple-element.23.own_ref, bf16[162,128]{1,0:T(8,128)(2,1)S(1)} %collective-permute-done.1.corner_ref, ...), custom_call_target="tpu_custom_call" | custom-call | flops 3000000000 | bytes 2515976 | tf_op jit(solution)/shard_map/pallas_call | solution.py:332
  33.4 0.0 collective-permute-done.3.got_ref
  33.4 0.0 copy-done
  33.4 0.0 copy-done.1
  33.4 0.0 copy-done.2
  33.4 0.0 copy-done.3
  33.4 4.8 %shard_map.122 = (bf16[3,6,2,384]{3,2,1,0:T(2,128)(2,1)S(1)}, bf16[3,6,2,384]{3,2,1,0:T(2,128)(2,1)S(1)}, bf16[3,6,2,384]{3,2,1,0:T(2,128)(2,1)S(1)}, bf16[3,6,2,384]{3,2,1,0:T(2,128)(2,1)S(1)}) custom-call(s32[2]{0:T(128)S(1)} %add_convert_fusion.flags_ref, bf16[432,192]{1,0:T(8,128)(2,1)S(1)} %shard_map.121.y_ref, ...), custom_call_target="tpu_custom_call" | custom-call | flops 4000000000 | bytes 6930440 | tf_op jit(solution)/shard_map/pallas_call | solution.py:332
  38.2 5.9 %collective-permute-start.4 = (bf16[3,6,2,384]{3,2,1,0:T(2,128)(2,1)S(1)}, bf16[3,6,2,384]{3,2,1,0:T(2,128)(2,1)S(1)}, u32[]{:S(2)}, u32[]{:S(2)}) collective-permute-start(bf16[3,6,2,384]{3,2,1,0:T(2,128)(2,1)S(1)} %get-tuple-element.37), channel_id=1, source_target_pairs={{0,1},{1,2},{2,3},{3,4},{4,5},{5,6},{6,7},{7,0},{8,9},{9,10},{10,1... | collective-permute-start | bytes 82952 | tf_op jit(solution)/shard_map/ppermute | solution.py:30
  44.1 4.5 %collective-permute-start.5 = (bf16[3,6,2,384]{3,2,1,0:T(2,128)(2,1)S(1)}, bf16[3,6,2,384]{3,2,1,0:T(2,128)(2,1)S(1)}, u32[]{:S(2)}, u32[]{:S(2)}) collective-permute-start(bf16[3,6,2,384]{3,2,1,0:T(2,128)(2,1)S(1)} %get-tuple-element.38), channel_id=1, source_target_pairs={{0,505},{1,506},{2,507},{3,508},{4,509},{5,510},{6,511},{7,504},{8... | collective-permute-start | bytes 82952 | tf_op jit(solution)/shard_map/ppermute | solution.py:30
  48.6 1.9 %collective-permute-start.6 = (bf16[3,6,2,384]{3,2,1,0:T(2,128)(2,1)S(1)}, bf16[3,6,2,384]{3,2,1,0:T(2,128)(2,1)S(1)}, u32[]{:S(2)}, u32[]{:S(2)}) collective-permute-start(bf16[3,6,2,384]{3,2,1,0:T(2,128)(2,1)S(1)} %get-tuple-element.40), channel_id=1, source_target_pairs={{0,504},{1,505},{2,506},{3,507},{4,508},{5,509},{6,510},{7,511},{8... | collective-permute-start | bytes 82952 | tf_op jit(solution)/shard_map/ppermute | solution.py:30
  50.5 0.0 collective-permute-done.4
  50.5 8.4 %collective-permute-done.5 = bf16[3,6,2,384]{3,2,1,0:T(2,128)(2,1)S(1)} collective-permute-done((bf16[3,6,2,384]{3,2,1,0:T(2,128)(2,1)S(1)}, bf16[3,6,2,384]{3,2,1,0:T(2,128)(2,1)S(1)}, u32[]{:S(2)}, u32[]{:S(2)}) %collective-permute-start.5) | collective-permute-done | bytes 27680 | tf_op jit(solution)/shard_map/ppermute | solution.py:30
  58.9 3.6 %collective-permute-done.6 = bf16[3,6,2,384]{3,2,1,0:T(2,128)(2,1)S(1)} collective-permute-done((bf16[3,6,2,384]{3,2,1,0:T(2,128)(2,1)S(1)}, bf16[3,6,2,384]{3,2,1,0:T(2,128)(2,1)S(1)}, u32[]{:S(2)}, u32[]{:S(2)}) %collective-permute-start.6) | collective-permute-done | bytes 27680 | tf_op jit(solution)/shard_map/ppermute | solution.py:30
  62.5 0.8 %maximum_bitcast_fusion = bf16[2,6,12,384]{3,0,2,1:T(2,128)(2,1)} fusion(bf16[3,6,2,384]{3,2,1,0:T(2,128)(2,1)S(1)} %collective-permute-done.6, bf16[3,6,2,384]{3,2,1,0:T(2,128)(2,1)S(1)} %get-tuple-element.39, bf16[3,6,2,384]{3,2,1,0:T(2,128)(2,1)S(1)} %collective-permute-done.5, bf16[3,6,2,384]{3,2,1,0:T(2,128)(2,1)S(1)} %collective-permute-done.4), kind=kLoop, calls=%fused_computation | loop fusion | flops 165888 | bytes 221184 | tf_op jit(solution)/shard_map/transpose | solution.py:420
  (3 shorter events, 0.0 us)
Async XLA Ops:
  0.0 13.2 %collective-permute-start = (bf16[2,12,24,192]{3,2,1,0:T(8,128)(2,1)}, bf16[2,12,24,192]{3,2,1,0:T(8,128)(2,1)S(1)}, u32[]{:S(2)}, u32[]{:S(2)}) collective-permute-start(bf16[2,12,24,192]{3,2,1,0:T(8,128)(2,1)} %fields_hbm.1), channel_id=1, source_target_pairs={{0,8},{1,9},{2,10},{3,11},{4,12},{5,13},{6,14},{7,15},{8,16},{9,17... | collective-permute-start | bytes 663560 | tf_op jit(solution)/shard_map/ppermute | solution.py:30
  8.9 20.8 %collective-permute-start.1 = (bf16[162,128]{1,0:T(8,128)(2,1)S(1)}, bf16[162,128]{1,0:T(8,128)(2,1)S(1)}, u32[]{:S(2)}, u32[]{:S(2)}) collective-permute-start(bf16[162,128]{1,0:T(8,128)(2,1)S(1)} %get-tuple-element.24), channel_id=1, source_target_pairs={{0,15},{1,8},{2,9},{3,10},{4,11},{5,12},{6,13},{7,14},{8,23},{9,16... | collective-permute-start | bytes 124424 | tf_op jit(solution)/shard_map/ppermute | solution.py:30
  11.0 19.2 %collective-permute-start.2 = (bf16[162,128]{1,0:T(8,128)(2,1)S(1)}, bf16[162,128]{1,0:T(8,128)(2,1)S(1)}, u32[]{:S(2)}, u32[]{:S(2)}) collective-permute-start(bf16[162,128]{1,0:T(8,128)(2,1)S(1)} %get-tuple-element.25), channel_id=1, source_target_pairs={{0,7},{1,0},{2,1},{3,2},{4,3},{5,4},{6,5},{7,6},{8,15},{9,8},{10,9... | collective-permute-start | bytes 124424 | tf_op jit(solution)/shard_map/ppermute | solution.py:30
  16.7 16.7 %collective-permute-start.3 = (bf16[216,128]{1,0:T(8,128)(2,1)S(1)}, bf16[216,128]{1,0:T(8,128)(2,1)S(1)}, u32[]{:S(2)}, u32[]{:S(2)}) collective-permute-start(bf16[216,128]{1,0:T(8,128)(2,1)S(1)} %get-tuple-element.34), channel_id=1, source_target_pairs={{0,7},{1,0},{2,1},{3,2},{4,3},{5,4},{6,5},{7,6},{8,15},{9,8},{10,9... | collective-permute-start | bytes 165896 | tf_op jit(solution)/shard_map/ppermute | solution.py:30
  18.8 11.4 %copy-start.4 = (bf16[192,768]{1,0:T(8,128)(2,1)S(1)}, bf16[192,768]{1,0:T(8,128)(2,1)}, u32[]{:S(2)}) copy-start(bf16[192,768]{1,0:T(8,128)(2,1)} %fine_up_ref.1) | copy-start | bytes 884740
  18.8 11.4 %copy-start.5 = (bf16[768,192]{0,1:T(8,128)(2,1)S(1)}, bf16[768,192]{0,1:T(8,128)(2,1)}, u32[]{:S(2)}) copy-start(bf16[768,192]{0,1:T(8,128)(2,1)} %param.17) | copy-start | bytes 884740
  30.2 3.2 %copy-start = (bf16[384,1536]{1,0:T(8,128)(2,1)S(1)}, bf16[384,1536]{1,0:T(8,128)(2,1)}, u32[]{:S(2)}) copy-start(bf16[384,1536]{1,0:T(8,128)(2,1)} %up_ref.3) | copy-start | bytes 3538948
  30.3 3.2 %copy-start.1 = (bf16[1536,384]{1,0:T(8,128)(2,1)S(1)}, bf16[1536,384]{1,0:T(8,128)(2,1)}, u32[]{:S(2)}) copy-start(bf16[1536,384]{1,0:T(8,128)(2,1)} %down_ref.1) | copy-start | bytes 3538948
  30.3 3.2 %copy-start.2 = (bf16[384,1152]{1,0:T(8,128)(2,1)S(1)}, bf16[384,1152]{1,0:T(8,128)(2,1)}, u32[]{:S(2)}) copy-start(bf16[384,1152]{1,0:T(8,128)(2,1)} %qkv_ref.1) | copy-start | bytes 2654212
  30.3 3.2 %copy-start.3 = (bf16[768,384]{1,0:T(8,128)(2,1)S(1)}, bf16[768,384]{1,0:T(8,128)(2,1)}, u32[]{:S(2)}) copy-start(bf16[768,384]{1,0:T(8,128)(2,1)} %merge_ref.1) | copy-start | bytes 1769476
  30.3 3.2 %copy-start.6 = (bf16[384,384]{1,0:T(8,128)(2,1)S(1)}, bf16[384,384]{1,0:T(8,128)(2,1)}, u32[]{:S(2)}) copy-start(bf16[384,384]{1,0:T(8,128)(2,1)} %proj_ref.1) | copy-start | bytes 884740
  38.2 12.3 %collective-permute-start.4 = (bf16[3,6,2,384]{3,2,1,0:T(2,128)(2,1)S(1)}, bf16[3,6,2,384]{3,2,1,0:T(2,128)(2,1)S(1)}, u32[]{:S(2)}, u32[]{:S(2)}) collective-permute-start(bf16[3,6,2,384]{3,2,1,0:T(2,128)(2,1)S(1)} %get-tuple-element.37), channel_id=1, source_target_pairs={{0,1},{1,2},{2,3},{3,4},{4,5},{5,6},{6,7},{7,0},{8,9},{9,10},{10,1... | collective-permute-start | bytes 82952 | tf_op jit(solution)/shard_map/ppermute | solution.py:30
  44.1 14.8 %collective-permute-start.5 = (bf16[3,6,2,384]{3,2,1,0:T(2,128)(2,1)S(1)}, bf16[3,6,2,384]{3,2,1,0:T(2,128)(2,1)S(1)}, u32[]{:S(2)}, u32[]{:S(2)}) collective-permute-start(bf16[3,6,2,384]{3,2,1,0:T(2,128)(2,1)S(1)} %get-tuple-element.38), channel_id=1, source_target_pairs={{0,505},{1,506},{2,507},{3,508},{4,509},{5,510},{6,511},{7,504},{8... | collective-permute-start | bytes 82952 | tf_op jit(solution)/shard_map/ppermute | solution.py:30
  48.6 13.9 %collective-permute-start.6 = (bf16[3,6,2,384]{3,2,1,0:T(2,128)(2,1)S(1)}, bf16[3,6,2,384]{3,2,1,0:T(2,128)(2,1)S(1)}, u32[]{:S(2)}, u32[]{:S(2)}) collective-permute-start(bf16[3,6,2,384]{3,2,1,0:T(2,128)(2,1)S(1)} %get-tuple-element.40), channel_id=1, source_target_pairs={{0,504},{1,505},{2,506},{3,507},{4,508},{5,509},{6,510},{7,511},{8... | collective-permute-start | bytes 82952 | tf_op jit(solution)/shard_map/ppermute | solution.py:30

commit v7 on v6

--- a/solution.py
+++ b/solution.py
@@ -211,52 +211,91 @@
         expand_others(flags_ref[0], fine_ref, coarse_ref, bias1_ref, bias2_ref, stacked, spread_from)
 
 
-def attend_fine(x_ref, bias, qkv_ref, proj_ref):
+def attend_fine(x_ref, m_ref, qkv_ref, proj_ref, with_bias):
     normed = normalise(get(x_ref, 72, 432, 1, 192))
     q = dot(normed, qkv_ref[:, 0:192]).astype(bf16).astype(f32)
     k = dot(normed, qkv_ref[:, 192:384]).astype(bf16)
     v = dot(normed, qkv_ref[:, 384:576]).astype(bf16)
-    left, right = [], []
-    for window, start, stop in ((0, 72, 144), (1, 0, 144), (2, 0, 72)):
-        at = window * CELLS
-        q_rows = q[at + start : at + stop]
-        k_rows, v_rows = k[at : at + CELLS], v[at : at + CELLS]
-        left.append(attend_group(q_rows[:, :128], k_rows[:, :128], v_rows[:, :128], bias(0, 4, start, stop), 4))
-        right.append(attend_group(q_rows[:, 128:], k_rows[:, 128:], v_rows[:, 128:], bias(4, 6, start, stop), 2))
-    left = jnp.concatenate(left, axis=0).astype(bf16)
-    right = jnp.concatenate(right, axis=0).astype(bf16)
-    product = dot(left, proj_ref[0:128, :]) + dot(right, proj_ref[128:192, :])
+
+    def attend(bias_ref):
+        to = 0
+        for window, start, stop in ((0, 72, 144), (1, 0, 144), (2, 0, 72)):
+            at, rows = window * CELLS, stop - start
+            q_rows = q[at + start : at + stop]
+            k_rows, v_rows = k[at : at + CELLS], v[at : at + CELLS]
+            for t, lanes, heads in ((0, slice(0, 128), slice(0, 4)), (1, slice(128, 192), slice(4, 6))):
+                mixed = attend_group(
+                    q_rows[:, lanes], k_rows[:, lanes], v_rows[:, lanes], bias_ref[heads, start:stop, :],
+                    heads.stop - heads.start,
+                )
+                m_ref[t, to : to + rows, 0 : mixed.shape[-1]] = mixed
+            to += rows
+
+    with_bias(attend)
+    product = dot(m_ref[0].astype(bf16), proj_ref[0:128, :]) + dot(m_ref[1, :, 0:64].astype(bf16), proj_ref[128:192, :])
     return (get(x_ref, 144, 288, 1, 192) + product).astype(bf16)
 
 
 def early_or_late(flags_ref, early_ref, late_ref):
-    return lambda head, last, start, stop: jnp.where(
-        flags_ref[1] > 0, early_ref[head:last, start:stop, :], late_ref[head:last, start:stop, :]
-    )
+    def with_bias(attend):
+        @pl.when(flags_ref[1] > 0)
+        def _():
+            attend(early_ref)
+
+        @pl.when(flags_ref[1] == 0)
+        def _():
+            attend(late_ref)
+
+    return with_bias
+
+
+def merge_tokens(parts, merge_ref):
+    mean = sum(jnp.sum(part, axis=-1, keepdims=True) for part in parts) * (1.0 / 768)
+    parts = [part - mean for part in parts]
+    variance = sum(jnp.sum(part * part, axis=-1, keepdims=True) for part in parts) * (1.0 / 768)
+    scale = lax.rsqrt(variance + EPSILON)
+    merged = sum(
+        dot((part * scale).astype(bf16), merge_ref[i * 192 : (i + 1) * 192, :]) for i, part in enumerate(parts)
+    )
+    return merged.astype(bf16)
 
 
 def first_rows_kernel(
-    flags_ref, left_ref, own_ref, fine_ref, early0_ref, qkv_ref, proj_ref,
-    out_ref, send_ref, late0_ref, x_ref, a_ref, stacked, spread_from,
+    flags_ref, left_ref, own_ref, fine_ref, early0_ref, qkv_ref, proj_ref, up_hbm, down_hbm, merge_hbm,
+    out_ref, send_ref, up_ref, down_ref, merge_ref,
+    late0_ref, x_ref, a_ref, m_ref, e_ref, stacked, spread_from, sems,
 ):
-    @pl.when(flags_ref[1] == 0)
-    def _():
-        expand_first(fine_ref, late0_ref, stacked, spread_from)
-
+    moves = [(up_hbm, up_ref), (down_hbm, down_ref), (merge_hbm, merge_ref)]
+    copies = [pltpu.make_async_copy(source, to, sems.at[i]) for i, (source, to) in enumerate(moves)]
+    for copy in copies:
+        copy.start()
     for z in range(WZ):
         for a in range(WLAT):
             put(x_ref, z * WLAT + a, 24, LINES, left_ref[z, 3 + a].astype(f32))
             put(x_ref, 288 + z * WLAT + a, 24, LINES, own_ref[z, 3 + a].astype(f32))
-    attended = attend_fine(x_ref, early_or_late(flags_ref, early0_ref, late0_ref), qkv_ref, proj_ref)
+
+    @pl.when(flags_ref[1] == 0)
+    def _():
+        expand_first(fine_ref, late0_ref, stacked, spread_from)
+
+    attended = attend_fine(x_ref, m_ref, qkv_ref, proj_ref, early_or_late(flags_ref, early0_ref, late0_ref))
     out_ref[...] = attended
     put(a_ref, 0, 288, 1, attended.astype(f32))
-    lines = [a_ref[t, pl.ds(z * WLAT + a, 24, stride=LINES), :] for t in range(2) for z in range(WZ) for a in range(3)]
-    send_ref[...] = pack_lines(lines[:6], [line[:, :64] for line in lines[6:]]).astype(bf16)
+    for copy in copies:
+        copy.wait()
+    edge = [get(a_ref, z * WLAT + a, 24, LINES, 192) for a in range(3) for z in range(WZ)]
+    put(e_ref, 0, 144, 1, fine_feed_forward(jnp.concatenate(edge, axis=0), up_ref, down_ref))
+    parts = [get(e_ref, 48 + pa * 48 + pb, 24, 2, 192) for pa in range(2) for pb in range(2)]
+    merged = merge_tokens(parts, merge_ref).astype(f32)
+    row = get(e_ref, 0, 48, 1, 192)
+    pieces = [row[:, :128], jnp.concatenate([row[:24, 128:], row[24:, 128:]], axis=-1)]
+    pieces += [merged[:, t * 128 : (t + 1) * 128] for t in range(3)]
+    send_ref[...] = jnp.concatenate(pieces, axis=0).astype(bf16)
 
 
 def second_rows_kernel(
     flags_ref, left_ref, own_ref, corner_ref, below_ref, first_ref, early1_ref, late1_ref, qkv_ref, proj_ref, up_ref,
-    down_ref, out_ref, x_ref, a_ref, w_ref,
+    down_ref, merge_ref, out_ref, last_ref, x_ref, a_ref, w_ref, m_ref,
 ):
     below, corner = below_ref[...].astype(f32), corner_ref[...].astype(f32)
     for z in range(WZ):
@@ -269,8 +308,8 @@
                 put(x_ref, 72 + at, 18, LINES, unpack_line(corner, z * 3 + a - 3, 18))
                 put(x_ref, 288 + at, 18, LINES, unpack_line(below, z * 3 + a - 3, 18))
     put(a_ref, 0, 288, 1, first_ref[...].astype(f32))
-    bias = early_or_late(flags_ref, early1_ref, late1_ref)
-    put(a_ref, 288, 288, 1, attend_fine(x_ref, bias, qkv_ref, proj_ref).astype(f32))
+    attended = attend_fine(x_ref, m_ref, qkv_ref, proj_ref, early_or_late(flags_ref, early1_ref, late1_ref))
+    put(a_ref, 288, 288, 1, attended.astype(f32))
     for t in range(2):
         for rho in range(3, 12):
             for z in range(WZ):
@@ -278,46 +317,45 @@
                 to = ((rho - 3) * WZ + z) * 24
                 w_ref[t, to : to + 24, :] = a_ref[t, pl.ds(at, 24, stride=LINES), :]
     for i in range(3):
-        x = get(w_ref, i * 144, 144, 1, 192)
-        out_ref[i * 144 : (i + 1) * 144, :] = fine_feed_forward(x, up_ref, down_ref).astype(bf16)
+        put(w_ref, i * 144, 144, 1, fine_feed_forward(get(w_ref, i * 144, 144, 1, 192), up_ref, down_ref))
+    parts = [
+        jnp.concatenate([get(w_ref, (2 * i + pa) * 48 + pb, 24, 2, 192) for i in range(4)], axis=0)
+        for pa in range(2)
+        for pb in range(2)
+    ]
+    out_ref[...] = merge_tokens(parts, merge_ref)
+    last_ref[...] = get(w_ref, 384, 48, 1, 192).astype(bf16)
 
 
 def coarse_kernel(
-    flags_ref, y_ref, got_ref, fine_up_ref, fine_down_ref, merge_ref, early2_ref, late2_ref, qkv_ref, proj_ref, up_ref, down_ref,
-    keep_ref, lower_ref, corner_ref, left_ref, w_ref, p_ref, o_ref,
+    flags_ref, rows_ref, last_ref, got_ref, merge_ref, early2_ref, late2_ref, qkv_ref, proj_ref, up_ref, down_ref,
+    keep_ref, lower_ref, corner_ref, left_ref, r_ref, o_ref, m_ref,
 ):
     got = got_ref[...].astype(f32)
-    got = jnp.concatenate([unpack_line(got, z * 3 + a, 24) for a in range(3) for z in range(WZ)], axis=0)
-    put(w_ref, 0, 432, 1, y_ref[...].astype(f32))
-    put(w_ref, 432, 144, 1, fine_feed_forward(got, fine_up_ref, fine_down_ref))
-    parts = []
-    for pa in range(2):
-        for pb in range(2):
-            for t in range(2):
-                for z in range(WZ):
-                    for i in range(WLAT):
-                        at = ((2 * i + pa) * WZ + z) * 24 + pb
-                        line = w_ref[t, pl.ds(at, WLON, stride=2), :]
-                        p_ref[t, pl.ds(len(parts) * CELLS + z * WLAT + i, WLON, stride=LINES), :] = line
-            parts.append(get(p_ref, len(parts) * CELLS, CELLS, 1, 192))
-    mean = sum(jnp.sum(part, axis=-1, keepdims=True) for part in parts) * (1.0 / 768)
-    parts = [part - mean for part in parts]
-    variance = sum(jnp.sum(part * part, axis=-1, keepdims=True) for part in parts) * (1.0 / 768)
-    scale = lax.rsqrt(variance + EPSILON)
-    merged = sum(
-        dot((part * scale).astype(bf16), merge_ref[i * 192 : (i + 1) * 192, :]) for i, part in enumerate(parts)
-    )
-    merged = merged.astype(bf16).astype(f32)
+    put(r_ref, 0, 48, 1, last_ref[...].astype(f32))
+    second = jnp.concatenate([got[48:72, :64], got[48:72, 64:]], axis=0)
+    put(r_ref, 48, 48, 1, jnp.concatenate([got[:48], second], axis=-1))
+    parts = [get(r_ref, pa * 48 + pb, 24, 2, 192) for pa in range(2) for pb in range(2)]
+    fifth = merge_tokens(parts, merge_ref).astype(f32)
+    sixth = jnp.concatenate([got[72 + t * 24 : 96 + t * 24] for t in range(3)], axis=-1)
+    rows = jnp.concatenate([rows_ref[...].astype(f32), fifth, sixth], axis=0)
+    for i in range(WLAT):
+        for z in range(WZ):
+            at = (i * WZ + z) * WLON
+            put(o_ref, z * WLAT + i, WLON, LINES, rows[at : at + WLON])
+    merged = get(o_ref, 0, CELLS, 1, 384)
     normed = normalise(merged)
     qkv = dot(normed, qkv_ref[...]).astype(bf16)
-    product = merged
-    bias = early_or_late(flags_ref, early2_ref, late2_ref)
-    for g in range(3):
-        q = qkv[:, g * 128 : (g + 1) * 128].astype(f32)
-        k = qkv[:, 384 + g * 128 : 384 + (g + 1) * 128]
-        v = qkv[:, 768 + g * 128 : 768 + (g + 1) * 128]
-        mixed = attend_group(q, k, v, bias(g * 4, (g + 1) * 4, 0, CELLS), 4)
-        product = product + dot(mixed.astype(bf16), proj_ref[g * 128 : (g + 1) * 128, :])
+
+    def attend(bias_ref):
+        for g in range(3):
+            q = qkv[:, g * 128 : (g + 1) * 128].astype(f32)
+            k = qkv[:, 384 + g * 128 : 384 + (g + 1) * 128]
+            v = qkv[:, 768 + g * 128 : 768 + (g + 1) * 128]
+            m_ref[:, g * 128 : (g + 1) * 128] = attend_group(q, k, v, bias_ref[g * 4 : (g + 1) * 4], 4).astype(bf16)
+
+    early_or_late(flags_ref, early2_ref, late2_ref)(attend)
+    product = merged + dot(m_ref[...], proj_ref[...])
     attended = product.astype(bf16).astype(f32)
     put(o_ref, 0, CELLS, 1, feed_forward(attended, up_ref, down_ref))
     for i in range(3):
@@ -360,7 +398,8 @@
 ):
     lat, lats = lax.axis_index("lat"), lax.axis_size("lat")
     lon, lons = lax.axis_index("lon"), lax.axis_size("lon")
-    flags = jnp.stack([lat == lats - 1, (lat < lats // 2) & (lon < lons // 2)]).astype(jnp.int32)
+    early = (lat < lats // 4) | ((lat < lats // 2) & (lon < lons // 2))
+    flags = jnp.stack([lat == lats - 1, early]).astype(jnp.int32)
     fine_tables = fine_bias.transpose(0, 2, 3, 1, 4)
     coarse_tables = coarse_bias.transpose(0, 2, 3, 1, 4)
     fine_down = fine_down.T
@@ -383,23 +422,34 @@
     )(flags, *(pltpu.with_memory_space_constraint(source, pltpu.HBM) for source in sources))
     corner = from_behind(corner, 1, -1)
     below = from_behind(below, 0, -1)
-    first, edge = call(
+    weights = [fine_up, fine_down, merge_weight]
+    first, edge, fine_up, fine_down, merge_weight = pl.pallas_call(
         first_rows_kernel,
-        [((288, 192), bf16), ((216, 128), bf16)],
-        [((6, CELLS, CELLS), f32), tiles_of(576, 192), tiles_of(288, 192)] + expansion,
-        [flags, left, own, fine_tables, bias0, fine_qkv, fine_proj],
-        1_000_000_000,
-        smem=1,
+        out_shape=[jax.ShapeDtypeStruct((288, 192), bf16), jax.ShapeDtypeStruct((144, 128), bf16)]
+        + [jax.ShapeDtypeStruct(weight.shape, weight.dtype) for weight in weights],
+        in_specs=[smem] + [vmem] * 6 + [hbm] * 3,
+        out_specs=[vmem] * 5,
+        scratch_shapes=[
+            pltpu.VMEM(shape, dtype)
+            for shape, dtype in [((6, CELLS, CELLS), f32), tiles_of(576, 192), tiles_of(288, 192), tiles_of(288, 192)]
+            + [tiles_of(144, 192)]
+            + expansion
+        ]
+        + [pltpu.SemaphoreType.DMA((3,))],
+        compiler_params=pltpu.CompilerParams(vmem_limit_bytes=VMEM_LIMIT),
+    )(
+        *[flags, left, own, fine_tables, bias0, fine_qkv, fine_proj],
+        *(pltpu.with_memory_space_constraint(weight, pltpu.HBM) for weight in weights),
     )
     got = from_behind(edge, 0, -1)
     late1, late2 = call(
         other_bias_kernel, biases, expansion, [flags, fine_tables, coarse_tables, first], 2_000_000_000, smem=1
     )
-    (finished,) = call(
+    rows, row = call(
         second_rows_kernel,
-        [((432, 192), bf16)],
-        [tiles_of(576, 192), tiles_of(576, 192), tiles_of(432, 192)],
-        [flags, left, own, corner, below, first, bias1, late1, fine_qkv, fine_proj, fine_up, fine_down],
+        [((96, 384), bf16), ((48, 192), bf16)],
+        [tiles_of(576, 192), tiles_of(576, 192), tiles_of(432, 192), tiles_of(288, 192)],
+        [flags, left, own, corner, below, first, bias1, late1, fine_qkv, fine_proj, fine_up, fine_down, merge_weight],
         3_000_000_000,
         smem=1,
     )
@@ -407,9 +457,8 @@
     keep, lower, far_corner, upper_left = call(
         coarse_kernel,
         [quarter] * 4,
-        [tiles_of(576, 192), tiles_of(576, 192), tiles_of(CELLS, 384)],
-        [flags, finished, got, fine_up, fine_down, merge_weight, bias2, late2]
-        + [coarse_qkv, coarse_proj, coarse_up, coarse_down],
+        [tiles_of(96, 192), tiles_of(CELLS, 384), ((CELLS, 384), bf16)],
+        [flags, rows, row, got, merge_weight, bias2, late2, coarse_qkv, coarse_proj, coarse_up, coarse_down],
         4_000_000_000,
         smem=1,
     )

time: 63.6 us -> 64.8 us (1.019)
  the two profiles are of different devices: /device:TPU:511 before, /device:TPU:16 now
where the time goes in v7:
time: 64.8 us; the launch traced here: 64.5 us
  starting transfers between devices  38.7 us (60%)
  Pallas kernels  16.9 us (26%)
  waiting for transfers between devices  7.75 us (12%)
  other arithmetic  0.88 us (1%)
    ppermute x7, starting transfers between devices, from_behind(): return lax.ppermute(shard, ('lon', 'lat'), pairs)  38.7 us
    pallas_call x3, Pallas kernels, call(): pl.pallas_call(kernel, out_shape=[jax.ShapeDtypeStruct(shape, dtype) for...  8.11 us
    ppermute x7, waiting for transfers between devices, from_behind(): return lax.ppermute(shard, ('lon', 'lat'), pairs)  7.75 us
    pallas_call x1, Pallas kernels, body(): pl.pallas_call(prepare_kernel, out_shape=[jax.ShapeDtypeStruct((162, 128)...  5.21 us
    pallas_call x1, Pallas kernels, body(): pl.pallas_call(first_rows_kernel, out_shape=[jax.ShapeDtypeStruct((288, 1...  3.56 us
  transfers between devices with their start and end apart: 7, of which 2 were waited for; matrix products, arithmetic and copies ran while one was open for 0% of the time, Pallas kernels for 20%

profile of v7, /device:TPU:16, one launch (start us, length us, event | category | flops | bytes accessed | tf_op | source)
XLA Modules:
  0.0 64.5 jit_solution(5823670161492973588)
XLA Ops:
  0.0 1.9 %collective-permute-start = (bf16[2,12,24,192]{3,2,1,0:T(8,128)(2,1)}, bf16[2,12,24,192]{3,2,1,0:T(8,128)(2,1)S(1)}, u32[]{:S(2)}, u32[]{:S(2)}) collective-permute-start(bf16[2,12,24,192]{3,2,1,0:T(8,128)(2,1)} %fields_hbm.1), channel_id=1, source_target_pairs={{0,8},{1,9},{2,10},{3,11},{4,12},{5,13},{6,14},{7,15},{8,16},{9,17... | collective-permute-start | bytes 663560 | tf_op jit(solution)/shard_map/ppermute | solution.py:30
  1.9 0.1 add_convert_fusion.flags_ref
  2.0 5.2 %shard_map.118 = (bf16[162,128]{1,0:T(8,128)(2,1)S(1)}, bf16[162,128]{1,0:T(8,128)(2,1)S(1)}, bf16[2,12,24,192]{3,2,1,0:T(8,128)(2,1)S(1)}, f32[2,6,23,1,144]{4,...) custom-call(s32[2]{0:T(128)S(1)} %add_convert_fusion.flags_ref, ...), custom_call_target="tpu_custom_call" | custom-call | tf_op jit(solution)/shard_map/pallas_call | solution.py:411
  7.2 3.5 %collective-permute-start.1 = (bf16[162,128]{1,0:T(8,128)(2,1)S(1)}, bf16[162,128]{1,0:T(8,128)(2,1)S(1)}, u32[]{:S(2)}, u32[]{:S(2)}) collective-permute-start(bf16[162,128]{1,0:T(8,128)(2,1)S(1)} %get-tuple-element.29), channel_id=1, source_target_pairs={{0,15},{1,8},{2,9},{3,10},{4,11},{5,12},{6,13},{7,14},{8,23},{9,16... | collective-permute-start | bytes 124424 | tf_op jit(solution)/shard_map/ppermute | solution.py:30
  10.8 2.4 %collective-permute-start.2 = (bf16[162,128]{1,0:T(8,128)(2,1)S(1)}, bf16[162,128]{1,0:T(8,128)(2,1)S(1)}, u32[]{:S(2)}, u32[]{:S(2)}) collective-permute-start(bf16[162,128]{1,0:T(8,128)(2,1)S(1)} %get-tuple-element.30), channel_id=1, source_target_pairs={{0,7},{1,0},{2,1},{3,2},{4,3},{5,4},{6,5},{7,6},{8,15},{9,8},{10,9... | collective-permute-start | bytes 124424 | tf_op jit(solution)/shard_map/ppermute | solution.py:30
  13.2 6.2 %collective-permute-done.left_ref = bf16[2,12,24,192]{3,2,1,0:T(8,128)(2,1)S(1)} collective-permute-done((bf16[2,12,24,192]{3,2,1,0:T(8,128)(2,1)}, bf16[2,12,24,192]{3,2,1,0:T(8,128)(2,1)S(1)}, u32[]{:S(2)}, u32[]{:S(2)}) %collective-permute-start) | collective-permute-done | bytes 221216 | tf_op jit(solution)/shard_map/ppermute | solution.py:30
  19.4 3.6 %shard_map.119 = (bf16[288,192]{1,0:T(8,128)(2,1)S(1)}, bf16[144,128]{1,0:T(8,128)(2,1)S(1)}, bf16[192,768]{1,0:T(8,128)(2,1)S(1)}, bf16[192,768]{1,0:T(8,128)(2,1)S(1)}, bf16[768,384]{1,0:T(8,128)(2,1)S(1)}) custom-call(s32[2]{0:T(128)S(1)} %add_convert_fusion.flags_ref, bf16[2,12,24,192]{3,2,1,0:T(8,128)(2,1)S(1)} %collective-permute-done.left_ref, ...), custom_call_target="tpu_custom_call" | custom-call | tf_op jit(solution)/shard_map/pallas_call | solution.py:426
  23.0 8.6 %collective-permute-start.3 = (bf16[144,128]{1,0:T(8,128)(2,1)S(1)}, bf16[144,128]{1,0:T(8,128)(2,1)S(1)}, u32[]{:S(2)}, u32[]{:S(2)}) collective-permute-start(bf16[144,128]{1,0:T(8,128)(2,1)S(1)} %get-tuple-element.44), channel_id=1, source_target_pairs={{0,7},{1,0},{2,1},{3,2},{4,3},{5,4},{6,5},{7,6},{8,15},{9,8},{10,9... | collective-permute-start | bytes 110600 | tf_op jit(solution)/shard_map/ppermute | solution.py:30
  31.5 0.6 shard_map.120
  32.1 0.0 collective-permute-done.1.corner_ref
  32.1 0.0 collective-permute-done.2.below_ref
  32.1 0.0 copy-start
  32.1 0.0 copy-start.1
  32.1 0.0 copy-start.2
  32.2 0.0 copy-start.3
  32.2 3.9 %shard_map.121 = (bf16[96,384]{1,0:T(8,128)(2,1)S(1)}, bf16[48,192]{1,0:T(8,128)(2,1)S(1)}) custom-call(s32[2]{0:T(128)S(1)} %add_convert_fusion.flags_ref, bf16[2,12,24,192]{3,2,1,0:T(8,128)(2,1)S(1)} %collective-permute-done.left_ref, bf16[2,12,24,192]{3,2,1,0:T(8,128)(2,1)S(1)} %get-tuple-element.28.own_ref, ...), custom_call_target="tpu_custom_call" | custom-call | flops 3000000000 | bytes 3105800 | tf_op jit(solution)/shard_map/pallas_call | solution.py:370
  36.1 0.0 collective-permute-done.3.got_ref
  36.1 0.0 copy-done
  36.1 0.0 copy-done.1
  36.1 0.0 copy-done.2
  36.1 0.0 copy-done.3
  36.1 3.7 %shard_map.122 = (bf16[3,6,2,384]{3,2,1,0:T(2,128)(2,1)S(1)}, bf16[3,6,2,384]{3,2,1,0:T(2,128)(2,1)S(1)}, bf16[3,6,2,384]{3,2,1,0:T(2,128)(2,1)S(1)}, bf16[3,6,2,384]{3,2,1,0:T(2,128)(2,1)S(1)}) custom-call(s32[2]{0:T(128)S(1)} %add_convert_fusion.flags_ref, bf16[96,384]{1,0:T(8,128)(2,1)S(1)} %get-tuple-element.42.rows_ref, ...), custom_call_target="tpu_custom_call" | custom-call | flops 4000000000 | bytes 6248456 | tf_op jit(solution)/shard_map/pallas_call | solution.py:370
  39.8 7.1 %collective-permute-start.4 = (bf16[3,6,2,384]{3,2,1,0:T(2,128)(2,1)S(1)}, bf16[3,6,2,384]{3,2,1,0:T(2,128)(2,1)S(1)}, u32[]{:S(2)}, u32[]{:S(2)}) collective-permute-start(bf16[3,6,2,384]{3,2,1,0:T(2,128)(2,1)S(1)} %get-tuple-element.47), channel_id=1, source_target_pairs={{0,1},{1,2},{2,3},{3,4},{4,5},{5,6},{6,7},{7,0},{8,9},{9,10},{10,1... | collective-permute-start | bytes 82952 | tf_op jit(solution)/shard_map/ppermute | solution.py:30
  46.9 9.2 %collective-permute-start.5 = (bf16[3,6,2,384]{3,2,1,0:T(2,128)(2,1)S(1)}, bf16[3,6,2,384]{3,2,1,0:T(2,128)(2,1)S(1)}, u32[]{:S(2)}, u32[]{:S(2)}) collective-permute-start(bf16[3,6,2,384]{3,2,1,0:T(2,128)(2,1)S(1)} %get-tuple-element.48), channel_id=1, source_target_pairs={{0,505},{1,506},{2,507},{3,508},{4,509},{5,510},{6,511},{7,504},{8... | collective-permute-start | bytes 82952 | tf_op jit(solution)/shard_map/ppermute | solution.py:30
  56.1 6.0 %collective-permute-start.6 = (bf16[3,6,2,384]{3,2,1,0:T(2,128)(2,1)S(1)}, bf16[3,6,2,384]{3,2,1,0:T(2,128)(2,1)S(1)}, u32[]{:S(2)}, u32[]{:S(2)}) collective-permute-start(bf16[3,6,2,384]{3,2,1,0:T(2,128)(2,1)S(1)} %get-tuple-element.50), channel_id=1, source_target_pairs={{0,504},{1,505},{2,506},{3,507},{4,508},{5,509},{6,510},{7,511},{8... | collective-permute-start | bytes 82952 | tf_op jit(solution)/shard_map/ppermute | solution.py:30
  62.1 0.0 collective-permute-done.4
  62.1 0.0 collective-permute-done.5
  62.2 1.5 %collective-permute-done.6 = bf16[3,6,2,384]{3,2,1,0:T(2,128)(2,1)S(1)} collective-permute-done((bf16[3,6,2,384]{3,2,1,0:T(2,128)(2,1)S(1)}, bf16[3,6,2,384]{3,2,1,0:T(2,128)(2,1)S(1)}, u32[]{:S(2)}, u32[]{:S(2)}) %collective-permute-start.6) | collective-permute-done | bytes 27680 | tf_op jit(solution)/shard_map/ppermute | solution.py:30
  63.7 0.8 %maximum_bitcast_fusion = bf16[2,6,12,384]{3,0,2,1:T(2,128)(2,1)} fusion(bf16[3,6,2,384]{3,2,1,0:T(2,128)(2,1)S(1)} %collective-permute-done.6, bf16[3,6,2,384]{3,2,1,0:T(2,128)(2,1)S(1)} %get-tuple-element.49, bf16[3,6,2,384]{3,2,1,0:T(2,128)(2,1)S(1)} %collective-permute-done.5, bf16[3,6,2,384]{3,2,1,0:T(2,128)(2,1)S(1)} %collective-permute-done.4), kind=kLoop, calls=%fused_computation | loop fusion | flops 165888 | bytes 221184 | tf_op jit(solution)/shard_map/transpose | solution.py:469
Async XLA Ops:
  0.0 19.4 %collective-permute-start = (bf16[2,12,24,192]{3,2,1,0:T(8,128)(2,1)}, bf16[2,12,24,192]{3,2,1,0:T(8,128)(2,1)S(1)}, u32[]{:S(2)}, u32[]{:S(2)}) collective-permute-start(bf16[2,12,24,192]{3,2,1,0:T(8,128)(2,1)} %fields_hbm.1), channel_id=1, source_target_pairs={{0,8},{1,9},{2,10},{3,11},{4,12},{5,13},{6,14},{7,15},{8,16},{9,17... | collective-permute-start | bytes 663560 | tf_op jit(solution)/shard_map/ppermute | solution.py:30
  7.2 24.9 %collective-permute-start.1 = (bf16[162,128]{1,0:T(8,128)(2,1)S(1)}, bf16[162,128]{1,0:T(8,128)(2,1)S(1)}, u32[]{:S(2)}, u32[]{:S(2)}) collective-permute-start(bf16[162,128]{1,0:T(8,128)(2,1)S(1)} %get-tuple-element.29), channel_id=1, source_target_pairs={{0,15},{1,8},{2,9},{3,10},{4,11},{5,12},{6,13},{7,14},{8,23},{9,16... | collective-permute-start | bytes 124424 | tf_op jit(solution)/shard_map/ppermute | solution.py:30
  10.8 21.3 %collective-permute-start.2 = (bf16[162,128]{1,0:T(8,128)(2,1)S(1)}, bf16[162,128]{1,0:T(8,128)(2,1)S(1)}, u32[]{:S(2)}, u32[]{:S(2)}) collective-permute-start(bf16[162,128]{1,0:T(8,128)(2,1)S(1)} %get-tuple-element.30), channel_id=1, source_target_pairs={{0,7},{1,0},{2,1},{3,2},{4,3},{5,4},{6,5},{7,6},{8,15},{9,8},{10,9... | collective-permute-start | bytes 124424 | tf_op jit(solution)/shard_map/ppermute | solution.py:30
  23.0 13.1 %collective-permute-start.3 = (bf16[144,128]{1,0:T(8,128)(2,1)S(1)}, bf16[144,128]{1,0:T(8,128)(2,1)S(1)}, u32[]{:S(2)}, u32[]{:S(2)}) collective-permute-start(bf16[144,128]{1,0:T(8,128)(2,1)S(1)} %get-tuple-element.44), channel_id=1, source_target_pairs={{0,7},{1,0},{2,1},{3,2},{4,3},{5,4},{6,5},{7,6},{8,15},{9,8},{10,9... | collective-permute-start | bytes 110600 | tf_op jit(solution)/shard_map/ppermute | solution.py:30
  32.1 3.9 %copy-start = (bf16[384,1536]{1,0:T(8,128)(2,1)S(1)}, bf16[384,1536]{1,0:T(8,128)(2,1)}, u32[]{:S(2)}) copy-start(bf16[384,1536]{1,0:T(8,128)(2,1)} %up_ref.1) | copy-start | bytes 3538948
  32.1 3.9 %copy-start.1 = (bf16[1536,384]{1,0:T(8,128)(2,1)S(1)}, bf16[1536,384]{1,0:T(8,128)(2,1)}, u32[]{:S(2)}) copy-start(bf16[1536,384]{1,0:T(8,128)(2,1)} %down_ref.1) | copy-start | bytes 3538948
  32.1 3.9 %copy-start.2 = (bf16[384,1152]{1,0:T(8,128)(2,1)S(1)}, bf16[384,1152]{1,0:T(8,128)(2,1)}, u32[]{:S(2)}) copy-start(bf16[384,1152]{1,0:T(8,128)(2,1)} %qkv_ref.1) | copy-start | bytes 2654212
  32.2 3.9 %copy-start.3 = (bf16[384,384]{1,0:T(8,128)(2,1)S(1)}, bf16[384,384]{1,0:T(8,128)(2,1)}, u32[]{:S(2)}) copy-start(bf16[384,384]{1,0:T(8,128)(2,1)} %proj_ref.1) | copy-start | bytes 884740
  39.8 22.3 %collective-permute-start.4 = (bf16[3,6,2,384]{3,2,1,0:T(2,128)(2,1)S(1)}, bf16[3,6,2,384]{3,2,1,0:T(2,128)(2,1)S(1)}, u32[]{:S(2)}, u32[]{:S(2)}) collective-permute-start(bf16[3,6,2,384]{3,2,1,0:T(2,128)(2,1)S(1)} %get-tuple-element.47), channel_id=1, source_target_pairs={{0,1},{1,2},{2,3},{3,4},{4,5},{5,6},{6,7},{7,0},{8,9},{9,10},{10,1... | collective-permute-start | bytes 82952 | tf_op jit(solution)/shard_map/ppermute | solution.py:30
  46.9 15.2 %collective-permute-start.5 = (bf16[3,6,2,384]{3,2,1,0:T(2,128)(2,1)S(1)}, bf16[3,6,2,384]{3,2,1,0:T(2,128)(2,1)S(1)}, u32[]{:S(2)}, u32[]{:S(2)}) collective-permute-start(bf16[3,6,2,384]{3,2,1,0:T(2,128)(2,1)S(1)} %get-tuple-element.48), channel_id=1, source_target_pairs={{0,505},{1,506},{2,507},{3,508},{4,509},{5,510},{6,511},{7,504},{8... | collective-permute-start | bytes 82952 | tf_op jit(solution)/shard_map/ppermute | solution.py:30
  56.1 7.6 %collective-permute-start.6 = (bf16[3,6,2,384]{3,2,1,0:T(2,128)(2,1)S(1)}, bf16[3,6,2,384]{3,2,1,0:T(2,128)(2,1)S(1)}, u32[]{:S(2)}, u32[]{:S(2)}) collective-permute-start(bf16[3,6,2,384]{3,2,1,0:T(2,128)(2,1)S(1)} %get-tuple-element.50), channel_id=1, source_target_pairs={{0,504},{1,505},{2,506},{3,507},{4,508},{5,509},{6,510},{7,511},{8... | collective-permute-start | bytes 82952 | tf_op jit(solution)/shard_map/ppermute | solution.py:30

commit v8 on v6

--- a/solution.py
+++ b/solution.py
@@ -58,12 +58,9 @@
     return (x + dot_nt(hidden, down_ref[...])).astype(bf16).astype(f32)
 
 
-def three_parts(x):
+def two_parts(x):
     high = x.astype(bf16)
-    rest = x - high.astype(f32)
-    middle = rest.astype(bf16)
-    low = (rest - middle.astype(f32)).astype(bf16)
-    return high, middle, low
+    return high, (x - high.astype(f32)).astype(bf16)
 
 
 def iota(shape, axis):
@@ -81,14 +78,14 @@
     lane = iota((LINES * 32, 384), 1)
     spread = (lane == (SPAN - 1 - row % 32) * LINES + row // 32) & (row % 32 < SPAN)
     spread = spread.astype(f32).astype(bf16)
-    row, lane = iota((6 * 16, 384), 0) % 16, iota((6 * 16, 384), 1) % LINES
+    row, lane = iota((6 * LINES, 384), 0) % LINES, iota((6 * LINES, 384), 1) % LINES
     levels_differ = row // WLAT != lane // WLAT
     rows_differ = (row % WLAT >= WLAT // 2) != (lane % WLAT >= WLAT // 2)
     slot = iota((16, 128), 1) // 32
     for (table_of, last), out_of in zip(tables, outs, strict=True):
         for head in range(6):
             stacked[head * 32 : head * 32 + SPAN, :] = table_of(head)
-        picked = sum(dot_nt(pick, part) for part in three_parts(stacked[...]))
+        picked = sum(dot_nt(pick, part) for part in two_parts(stacked[...]))
         picked = [picked[:, :128], jnp.concatenate([picked[:, 128:], jnp.zeros((LINES * 16, 64), f32)], axis=-1)]
         rolled = [[half] + [pltpu.roll(half, 32 * r, 1) for r in range(1, 4)] for half in picked]
         for head in range(6):
@@ -98,15 +95,15 @@
                     key = group * 4 + at
                     piece = rolled[head // 4][(at - head) % 4][key * 16 : (key + 1) * 16]
                     block = piece if block is None else jnp.where(slot == at, piece, block)
-                spread_from[head * 16 : (head + 1) * 16, group * 128 : (group + 1) * 128] = block
-        flat = sum(dot(part, spread) for part in three_parts(spread_from[...]))
+                spread_from[head * LINES : (head + 1) * LINES, group * 128 : (group + 1) * 128] = block[:LINES]
+        flat = sum(dot(part, spread) for part in two_parts(spread_from[...]))
         apart = levels_differ if last is None else levels_differ | (rows_differ & (last > 0))
         flat = jnp.where(apart, MASKED, flat)
         for o in range(WLON):
             start = (WLON - 1 - o) * LINES
             piece = flat[:, start : start + CELLS]
             for head in range(6):
-                out_of(head, o * LINES, piece[head * 16 : head * 16 + LINES])
+                out_of(head, o * LINES, piece[head * LINES : (head + 1) * LINES])
 
 
 def writer(out_ref, base):
@@ -205,13 +202,20 @@
         expand_others(flags_ref[0], fine_ref, coarse_ref, bias1_ref, bias2_ref, stacked, spread_from)
 
 
-def other_bias_kernel(flags_ref, fine_ref, coarse_ref, after_ref, bias1_ref, bias2_ref, stacked, spread_from):
+def other_bias_kernel(
+    flags_ref, fine_ref, coarse_ref, early1_ref, early2_ref, after_ref, bias1_ref, bias2_ref, stacked, spread_from
+):
+    @pl.when(flags_ref[1] > 0)
+    def _():
+        bias1_ref[...] = early1_ref[...]
+        bias2_ref[...] = early2_ref[...]
+
     @pl.when(flags_ref[1] == 0)
     def _():
         expand_others(flags_ref[0], fine_ref, coarse_ref, bias1_ref, bias2_ref, stacked, spread_from)
 
 
-def attend_fine(x_ref, bias, qkv_ref, proj_ref):
+def attend_fine(x_ref, bias_ref, qkv_ref, proj_ref):
     normed = normalise(get(x_ref, 72, 432, 1, 192))
     q = dot(normed, qkv_ref[:, 0:192]).astype(bf16).astype(f32)
     k = dot(normed, qkv_ref[:, 192:384]).astype(bf16)
@@ -221,33 +225,32 @@
         at = window * CELLS
         q_rows = q[at + start : at + stop]
         k_rows, v_rows = k[at : at + CELLS], v[at : at + CELLS]
-        left.append(attend_group(q_rows[:, :128], k_rows[:, :128], v_rows[:, :128], bias(0, 4, start, stop), 4))
-        right.append(attend_group(q_rows[:, 128:], k_rows[:, 128:], v_rows[:, 128:], bias(4, 6, start, stop), 2))
+        bias = bias_ref[:, start:stop, :]
+        left.append(attend_group(q_rows[:, :128], k_rows[:, :128], v_rows[:, :128], bias[:4], 4))
+        right.append(attend_group(q_rows[:, 128:], k_rows[:, 128:], v_rows[:, 128:], bias[4:], 2))
     left = jnp.concatenate(left, axis=0).astype(bf16)
     right = jnp.concatenate(right, axis=0).astype(bf16)
     product = dot(left, proj_ref[0:128, :]) + dot(right, proj_ref[128:192, :])
     return (get(x_ref, 144, 288, 1, 192) + product).astype(bf16)
 
 
-def early_or_late(flags_ref, early_ref, late_ref):
-    return lambda head, last, start, stop: jnp.where(
-        flags_ref[1] > 0, early_ref[head:last, start:stop, :], late_ref[head:last, start:stop, :]
-    )
-
-
 def first_rows_kernel(
     flags_ref, left_ref, own_ref, fine_ref, early0_ref, qkv_ref, proj_ref,
-    out_ref, send_ref, late0_ref, x_ref, a_ref, stacked, spread_from,
+    out_ref, send_ref, bias0_ref, x_ref, a_ref, stacked, spread_from,
 ):
     @pl.when(flags_ref[1] == 0)
     def _():
-        expand_first(fine_ref, late0_ref, stacked, spread_from)
+        expand_first(fine_ref, bias0_ref, stacked, spread_from)
+
+    @pl.when(flags_ref[1] > 0)
+    def _():
+        bias0_ref[...] = early0_ref[...]
 
     for z in range(WZ):
         for a in range(WLAT):
             put(x_ref, z * WLAT + a, 24, LINES, left_ref[z, 3 + a].astype(f32))
             put(x_ref, 288 + z * WLAT + a, 24, LINES, own_ref[z, 3 + a].astype(f32))
-    attended = attend_fine(x_ref, early_or_late(flags_ref, early0_ref, late0_ref), qkv_ref, proj_ref)
+    attended = attend_fine(x_ref, bias0_ref, qkv_ref, proj_ref)
     out_ref[...] = attended
     put(a_ref, 0, 288, 1, attended.astype(f32))
     lines = [a_ref[t, pl.ds(z * WLAT + a, 24, stride=LINES), :] for t in range(2) for z in range(WZ) for a in range(3)]
@@ -255,8 +258,8 @@
 
 
 def second_rows_kernel(
-    flags_ref, left_ref, own_ref, corner_ref, below_ref, first_ref, early1_ref, late1_ref, qkv_ref, proj_ref, up_ref,
-    down_ref, out_ref, x_ref, a_ref, w_ref,
+    left_ref, own_ref, corner_ref, below_ref, first_ref, bias1_ref, qkv_ref, proj_ref, up_ref, down_ref,
+    out_ref, x_ref, a_ref, w_ref,
 ):
     below, corner = below_ref[...].astype(f32), corner_ref[...].astype(f32)
     for z in range(WZ):
@@ -269,8 +272,7 @@
                 put(x_ref, 72 + at, 18, LINES, unpack_line(corner, z * 3 + a - 3, 18))
                 put(x_ref, 288 + at, 18, LINES, unpack_line(below, z * 3 + a - 3, 18))
     put(a_ref, 0, 288, 1, first_ref[...].astype(f32))
-    bias = early_or_late(flags_ref, early1_ref, late1_ref)
-    put(a_ref, 288, 288, 1, attend_fine(x_ref, bias, qkv_ref, proj_ref).astype(f32))
+    put(a_ref, 288, 288, 1, attend_fine(x_ref, bias1_ref, qkv_ref, proj_ref).astype(f32))
     for t in range(2):
         for rho in range(3, 12):
             for z in range(WZ):
@@ -283,7 +285,7 @@
 
 
 def coarse_kernel(
-    flags_ref, y_ref, got_ref, fine_up_ref, fine_down_ref, merge_ref, early2_ref, late2_ref, qkv_ref, proj_ref, up_ref, down_ref,
+    y_ref, got_ref, fine_up_ref, fine_down_ref, merge_ref, bias_ref, qkv_ref, proj_ref, up_ref, down_ref,
     keep_ref, lower_ref, corner_ref, left_ref, w_ref, p_ref, o_ref,
 ):
     got = got_ref[...].astype(f32)
@@ -311,12 +313,11 @@
     normed = normalise(merged)
     qkv = dot(normed, qkv_ref[...]).astype(bf16)
     product = merged
-    bias = early_or_late(flags_ref, early2_ref, late2_ref)
     for g in range(3):
         q = qkv[:, g * 128 : (g + 1) * 128].astype(f32)
         k = qkv[:, 384 + g * 128 : 384 + (g + 1) * 128]
         v = qkv[:, 768 + g * 128 : 768 + (g + 1) * 128]
-        mixed = attend_group(q, k, v, bias(g * 4, (g + 1) * 4, 0, CELLS), 4)
+        mixed = attend_group(q, k, v, bias_ref[g * 4 : (g + 1) * 4], 4)
         product = product + dot(mixed.astype(bf16), proj_ref[g * 128 : (g + 1) * 128, :])
     attended = product.astype(bf16).astype(f32)
     put(o_ref, 0, CELLS, 1, feed_forward(attended, up_ref, down_ref))
@@ -364,7 +365,7 @@
     fine_tables = fine_bias.transpose(0, 2, 3, 1, 4)
     coarse_tables = coarse_bias.transpose(0, 2, 3, 1, 4)
     fine_down = fine_down.T
-    expansion = [((6 * 32, CELLS), f32), ((6 * 16, LINES * 32), f32)]
+    expansion = [((6 * 32, CELLS), f32), ((6 * LINES, LINES * 32), f32)]
     biases = [((6, CELLS, CELLS), f32), ((12, CELLS, CELLS), f32)]
     left = from_behind(fields, 1, 0)
     sources = [fields, fine_tables, coarse_tables, fine_qkv, fine_proj]
@@ -392,26 +393,28 @@
         smem=1,
     )
     got = from_behind(edge, 0, -1)
-    late1, late2 = call(
-        other_bias_kernel, biases, expansion, [flags, fine_tables, coarse_tables, first], 2_000_000_000, smem=1
+    bias1, bias2 = call(
+        other_bias_kernel,
+        biases,
+        expansion,
+        [flags, fine_tables, coarse_tables, bias1, bias2, first],
+        2_000_000_000,
+        smem=1,
     )
     (finished,) = call(
         second_rows_kernel,
         [((432, 192), bf16)],
         [tiles_of(576, 192), tiles_of(576, 192), tiles_of(432, 192)],
-        [flags, left, own, corner, below, first, bias1, late1, fine_qkv, fine_proj, fine_up, fine_down],
+        [left, own, corner, below, first, bias1, fine_qkv, fine_proj, fine_up, fine_down],
         3_000_000_000,
-        smem=1,
     )
     quarter = ((3, 6, WZ, 384), bf16)
     keep, lower, far_corner, upper_left = call(
         coarse_kernel,
         [quarter] * 4,
         [tiles_of(576, 192), tiles_of(576, 192), tiles_of(CELLS, 384)],
-        [flags, finished, got, fine_up, fine_down, merge_weight, bias2, late2]
-        + [coarse_qkv, coarse_proj, coarse_up, coarse_down],
+        [finished, got, fine_up, fine_down, merge_weight, bias2, coarse_qkv, coarse_proj, coarse_up, coarse_down],
         4_000_000_000,
-        smem=1,
     )
     above = from_behind(lower, 0, 1)
     corner = from_behind(far_corner, -1, 1)

time: 63.6 us -> 62.4 us (0.981)
  the two profiles are of different devices: /device:TPU:511 before, /device:TPU:1 now
where the time goes in v8:
time: 62.4 us; the launch traced here: 61.5 us
  starting transfers between devices  42.9 us (69%)
  Pallas kernels  14.9 us (24%)
  waiting for transfers between devices  2.47 us (4%)
  other arithmetic  0.88 us (1%)
    ppermute x7, starting transfers between devices, from_behind(): return lax.ppermute(shard, ('lon', 'lat'), pairs)  42.9 us
    pallas_call x4, Pallas kernels, call(): pl.pallas_call(kernel, out_shape=[jax.ShapeDtypeStruct(shape, dtype) for...  9.83 us
    pallas_call x1, Pallas kernels, body(): pl.pallas_call(prepare_kernel, out_shape=[jax.ShapeDtypeStruct((162, 128)...  5.07 us
    ppermute x7, waiting for transfers between devices, from_behind(): return lax.ppermute(shard, ('lon', 'lat'), pairs)  2.47 us
  transfers between devices with their start and end apart: 7, of which 1 were waited for; matrix products, arithmetic and copies ran while one was open for 0% of the time, Pallas kernels for 17%

profile of v8, /device:TPU:1, one launch (start us, length us, event | category | flops | bytes accessed | tf_op | source)
XLA Modules:
  0.0 61.5 jit_solution(6007905784117669743)
XLA Ops:
  0.0 4.5 %collective-permute-start = (bf16[2,12,24,192]{3,2,1,0:T(8,128)(2,1)}, bf16[2,12,24,192]{3,2,1,0:T(8,128)(2,1)S(1)}, u32[]{:S(2)}, u32[]{:S(2)}) collective-permute-start(bf16[2,12,24,192]{3,2,1,0:T(8,128)(2,1)} %fields_hbm.1), channel_id=1, source_target_pairs={{0,8},{1,9},{2,10},{3,11},{4,12},{5,13},{6,14},{7,15},{8,16},{9,17... | collective-permute-start | bytes 663560 | tf_op jit(solution)/shard_map/ppermute | solution.py:30
  4.5 0.1 add_convert_fusion.flags_ref
  4.6 5.1 %shard_map.118 = (bf16[162,128]{1,0:T(8,128)(2,1)S(1)}, bf16[162,128]{1,0:T(8,128)(2,1)S(1)}, bf16[2,12,24,192]{3,2,1,0:T(8,128)(2,1)S(1)}, f32[2,6,23,1,144]{4,...) custom-call(s32[2]{0:T(128)S(1)} %add_convert_fusion.flags_ref, ...), custom_call_target="tpu_custom_call" | custom-call | tf_op jit(solution)/shard_map/pallas_call | solution.py:373
  9.7 14.4 %collective-permute-start.1 = (bf16[162,128]{1,0:T(8,128)(2,1)S(1)}, bf16[162,128]{1,0:T(8,128)(2,1)S(1)}, u32[]{:S(2)}, u32[]{:S(2)}) collective-permute-start(bf16[162,128]{1,0:T(8,128)(2,1)S(1)} %get-tuple-element.24), channel_id=1, source_target_pairs={{0,15},{1,8},{2,9},{3,10},{4,11},{5,12},{6,13},{7,14},{8,23},{9,16... | collective-permute-start | bytes 124424 | tf_op jit(solution)/shard_map/ppermute | solution.py:30
  24.1 2.4 %collective-permute-start.2 = (bf16[162,128]{1,0:T(8,128)(2,1)S(1)}, bf16[162,128]{1,0:T(8,128)(2,1)S(1)}, u32[]{:S(2)}, u32[]{:S(2)}) collective-permute-start(bf16[162,128]{1,0:T(8,128)(2,1)S(1)} %get-tuple-element.25), channel_id=1, source_target_pairs={{0,7},{1,0},{2,1},{3,2},{4,3},{5,4},{6,5},{7,6},{8,15},{9,8},{10,9... | collective-permute-start | bytes 124424 | tf_op jit(solution)/shard_map/ppermute | solution.py:30
  26.4 0.0 collective-permute-done.left_ref
  26.5 2.3 %shard_map.119 = (bf16[288,192]{1,0:T(8,128)(2,1)S(1)}, bf16[216,128]{1,0:T(8,128)(2,1)S(1)}) custom-call(s32[2]{0:T(128)S(1)} %add_convert_fusion.flags_ref, bf16[2,12,24,192]{3,2,1,0:T(8,128)(2,1)S(1)} %collective-permute-done.left_ref, bf16[2,12,24,192]{3,2,1,0:T(8,128)(2,1)S(1)} %get-tuple-element.23.own_ref, ...), custom_call_target="tpu_custom_call" | custom-call | flops 1000000000 | bytes 1393928 | tf_op jit(solution)/shard_map/pallas_call | solution.py:333
  28.8 3.3 %collective-permute-start.3 = (bf16[216,128]{1,0:T(8,128)(2,1)S(1)}, bf16[216,128]{1,0:T(8,128)(2,1)S(1)}, u32[]{:S(2)}, u32[]{:S(2)}) collective-permute-start(bf16[216,128]{1,0:T(8,128)(2,1)S(1)} %get-tuple-element.35), channel_id=1, source_target_pairs={{0,7},{1,0},{2,1},{3,2},{4,3},{5,4},{6,5},{7,6},{8,15},{9,8},{10,9... | collective-permute-start | bytes 165896 | tf_op jit(solution)/shard_map/ppermute | solution.py:30
  32.0 0.0 copy-start.4
  32.1 0.0 copy-start.5
  32.1 0.9 %shard_map.120 = (f32[6,144,144]{2,1,0:T(8,128)S(1)}, f32[12,144,144]{2,1,0:T(8,128)S(1)}) custom-call(s32[2]{0:T(128)S(1)} %add_convert_fusion.flags_ref, f32[2,6,23,1,144]{4,3,2,1,0:T(1,128)S(1)} %get-tuple-element.26.fine_ref, f32[1,12,23,1,144]{4,3,2,1,0:T(1,128)S(1)} %get-tuple-element.31.coarse_ref, f32[6,144,144]{2,1,0:T(8,128)S(1)} %get-tuple-element.32.early1_ref, ...), custom_call_target="tpu_custom_call" | custom-call | flops 2000000000 | bytes 1921544 | tf_op jit(solution)/shard_map/pallas_call | solution.py:333
  33.0 0.0 collective-permute-done.1.corner_ref
  33.0 0.0 collective-permute-done.2.below_ref
  33.0 0.0 copy-done.4
  33.0 0.1 copy-done.5
  33.1 0.0 copy-start
  33.1 0.0 copy-start.6
  33.1 2.4 %shard_map.121.y_ref = bf16[432,192]{1,0:T(8,128)(2,1)S(1)} custom-call(bf16[2,12,24,192]{3,2,1,0:T(8,128)(2,1)S(1)} %collective-permute-done.left_ref, bf16[2,12,24,192]{3,2,1,0:T(8,128)(2,1)S(1)} %get-tuple-element.23.own_ref, bf16[162,128]{1,0:T(8,128)(2,1)S(1)} %collective-permute-done.1.corner_ref, ...), custom_call_target="tpu_custom_call" | custom-call | flops 3000000000 | bytes 2018304 | tf_op jit(solution)/shard_map/pallas_call | solution.py:333
  35.6 0.0 collective-permute-done.3.got_ref
  35.6 0.0 copy-done
  35.6 0.0 copy-done.1
  35.6 0.0 copy-done.2
  35.6 0.0 copy-done.3
  35.6 0.0 copy-done.6
  35.6 4.2 %shard_map.122 = (bf16[3,6,2,384]{3,2,1,0:T(2,128)(2,1)S(1)}, bf16[3,6,2,384]{3,2,1,0:T(2,128)(2,1)S(1)}, bf16[3,6,2,384]{3,2,1,0:T(2,128)(2,1)S(1)}, bf16[3,6,2,384]{3,2,1,0:T(2,128)(2,1)S(1)}) custom-call(bf16[432,192]{1,0:T(8,128)(2,1)S(1)} %shard_map.121.y_ref, bf16[216,128]{1,0:T(8,128)(2,1)S(1)} %collective-permute-done.3.got_ref, ...), custom_call_target="tpu_custom_call" | custom-call | flops 4000000000 | bytes 5935104 | tf_op jit(solution)/shard_map/pallas_call | solution.py:333
  39.8 2.0 %collective-permute-start.4 = (bf16[3,6,2,384]{3,2,1,0:T(2,128)(2,1)S(1)}, bf16[3,6,2,384]{3,2,1,0:T(2,128)(2,1)S(1)}, u32[]{:S(2)}, u32[]{:S(2)}) collective-permute-start(bf16[3,6,2,384]{3,2,1,0:T(2,128)(2,1)S(1)} %get-tuple-element.37), channel_id=1, source_target_pairs={{0,1},{1,2},{2,3},{3,4},{4,5},{5,6},{6,7},{7,0},{8,9},{9,10},{10,1... | collective-permute-start | bytes 82952 | tf_op jit(solution)/shard_map/ppermute | solution.py:30
  41.8 4.3 %collective-permute-start.5 = (bf16[3,6,2,384]{3,2,1,0:T(2,128)(2,1)S(1)}, bf16[3,6,2,384]{3,2,1,0:T(2,128)(2,1)S(1)}, u32[]{:S(2)}, u32[]{:S(2)}) collective-permute-start(bf16[3,6,2,384]{3,2,1,0:T(2,128)(2,1)S(1)} %get-tuple-element.38), channel_id=1, source_target_pairs={{0,505},{1,506},{2,507},{3,508},{4,509},{5,510},{6,511},{7,504},{8... | collective-permute-start | bytes 82952 | tf_op jit(solution)/shard_map/ppermute | solution.py:30
  46.1 12.0 %collective-permute-start.6 = (bf16[3,6,2,384]{3,2,1,0:T(2,128)(2,1)S(1)}, bf16[3,6,2,384]{3,2,1,0:T(2,128)(2,1)S(1)}, u32[]{:S(2)}, u32[]{:S(2)}) collective-permute-start(bf16[3,6,2,384]{3,2,1,0:T(2,128)(2,1)S(1)} %get-tuple-element.40), channel_id=1, source_target_pairs={{0,504},{1,505},{2,506},{3,507},{4,508},{5,509},{6,510},{7,511},{8... | collective-permute-start | bytes 82952 | tf_op jit(solution)/shard_map/ppermute | solution.py:30
  58.2 0.0 collective-permute-done.4
  58.2 2.5 %collective-permute-done.5 = bf16[3,6,2,384]{3,2,1,0:T(2,128)(2,1)S(1)} collective-permute-done((bf16[3,6,2,384]{3,2,1,0:T(2,128)(2,1)S(1)}, bf16[3,6,2,384]{3,2,1,0:T(2,128)(2,1)S(1)}, u32[]{:S(2)}, u32[]{:S(2)}) %collective-permute-start.5) | collective-permute-done | bytes 27680 | tf_op jit(solution)/shard_map/ppermute | solution.py:30
  60.6 0.0 collective-permute-done.6
  60.6 0.8 %maximum_bitcast_fusion = bf16[2,6,12,384]{3,0,2,1:T(2,128)(2,1)} fusion(bf16[3,6,2,384]{3,2,1,0:T(2,128)(2,1)S(1)} %collective-permute-done.6, bf16[3,6,2,384]{3,2,1,0:T(2,128)(2,1)S(1)} %get-tuple-element.39, bf16[3,6,2,384]{3,2,1,0:T(2,128)(2,1)S(1)} %collective-permute-done.5, bf16[3,6,2,384]{3,2,1,0:T(2,128)(2,1)S(1)} %collective-permute-done.4), kind=kLoop, calls=%fused_computation | loop fusion | flops 165888 | bytes 221184 | tf_op jit(solution)/shard_map/transpose | solution.py:423
  (3 shorter events, 0.0 us)
Async XLA Ops:
  0.0 26.4 %collective-permute-start = (bf16[2,12,24,192]{3,2,1,0:T(8,128)(2,1)}, bf16[2,12,24,192]{3,2,1,0:T(8,128)(2,1)S(1)}, u32[]{:S(2)}, u32[]{:S(2)}) collective-permute-start(bf16[2,12,24,192]{3,2,1,0:T(8,128)(2,1)} %fields_hbm.1), channel_id=1, source_target_pairs={{0,8},{1,9},{2,10},{3,11},{4,12},{5,13},{6,14},{7,15},{8,16},{9,17... | collective-permute-start | bytes 663560 | tf_op jit(solution)/shard_map/ppermute | solution.py:30
  9.7 23.3 %collective-permute-start.1 = (bf16[162,128]{1,0:T(8,128)(2,1)S(1)}, bf16[162,128]{1,0:T(8,128)(2,1)S(1)}, u32[]{:S(2)}, u32[]{:S(2)}) collective-permute-start(bf16[162,128]{1,0:T(8,128)(2,1)S(1)} %get-tuple-element.24), channel_id=1, source_target_pairs={{0,15},{1,8},{2,9},{3,10},{4,11},{5,12},{6,13},{7,14},{8,23},{9,16... | collective-permute-start | bytes 124424 | tf_op jit(solution)/shard_map/ppermute | solution.py:30
  24.1 8.9 %collective-permute-start.2 = (bf16[162,128]{1,0:T(8,128)(2,1)S(1)}, bf16[162,128]{1,0:T(8,128)(2,1)S(1)}, u32[]{:S(2)}, u32[]{:S(2)}) collective-permute-start(bf16[162,128]{1,0:T(8,128)(2,1)S(1)} %get-tuple-element.25), channel_id=1, source_target_pairs={{0,7},{1,0},{2,1},{3,2},{4,3},{5,4},{6,5},{7,6},{8,15},{9,8},{10,9... | collective-permute-start | bytes 124424 | tf_op jit(solution)/shard_map/ppermute | solution.py:30
  28.8 6.8 %collective-permute-start.3 = (bf16[216,128]{1,0:T(8,128)(2,1)S(1)}, bf16[216,128]{1,0:T(8,128)(2,1)S(1)}, u32[]{:S(2)}, u32[]{:S(2)}) collective-permute-start(bf16[216,128]{1,0:T(8,128)(2,1)S(1)} %get-tuple-element.35), channel_id=1, source_target_pairs={{0,7},{1,0},{2,1},{3,2},{4,3},{5,4},{6,5},{7,6},{8,15},{9,8},{10,9... | collective-permute-start | bytes 165896 | tf_op jit(solution)/shard_map/ppermute | solution.py:30
  32.0 1.0 %copy-start.4 = (bf16[192,768]{1,0:T(8,128)(2,1)S(1)}, bf16[192,768]{1,0:T(8,128)(2,1)}, u32[]{:S(2)}) copy-start(bf16[192,768]{1,0:T(8,128)(2,1)} %fine_up_ref.1) | copy-start | bytes 884740
  32.1 1.0 %copy-start.5 = (bf16[768,192]{0,1:T(8,128)(2,1)S(1)}, bf16[768,192]{0,1:T(8,128)(2,1)}, u32[]{:S(2)}) copy-start(bf16[768,192]{0,1:T(8,128)(2,1)} %param.17) | copy-start | bytes 884740
  33.1 2.5 %copy-start = (bf16[384,1536]{1,0:T(8,128)(2,1)S(1)}, bf16[384,1536]{1,0:T(8,128)(2,1)}, u32[]{:S(2)}) copy-start(bf16[384,1536]{1,0:T(8,128)(2,1)} %up_ref.3) | copy-start | bytes 3538948
  33.1 2.5 %copy-start.1 = (bf16[1536,384]{1,0:T(8,128)(2,1)S(1)}, bf16[1536,384]{1,0:T(8,128)(2,1)}, u32[]{:S(2)}) copy-start(bf16[1536,384]{1,0:T(8,128)(2,1)} %down_ref.1) | copy-start | bytes 3538948
  33.1 2.5 %copy-start.2 = (bf16[384,1152]{1,0:T(8,128)(2,1)S(1)}, bf16[384,1152]{1,0:T(8,128)(2,1)}, u32[]{:S(2)}) copy-start(bf16[384,1152]{1,0:T(8,128)(2,1)} %qkv_ref.1) | copy-start | bytes 2654212
  33.1 2.5 %copy-start.3 = (bf16[768,384]{1,0:T(8,128)(2,1)S(1)}, bf16[768,384]{1,0:T(8,128)(2,1)}, u32[]{:S(2)}) copy-start(bf16[768,384]{1,0:T(8,128)(2,1)} %merge_ref.1) | copy-start | bytes 1769476
  33.1 2.5 %copy-start.6 = (bf16[384,384]{1,0:T(8,128)(2,1)S(1)}, bf16[384,384]{1,0:T(8,128)(2,1)}, u32[]{:S(2)}) copy-start(bf16[384,384]{1,0:T(8,128)(2,1)} %proj_ref.1) | copy-start | bytes 884740
  39.8 18.4 %collective-permute-start.4 = (bf16[3,6,2,384]{3,2,1,0:T(2,128)(2,1)S(1)}, bf16[3,6,2,384]{3,2,1,0:T(2,128)(2,1)S(1)}, u32[]{:S(2)}, u32[]{:S(2)}) collective-permute-start(bf16[3,6,2,384]{3,2,1,0:T(2,128)(2,1)S(1)} %get-tuple-element.37), channel_id=1, source_target_pairs={{0,1},{1,2},{2,3},{3,4},{4,5},{5,6},{6,7},{7,0},{8,9},{9,10},{10,1... | collective-permute-start | bytes 82952 | tf_op jit(solution)/shard_map/ppermute | solution.py:30
  41.8 18.8 %collective-permute-start.5 = (bf16[3,6,2,384]{3,2,1,0:T(2,128)(2,1)S(1)}, bf16[3,6,2,384]{3,2,1,0:T(2,128)(2,1)S(1)}, u32[]{:S(2)}, u32[]{:S(2)}) collective-permute-start(bf16[3,6,2,384]{3,2,1,0:T(2,128)(2,1)S(1)} %get-tuple-element.38), channel_id=1, source_target_pairs={{0,505},{1,506},{2,507},{3,508},{4,509},{5,510},{6,511},{7,504},{8... | collective-permute-start | bytes 82952 | tf_op jit(solution)/shard_map/ppermute | solution.py:30
  46.1 14.5 %collective-permute-start.6 = (bf16[3,6,2,384]{3,2,1,0:T(2,128)(2,1)S(1)}, bf16[3,6,2,384]{3,2,1,0:T(2,128)(2,1)S(1)}, u32[]{:S(2)}, u32[]{:S(2)}) collective-permute-start(bf16[3,6,2,384]{3,2,1,0:T(2,128)(2,1)S(1)} %get-tuple-element.40), channel_id=1, source_target_pairs={{0,504},{1,505},{2,506},{3,507},{4,508},{5,509},{6,510},{7,511},{8... | collective-permute-start | bytes 82952 | tf_op jit(solution)/shard_map/ppermute | solution.py:30

commit v9 on v8

--- a/solution.py
+++ b/solution.py
@@ -81,7 +81,7 @@
     row, lane = iota((6 * LINES, 384), 0) % LINES, iota((6 * LINES, 384), 1) % LINES
     levels_differ = row // WLAT != lane // WLAT
     rows_differ = (row % WLAT >= WLAT // 2) != (lane % WLAT >= WLAT // 2)
-    slot = iota((16, 128), 1) // 32
+    slot, kept = iota((16, 128), 1) // 32, iota((6 * LINES, 128), 1)
     for (table_of, last), out_of in zip(tables, outs, strict=True):
         for head in range(6):
             stacked[head * 32 : head * 32 + SPAN, :] = table_of(head)
@@ -97,11 +97,16 @@
                     block = piece if block is None else jnp.where(slot == at, piece, block)
                 spread_from[head * LINES : (head + 1) * LINES, group * 128 : (group + 1) * 128] = block[:LINES]
         flat = sum(dot(part, spread) for part in two_parts(spread_from[...]))
-        apart = levels_differ if last is None else levels_differ | (rows_differ & (last > 0))
+        apart = levels_differ if last is None else levels_differ | (rows_differ & last)
         flat = jnp.where(apart, MASKED, flat)
         for o in range(WLON):
             start = (WLON - 1 - o) * LINES
-            piece = flat[:, start : start + CELLS]
+            tile, shift = divmod(start, 128)
+            parts = [flat[:, t * 128 : (t + 1) * 128] for t in range(tile, min(tile + 3, 3))]
+            if shift:
+                parts = [pltpu.roll(part, 128 - shift, 1) for part in parts]
+                parts = [jnp.where(kept < 128 - shift, a, b) for a, b in zip(parts, parts[1:] + parts[-1:], strict=True)]
+            piece = jnp.concatenate([parts[0], parts[1][:, : CELLS - 128]], axis=-1)
             for head in range(6):
                 out_of(head, o * LINES, piece[head * LINES : (head + 1) * LINES])
 
@@ -170,10 +175,17 @@
     expand_bias(tables, [writer(bias1_ref, 0), writer(bias2_ref, 0), writer(bias2_ref, 6)], stacked, spread_from)
 
 
+def place():
+    lat, lats = lax.axis_index("lat"), lax.axis_size("lat")
+    lon, lons = lax.axis_index("lon"), lax.axis_size("lon")
+    return lat == lats - 1, (lat < lats // 2) & (lon < lons // 2)
+
+
 def prepare_kernel(
-    flags_ref, fields_hbm, fine_hbm, coarse_hbm, qkv_hbm, proj_hbm, below_ref, corner_ref, own_ref, fine_ref,
+    fields_hbm, fine_hbm, coarse_hbm, qkv_hbm, proj_hbm, below_ref, corner_ref, own_ref, fine_ref,
     coarse_ref, qkv_ref, proj_ref, bias0_ref, bias1_ref, bias2_ref, line_ref, stacked, spread_from, sems,
 ):
+    last, early = place()
     moves = [
         (fields_hbm.at[:, 0:3], own_ref.at[:, 0:3]),
         (fine_hbm, fine_ref),
@@ -196,23 +208,25 @@
     for copy in copies[1:]:
         copy.wait()
 
-    @pl.when(flags_ref[1] > 0)
+    @pl.when(early)
     def _():
         expand_first(fine_ref, bias0_ref, stacked, spread_from)
-        expand_others(flags_ref[0], fine_ref, coarse_ref, bias1_ref, bias2_ref, stacked, spread_from)
+        expand_others(last, fine_ref, coarse_ref, bias1_ref, bias2_ref, stacked, spread_from)
 
 
 def other_bias_kernel(
-    flags_ref, fine_ref, coarse_ref, early1_ref, early2_ref, after_ref, bias1_ref, bias2_ref, stacked, spread_from
-):
-    @pl.when(flags_ref[1] > 0)
+    fine_ref, coarse_ref, early1_ref, early2_ref, after_ref, bias1_ref, bias2_ref, stacked, spread_from
+):
+    last, early = place()
+
+    @pl.when(early)
     def _():
         bias1_ref[...] = early1_ref[...]
         bias2_ref[...] = early2_ref[...]
 
-    @pl.when(flags_ref[1] == 0)
+    @pl.when(jnp.logical_not(early))
     def _():
-        expand_others(flags_ref[0], fine_ref, coarse_ref, bias1_ref, bias2_ref, stacked, spread_from)
+        expand_others(last, fine_ref, coarse_ref, bias1_ref, bias2_ref, stacked, spread_from)
 
 
 def attend_fine(x_ref, bias_ref, qkv_ref, proj_ref):
@@ -235,14 +249,16 @@
 
 
 def first_rows_kernel(
-    flags_ref, left_ref, own_ref, fine_ref, early0_ref, qkv_ref, proj_ref,
+    left_ref, own_ref, fine_ref, early0_ref, qkv_ref, proj_ref,
     out_ref, send_ref, bias0_ref, x_ref, a_ref, stacked, spread_from,
 ):
-    @pl.when(flags_ref[1] == 0)
+    _, early = place()
+
+    @pl.when(jnp.logical_not(early))
     def _():
         expand_first(fine_ref, bias0_ref, stacked, spread_from)
 
-    @pl.when(flags_ref[1] > 0)
+    @pl.when(early)
     def _():
         bias0_ref[...] = early0_ref[...]
 
@@ -327,9 +343,8 @@
                 ref[i, j % 6] = get(o_ref, j * LINES + row, WZ, WLAT, 384).astype(bf16)
 
 
-def call(kernel, outs, scratch, operands, flops, smem=0):
-    specs = [pl.BlockSpec(memory_space=pltpu.SMEM)] * smem
-    specs += [pl.BlockSpec(memory_space=pltpu.VMEM)] * (len(operands) - smem)
+def call(kernel, outs, scratch, operands, flops):
+    specs = [pl.BlockSpec(memory_space=pltpu.VMEM)] * len(operands)
     return pl.pallas_call(
         kernel,
         out_shape=[jax.ShapeDtypeStruct(shape, dtype) for shape, dtype in outs],
@@ -359,9 +374,6 @@
     coarse_up,
     coarse_down,
 ):
-    lat, lats = lax.axis_index("lat"), lax.axis_size("lat")
-    lon, lons = lax.axis_index("lon"), lax.axis_size("lon")
-    flags = jnp.stack([lat == lats - 1, (lat < lats // 2) & (lon < lons // 2)]).astype(jnp.int32)
     fine_tables = fine_bias.transpose(0, 2, 3, 1, 4)
     coarse_tables = coarse_bias.transpose(0, 2, 3, 1, 4)
     fine_down = fine_down.T
@@ -369,37 +381,35 @@
     biases = [((6, CELLS, CELLS), f32), ((12, CELLS, CELLS), f32)]
     left = from_behind(fields, 1, 0)
     sources = [fields, fine_tables, coarse_tables, fine_qkv, fine_proj]
-    hbm, vmem, smem = (pl.BlockSpec(memory_space=space) for space in (pltpu.HBM, pltpu.VMEM, pltpu.SMEM))
+    hbm, vmem = (pl.BlockSpec(memory_space=space) for space in (pltpu.HBM, pltpu.VMEM))
     below, corner, own, fine_tables, coarse_tables, fine_qkv, fine_proj, bias0, bias1, bias2 = pl.pallas_call(
         prepare_kernel,
         out_shape=[jax.ShapeDtypeStruct((162, 128), bf16)] * 2
         + [jax.ShapeDtypeStruct(source.shape, source.dtype) for source in sources]
         + [jax.ShapeDtypeStruct(shape, dtype) for shape, dtype in [((6, CELLS, CELLS), f32)] + biases],
-        in_specs=[smem] + [hbm] * 5,
+        in_specs=[hbm] * 5,
         out_specs=[vmem] * 10,
         scratch_shapes=[pltpu.VMEM((162, 128), f32)]
         + [pltpu.VMEM(shape, dtype) for shape, dtype in expansion]
         + [pltpu.SemaphoreType.DMA((6,))],
         compiler_params=pltpu.CompilerParams(vmem_limit_bytes=VMEM_LIMIT),
-    )(flags, *(pltpu.with_memory_space_constraint(source, pltpu.HBM) for source in sources))
+    )(*(pltpu.with_memory_space_constraint(source, pltpu.HBM) for source in sources))
     corner = from_behind(corner, 1, -1)
     below = from_behind(below, 0, -1)
     first, edge = call(
         first_rows_kernel,
         [((288, 192), bf16), ((216, 128), bf16)],
         [((6, CELLS, CELLS), f32), tiles_of(576, 192), tiles_of(288, 192)] + expansion,
-        [flags, left, own, fine_tables, bias0, fine_qkv, fine_proj],
+        [left, own, fine_tables, bias0, fine_qkv, fine_proj],
         1_000_000_000,
-        smem=1,
     )
     got = from_behind(edge, 0, -1)
     bias1, bias2 = call(
         other_bias_kernel,
         biases,
         expansion,
-        [flags, fine_tables, coarse_tables, bias1, bias2, first],
+        [fine_tables, coarse_tables, bias1, bias2, first],
         2_000_000_000,
-        smem=1,
     )
     (finished,) = call(
         second_rows_kernel,

time: 62.4 us -> 61.4 us (0.984)
  Pallas kernels: 14.9 us -> 13.3 us
  waiting for transfers between devices: 2.47 us -> 3.58 us
    ppermute x7, waiting for transfers between devices: 2.47 us -> 3.58 us  [from_behind(): return lax.ppermute(shard, ('lon', 'lat'), pairs)]
    pallas_call x4, Pallas kernels: 9.83 us -> 8.8 us  [call(): pl.pallas_call(kernel, out_shape=[jax.ShapeDtypeStruct(shape, dtype) for...]
  transfers between devices with their start and end apart: 7 -> 7, of which waited for: 1 -> 1; matrix products, arithmetic and copies ran while one was open for 0% -> 0% of each run, Pallas kernels for 17% -> 15%
where the time goes in v9:
time: 61.4 us; the launch traced here: 60.9 us
  starting transfers between devices  42.3 us (69%)
  Pallas kernels  13.3 us (22%)
  waiting for transfers between devices  3.58 us (6%)
  other arithmetic  0.81 us (1%)
  local copies, waits for them, and re-layouts  0.66 us (1%)
    ppermute x7, starting transfers between devices, from_behind(): return lax.ppermute(shard, ('lon', 'lat'), pairs)  42.3 us
    pallas_call x4, Pallas kernels, call(): pl.pallas_call(kernel, out_shape=[jax.ShapeDtypeStruct(shape, dtype) for...  8.8 us
    pallas_call x1, Pallas kernels, body(): pl.pallas_call(prepare_kernel, out_shape=[jax.ShapeDtypeStruct((162, 128)...  4.52 us
    ppermute x7, waiting for transfers between devices, from_behind(): return lax.ppermute(shard, ('lon', 'lat'), pairs)  3.58 us
  transfers between devices with their start and end apart: 7, of which 1 were waited for; matrix products, arithmetic and copies ran while one was open for 0% of the time, Pallas kernels for 15%

profile of v9, /device:TPU:1, one launch (start us, length us, event | category | flops | bytes accessed | tf_op | source)
XLA Modules:
  0.0 60.9 jit_solution(15396106204531265782)
XLA Ops:
  0.0 4.5 %collective-permute-start = (bf16[2,12,24,192]{3,2,1,0:T(8,128)(2,1)}, bf16[2,12,24,192]{3,2,1,0:T(8,128)(2,1)S(1)}, u32[]{:S(2)}, u32[]{:S(2)}) collective-permute-start(bf16[2,12,24,192]{3,2,1,0:T(8,128)(2,1)} %fields_hbm.1), channel_id=1, source_target_pairs={{0,8},{1,9},{2,10},{3,11},{4,12},{5,13},{6,14},{7,15},{8,16},{9,17... | collective-permute-start | bytes 663560 | tf_op jit(solution)/shard_map/ppermute | solution.py:30
  4.5 4.5 %shard_map.118 = (bf16[162,128]{1,0:T(8,128)(2,1)S(1)}, bf16[162,128]{1,0:T(8,128)(2,1)S(1)}, bf16[2,12,24,192]{3,2,1,0:T(8,128)(2,1)S(1)}, f32[2,6,23,1,144]{4,...) custom-call(bf16[2,12,24,192]{3,2,1,0:T(8,128)(2,1)} %fields_hbm.1, ...), custom_call_target="tpu_custom_call" | custom-call | tf_op jit(solution)/shard_map/pallas_call | solution.py:385
  9.0 14.4 %collective-permute-start.1 = (bf16[162,128]{1,0:T(8,128)(2,1)S(1)}, bf16[162,128]{1,0:T(8,128)(2,1)S(1)}, u32[]{:S(2)}, u32[]{:S(2)}) collective-permute-start(bf16[162,128]{1,0:T(8,128)(2,1)S(1)} %get-tuple-element.24), channel_id=1, source_target_pairs={{0,15},{1,8},{2,9},{3,10},{4,11},{5,12},{6,13},{7,14},{8,23},{9,16... | collective-permute-start | bytes 124424 | tf_op jit(solution)/shard_map/ppermute | solution.py:30
  23.4 2.4 %collective-permute-start.2 = (bf16[162,128]{1,0:T(8,128)(2,1)S(1)}, bf16[162,128]{1,0:T(8,128)(2,1)S(1)}, u32[]{:S(2)}, u32[]{:S(2)}) collective-permute-start(bf16[162,128]{1,0:T(8,128)(2,1)S(1)} %get-tuple-element.25), channel_id=1, source_target_pairs={{0,7},{1,0},{2,1},{3,2},{4,3},{5,4},{6,5},{7,6},{8,15},{9,8},{10,9... | collective-permute-start | bytes 124424 | tf_op jit(solution)/shard_map/ppermute | solution.py:30
  25.8 0.0 collective-permute-done.left_ref
  25.8 1.8 %shard_map.119 = (bf16[288,192]{1,0:T(8,128)(2,1)S(1)}, bf16[216,128]{1,0:T(8,128)(2,1)S(1)}) custom-call(bf16[2,12,24,192]{3,2,1,0:T(8,128)(2,1)S(1)} %collective-permute-done.left_ref, bf16[2,12,24,192]{3,2,1,0:T(8,128)(2,1)S(1)} %get-tuple-element.23.own_ref, f32[2,6,23,1,144]{4,3,2,1,0:T(1,128)S(1)} %get-tuple-element.26.fine_ref, ...), custom_call_target="tpu_custom_call" | custom-call | flops 1000000000 | bytes 1393920 | tf_op jit(solution)/shard_map/pallas_call | solution.py:348
  27.6 3.2 %collective-permute-start.3 = (bf16[216,128]{1,0:T(8,128)(2,1)S(1)}, bf16[216,128]{1,0:T(8,128)(2,1)S(1)}, u32[]{:S(2)}, u32[]{:S(2)}) collective-permute-start(bf16[216,128]{1,0:T(8,128)(2,1)S(1)} %get-tuple-element.35), channel_id=1, source_target_pairs={{0,7},{1,0},{2,1},{3,2},{4,3},{5,4},{6,5},{7,6},{8,15},{9,8},{10,9... | collective-permute-start | bytes 165896 | tf_op jit(solution)/shard_map/ppermute | solution.py:30
  30.9 0.0 copy-start.4
  30.9 0.0 copy-start.5
  30.9 0.4 shard_map.120
  31.3 0.0 collective-permute-done.1.corner_ref
  31.3 0.0 collective-permute-done.2.below_ref
  31.3 0.5 copy-done.4
  31.8 0.1 copy-done.5
  31.9 0.0 copy-start
  31.9 0.0 copy-start.1
  31.9 0.0 copy-start.6
  31.9 2.5 %shard_map.121.y_ref = bf16[432,192]{1,0:T(8,128)(2,1)S(1)} custom-call(bf16[2,12,24,192]{3,2,1,0:T(8,128)(2,1)S(1)} %collective-permute-done.left_ref, bf16[2,12,24,192]{3,2,1,0:T(8,128)(2,1)S(1)} %get-tuple-element.23.own_ref, bf16[162,128]{1,0:T(8,128)(2,1)S(1)} %collective-permute-done.1.corner_ref, ...), custom_call_target="tpu_custom_call" | custom-call | flops 3000000000 | bytes 2018304 | tf_op jit(solution)/shard_map/pallas_call | solution.py:348
  34.4 0.0 collective-permute-done.3.got_ref
  34.4 0.0 copy-done
  34.4 0.0 copy-done.1
  34.5 0.0 copy-done.2
  34.5 0.0 copy-done.3
  34.5 0.0 copy-done.6
  34.5 4.2 %shard_map.122 = (bf16[3,6,2,384]{3,2,1,0:T(2,128)(2,1)S(1)}, bf16[3,6,2,384]{3,2,1,0:T(2,128)(2,1)S(1)}, bf16[3,6,2,384]{3,2,1,0:T(2,128)(2,1)S(1)}, bf16[3,6,2,384]{3,2,1,0:T(2,128)(2,1)S(1)}) custom-call(bf16[432,192]{1,0:T(8,128)(2,1)S(1)} %shard_map.121.y_ref, bf16[216,128]{1,0:T(8,128)(2,1)S(1)} %collective-permute-done.3.got_ref, ...), custom_call_target="tpu_custom_call" | custom-call | flops 4000000000 | bytes 5935104 | tf_op jit(solution)/shard_map/pallas_call | solution.py:348
  38.7 2.0 %collective-permute-start.4 = (bf16[3,6,2,384]{3,2,1,0:T(2,128)(2,1)S(1)}, bf16[3,6,2,384]{3,2,1,0:T(2,128)(2,1)S(1)}, u32[]{:S(2)}, u32[]{:S(2)}) collective-permute-start(bf16[3,6,2,384]{3,2,1,0:T(2,128)(2,1)S(1)} %get-tuple-element.37), channel_id=1, source_target_pairs={{0,1},{1,2},{2,3},{3,4},{4,5},{5,6},{6,7},{7,0},{8,9},{9,10},{10,1... | collective-permute-start | bytes 82952 | tf_op jit(solution)/shard_map/ppermute | solution.py:30
  40.7 4.3 %collective-permute-start.5 = (bf16[3,6,2,384]{3,2,1,0:T(2,128)(2,1)S(1)}, bf16[3,6,2,384]{3,2,1,0:T(2,128)(2,1)S(1)}, u32[]{:S(2)}, u32[]{:S(2)}) collective-permute-start(bf16[3,6,2,384]{3,2,1,0:T(2,128)(2,1)S(1)} %get-tuple-element.38), channel_id=1, source_target_pairs={{0,505},{1,506},{2,507},{3,508},{4,509},{5,510},{6,511},{7,504},{8... | collective-permute-start | bytes 82952 | tf_op jit(solution)/shard_map/ppermute | solution.py:30
  45.0 11.5 %collective-permute-start.6 = (bf16[3,6,2,384]{3,2,1,0:T(2,128)(2,1)S(1)}, bf16[3,6,2,384]{3,2,1,0:T(2,128)(2,1)S(1)}, u32[]{:S(2)}, u32[]{:S(2)}) collective-permute-start(bf16[3,6,2,384]{3,2,1,0:T(2,128)(2,1)S(1)} %get-tuple-element.40), channel_id=1, source_target_pairs={{0,504},{1,505},{2,506},{3,507},{4,508},{5,509},{6,510},{7,511},{8... | collective-permute-start | bytes 82952 | tf_op jit(solution)/shard_map/ppermute | solution.py:30
  56.5 0.0 collective-permute-done.4
  56.5 3.6 %collective-permute-done.5 = bf16[3,6,2,384]{3,2,1,0:T(2,128)(2,1)S(1)} collective-permute-done((bf16[3,6,2,384]{3,2,1,0:T(2,128)(2,1)S(1)}, bf16[3,6,2,384]{3,2,1,0:T(2,128)(2,1)S(1)}, u32[]{:S(2)}, u32[]{:S(2)}) %collective-permute-start.5) | collective-permute-done | bytes 27680 | tf_op jit(solution)/shard_map/ppermute | solution.py:30
  60.1 0.0 collective-permute-done.6
  60.1 0.8 %maximum_bitcast_fusion = bf16[2,6,12,384]{3,0,2,1:T(2,128)(2,1)} fusion(bf16[3,6,2,384]{3,2,1,0:T(2,128)(2,1)S(1)} %collective-permute-done.6, bf16[3,6,2,384]{3,2,1,0:T(2,128)(2,1)S(1)} %get-tuple-element.39, bf16[3,6,2,384]{3,2,1,0:T(2,128)(2,1)S(1)} %collective-permute-done.5, bf16[3,6,2,384]{3,2,1,0:T(2,128)(2,1)S(1)} %collective-permute-done.4), kind=kLoop, calls=%fused_computation | loop fusion | flops 165888 | bytes 221184 | tf_op jit(solution)/shard_map/transpose | solution.py:433
  (2 shorter events, 0.0 us)
Async XLA Ops:
  0.0 25.8 %collective-permute-start = (bf16[2,12,24,192]{3,2,1,0:T(8,128)(2,1)}, bf16[2,12,24,192]{3,2,1,0:T(8,128)(2,1)S(1)}, u32[]{:S(2)}, u32[]{:S(2)}) collective-permute-start(bf16[2,12,24,192]{3,2,1,0:T(8,128)(2,1)} %fields_hbm.1), channel_id=1, source_target_pairs={{0,8},{1,9},{2,10},{3,11},{4,12},{5,13},{6,14},{7,15},{8,16},{9,17... | collective-permute-start | bytes 663560 | tf_op jit(solution)/shard_map/ppermute | solution.py:30
  9.0 22.2 %collective-permute-start.1 = (bf16[162,128]{1,0:T(8,128)(2,1)S(1)}, bf16[162,128]{1,0:T(8,128)(2,1)S(1)}, u32[]{:S(2)}, u32[]{:S(2)}) collective-permute-start(bf16[162,128]{1,0:T(8,128)(2,1)S(1)} %get-tuple-element.24), channel_id=1, source_target_pairs={{0,15},{1,8},{2,9},{3,10},{4,11},{5,12},{6,13},{7,14},{8,23},{9,16... | collective-permute-start | bytes 124424 | tf_op jit(solution)/shard_map/ppermute | solution.py:30
  23.4 7.8 %collective-permute-start.2 = (bf16[162,128]{1,0:T(8,128)(2,1)S(1)}, bf16[162,128]{1,0:T(8,128)(2,1)S(1)}, u32[]{:S(2)}, u32[]{:S(2)}) collective-permute-start(bf16[162,128]{1,0:T(8,128)(2,1)S(1)} %get-tuple-element.25), channel_id=1, source_target_pairs={{0,7},{1,0},{2,1},{3,2},{4,3},{5,4},{6,5},{7,6},{8,15},{9,8},{10,9... | collective-permute-start | bytes 124424 | tf_op jit(solution)/shard_map/ppermute | solution.py:30
  27.6 6.8 %collective-permute-start.3 = (bf16[216,128]{1,0:T(8,128)(2,1)S(1)}, bf16[216,128]{1,0:T(8,128)(2,1)S(1)}, u32[]{:S(2)}, u32[]{:S(2)}) collective-permute-start(bf16[216,128]{1,0:T(8,128)(2,1)S(1)} %get-tuple-element.35), channel_id=1, source_target_pairs={{0,7},{1,0},{2,1},{3,2},{4,3},{5,4},{6,5},{7,6},{8,15},{9,8},{10,9... | collective-permute-start | bytes 165896 | tf_op jit(solution)/shard_map/ppermute | solution.py:30
  30.9 1.0 %copy-start.4 = (bf16[192,768]{1,0:T(8,128)(2,1)S(1)}, bf16[192,768]{1,0:T(8,128)(2,1)}, u32[]{:S(2)}) copy-start(bf16[192,768]{1,0:T(8,128)(2,1)} %fine_up_ref.1) | copy-start | bytes 884740
  30.9 1.0 %copy-start.5 = (bf16[768,192]{0,1:T(8,128)(2,1)S(1)}, bf16[768,192]{0,1:T(8,128)(2,1)}, u32[]{:S(2)}) copy-start(bf16[768,192]{0,1:T(8,128)(2,1)} %param.17) | copy-start | bytes 884740
  31.9 2.5 %copy-start = (bf16[384,1536]{1,0:T(8,128)(2,1)S(1)}, bf16[384,1536]{1,0:T(8,128)(2,1)}, u32[]{:S(2)}) copy-start(bf16[384,1536]{1,0:T(8,128)(2,1)} %up_ref.3) | copy-start | bytes 3538948
  31.9 2.5 %copy-start.1 = (bf16[1536,384]{1,0:T(8,128)(2,1)S(1)}, bf16[1536,384]{1,0:T(8,128)(2,1)}, u32[]{:S(2)}) copy-start(bf16[1536,384]{1,0:T(8,128)(2,1)} %down_ref.1) | copy-start | bytes 3538948
  31.9 2.5 %copy-start.2 = (bf16[384,1152]{1,0:T(8,128)(2,1)S(1)}, bf16[384,1152]{1,0:T(8,128)(2,1)}, u32[]{:S(2)}) copy-start(bf16[384,1152]{1,0:T(8,128)(2,1)} %qkv_ref.1) | copy-start | bytes 2654212
  31.9 2.5 %copy-start.3 = (bf16[768,384]{1,0:T(8,128)(2,1)S(1)}, bf16[768,384]{1,0:T(8,128)(2,1)}, u32[]{:S(2)}) copy-start(bf16[768,384]{1,0:T(8,128)(2,1)} %merge_ref.1) | copy-start | bytes 1769476
  31.9 2.5 %copy-start.6 = (bf16[384,384]{1,0:T(8,128)(2,1)S(1)}, bf16[384,384]{1,0:T(8,128)(2,1)}, u32[]{:S(2)}) copy-start(bf16[384,384]{1,0:T(8,128)(2,1)} %proj_ref.1) | copy-start | bytes 884740
  38.7 17.8 %collective-permute-start.4 = (bf16[3,6,2,384]{3,2,1,0:T(2,128)(2,1)S(1)}, bf16[3,6,2,384]{3,2,1,0:T(2,128)(2,1)S(1)}, u32[]{:S(2)}, u32[]{:S(2)}) collective-permute-start(bf16[3,6,2,384]{3,2,1,0:T(2,128)(2,1)S(1)} %get-tuple-element.37), channel_id=1, source_target_pairs={{0,1},{1,2},{2,3},{3,4},{4,5},{5,6},{6,7},{7,0},{8,9},{9,10},{10,1... | collective-permute-start | bytes 82952 | tf_op jit(solution)/shard_map/ppermute | solution.py:30
  40.7 19.3 %collective-permute-start.5 = (bf16[3,6,2,384]{3,2,1,0:T(2,128)(2,1)S(1)}, bf16[3,6,2,384]{3,2,1,0:T(2,128)(2,1)S(1)}, u32[]{:S(2)}, u32[]{:S(2)}) collective-permute-start(bf16[3,6,2,384]{3,2,1,0:T(2,128)(2,1)S(1)} %get-tuple-element.38), channel_id=1, source_target_pairs={{0,505},{1,506},{2,507},{3,508},{4,509},{5,510},{6,511},{7,504},{8... | collective-permute-start | bytes 82952 | tf_op jit(solution)/shard_map/ppermute | solution.py:30
  45.0 15.0 %collective-permute-start.6 = (bf16[3,6,2,384]{3,2,1,0:T(2,128)(2,1)S(1)}, bf16[3,6,2,384]{3,2,1,0:T(2,128)(2,1)S(1)}, u32[]{:S(2)}, u32[]{:S(2)}) collective-permute-start(bf16[3,6,2,384]{3,2,1,0:T(2,128)(2,1)S(1)} %get-tuple-element.40), channel_id=1, source_target_pairs={{0,504},{1,505},{2,506},{3,507},{4,508},{5,509},{6,510},{7,511},{8... | collective-permute-start | bytes 82952 | tf_op jit(solution)/shard_map/ppermute | solution.py:30

commit v10 on v9

--- a/solution.py
+++ b/solution.py
@@ -22,10 +22,13 @@
 bf16 = jnp.bfloat16
 
 
-def from_behind(shard, lon, lat):
+def from_behind(shard, lon, lat, bands=lambda a: True):
     lons, lats = lax.axis_size("lon"), lax.axis_size("lat")
     pairs = [
-        (o * lats + a, (o + lon) % lons * lats + (a + lat) % lats) for o in range(lons) for a in range(lats)
+        (o * lats + a, (o + lon) % lons * lats + (a + lat) % lats)
+        for o in range(lons)
+        for a in range(lats)
+        if bands(a)
     ]
     return lax.ppermute(shard, ("lon", "lat"), pairs)
 
@@ -178,7 +181,8 @@
 def place():
     lat, lats = lax.axis_index("lat"), lax.axis_size("lat")
     lon, lons = lax.axis_index("lon"), lax.axis_size("lon")
-    return lat == lats - 1, (lat < lats // 2) & (lon < lons // 2)
+    early = ((lat < lats // 2) & (lon < lons // 2)) | ((lat == 0) & (lon >= lons - lons // 8))
+    return lat == lats - 1, early
 
 
 def prepare_kernel(
@@ -249,9 +253,13 @@
 
 
 def first_rows_kernel(
-    left_ref, own_ref, fine_ref, early0_ref, qkv_ref, proj_ref,
-    out_ref, send_ref, bias0_ref, x_ref, a_ref, stacked, spread_from,
-):
+    left_ref, own_ref, fine_ref, early0_ref, qkv_ref, proj_ref, up_hbm, down_hbm,
+    out_ref, send_ref, up_ref, down_ref, bias0_ref, x_ref, a_ref, stacked, spread_from, sems,
+):
+    moves = [(up_hbm, up_ref), (down_hbm, down_ref)]
+    copies = [pltpu.make_async_copy(source, to, sems.at[i]) for i, (source, to) in enumerate(moves)]
+    for copy in copies:
+        copy.start()
     _, early = place()
 
     @pl.when(jnp.logical_not(early))
@@ -271,6 +279,8 @@
     put(a_ref, 0, 288, 1, attended.astype(f32))
     lines = [a_ref[t, pl.ds(z * WLAT + a, 24, stride=LINES), :] for t in range(2) for z in range(WZ) for a in range(3)]
     send_ref[...] = pack_lines(lines[:6], [line[:, :64] for line in lines[6:]]).astype(bf16)
+    for copy in copies:
+        copy.wait()
 
 
 def second_rows_kernel(
@@ -302,7 +312,7 @@
 
 def coarse_kernel(
     y_ref, got_ref, fine_up_ref, fine_down_ref, merge_ref, bias_ref, qkv_ref, proj_ref, up_ref, down_ref,
-    keep_ref, lower_ref, corner_ref, left_ref, w_ref, p_ref, o_ref,
+    keep_ref, lower_ref, left_ref, corner_ref, again_ref, w_ref, p_ref, o_ref,
 ):
     got = got_ref[...].astype(f32)
     got = jnp.concatenate([unpack_line(got, z * 3 + a, 24) for a in range(3) for z in range(WZ)], axis=0)
@@ -339,8 +349,10 @@
     put(o_ref, 0, CELLS, 1, feed_forward(attended, up_ref, down_ref))
     for i in range(3):
         for j in range(WLON):
-            for ref, row in ((left_ref, i), (corner_ref, 3 + i)) if j < 6 else ((keep_ref, i), (lower_ref, 3 + i)):
-                ref[i, j % 6] = get(o_ref, j * LINES + row, WZ, WLAT, 384).astype(bf16)
+            for refs, row in (((left_ref, again_ref), i), ((corner_ref,), 3 + i)) if j < 6 else (((keep_ref,), i), ((lower_ref,), 3 + i)):
+                cell = get(o_ref, j * LINES + row, WZ, WLAT, 384).astype(bf16)
+                for ref in refs:
+                    ref[i, j % 6] = cell
 
 
 def call(kernel, outs, scratch, operands, flops):
@@ -374,6 +386,7 @@
     coarse_up,
     coarse_down,
 ):
+    lats = lax.axis_size("lat")
     fine_tables = fine_bias.transpose(0, 2, 3, 1, 4)
     coarse_tables = coarse_bias.transpose(0, 2, 3, 1, 4)
     fine_down = fine_down.T
@@ -396,12 +409,22 @@
     )(*(pltpu.with_memory_space_constraint(source, pltpu.HBM) for source in sources))
     corner = from_behind(corner, 1, -1)
     below = from_behind(below, 0, -1)
-    first, edge = call(
+    weights = [fine_up, fine_down]
+    first, edge, fine_up, fine_down = pl.pallas_call(
         first_rows_kernel,
-        [((288, 192), bf16), ((216, 128), bf16)],
-        [((6, CELLS, CELLS), f32), tiles_of(576, 192), tiles_of(288, 192)] + expansion,
-        [left, own, fine_tables, bias0, fine_qkv, fine_proj],
-        1_000_000_000,
+        out_shape=[jax.ShapeDtypeStruct((288, 192), bf16), jax.ShapeDtypeStruct((216, 128), bf16)]
+        + [jax.ShapeDtypeStruct(weight.shape, weight.dtype) for weight in weights],
+        in_specs=[vmem] * 6 + [hbm] * 2,
+        out_specs=[vmem] * 4,
+        scratch_shapes=[
+            pltpu.VMEM(shape, dtype)
+            for shape, dtype in [((6, CELLS, CELLS), f32), tiles_of(576, 192), tiles_of(288, 192)] + expansion
+        ]
+        + [pltpu.SemaphoreType.DMA((2,))],
+        compiler_params=pltpu.CompilerParams(vmem_limit_bytes=VMEM_LIMIT),
+    )(
+        *[left, own, fine_tables, bias0, fine_qkv, fine_proj],
+        *(pltpu.with_memory_space_constraint(weight, pltpu.HBM) for weight in weights),
     )
     got = from_behind(edge, 0, -1)
     bias1, bias2 = call(
@@ -419,16 +442,20 @@
         3_000_000_000,
     )
     quarter = ((3, 6, WZ, 384), bf16)
-    keep, lower, far_corner, upper_left = call(
+    keep, lower, first_left, far_corner, other_left = call(
         coarse_kernel,
-        [quarter] * 4,
+        [quarter] * 5,
         [tiles_of(576, 192), tiles_of(576, 192), tiles_of(CELLS, 384)],
         [finished, got, fine_up, fine_down, merge_weight, bias2, coarse_qkv, coarse_proj, coarse_up, coarse_down],
         4_000_000_000,
     )
     above = from_behind(lower, 0, 1)
+    band = lats // 2 + 1
+    right = from_behind(first_left, -1, 0, lambda a: a == band)
     corner = from_behind(far_corner, -1, 1)
-    right = from_behind(upper_left, -1, 0)
+    other = from_behind(other_left, -1, 0, lambda a: a != band)
+    above, right, corner, other = lax.optimization_barrier((above, right, corner, other))
+    right = right + other
     rows = [jnp.concatenate([above, corner], axis=1), jnp.concatenate([keep, right], axis=1)]
     return jnp.concatenate(rows, axis=0).transpose(2, 0, 1, 3)
 

time: 61.4 us -> 61.1 us (level)
  local copies, waits for them, and re-layouts: 0.66 us -> 0.03 us
    pallas_call x0 -> x1, Pallas kernels: none -> 1.83 us  [body(): pl.pallas_call(first_rows_kernel, out_shape=[jax.ShapeDtypeStruct((288, 1...]
    pallas_call x4 -> x3, Pallas kernels: 8.8 us -> 7.06 us  [call(): pl.pallas_call(kernel, out_shape=[jax.ShapeDtypeStruct(shape, dtype) for...]
    unnamed x14 -> x10, local copies, waits for them, and re-layouts: 0.66 us -> 0.03 us
    ppermute x7 -> x8, starting transfers between devices: 42.3 us -> 42.5 us  [from_behind(): return lax.ppermute(shard, ('lon', 'lat'), pairs)]
    ppermute x7 -> x8, waiting for transfers between devices: 3.58 us -> 3.73 us  [from_behind(): return lax.ppermute(shard, ('lon', 'lat'), pairs)]
  transfers between devices with their start and end apart: 7 -> 8, of which waited for: 1 -> 1; matrix products, arithmetic and copies ran while one was open for 0% -> 0% of each run, Pallas kernels for 15% -> 15%
where the time goes in v10:
time: 61.1 us; the launch traced here: 60.8 us
  starting transfers between devices  42.5 us (70%)
  Pallas kernels  13.4 us (22%)
  waiting for transfers between devices  3.73 us (6%)
  other arithmetic  0.84 us (1%)
    ppermute x8, starting transfers between devices, from_behind(): return lax.ppermute(shard, ('lon', 'lat'), pairs)  42.5 us
    pallas_call x3, Pallas kernels, call(): pl.pallas_call(kernel, out_shape=[jax.ShapeDtypeStruct(shape, dtype) for...  7.06 us
    pallas_call x1, Pallas kernels, body(): pl.pallas_call(prepare_kernel, out_shape=[jax.ShapeDtypeStruct((162, 128)...  4.52 us
    ppermute x8, waiting for transfers between devices, from_behind(): return lax.ppermute(shard, ('lon', 'lat'), pairs)  3.73 us
    pallas_call x1, Pallas kernels, body(): pl.pallas_call(first_rows_kernel, out_shape=[jax.ShapeDtypeStruct((288, 1...  1.83 us
  transfers between devices with their start and end apart: 8, of which 1 were waited for; matrix products, arithmetic and copies ran while one was open for 0% of the time, Pallas kernels for 15%

profile of v10, /device:TPU:1, one launch (start us, length us, event | category | flops | bytes accessed | tf_op | source)
XLA Modules:
  0.0 60.8 jit_solution(9948678760594403753)
XLA Ops:
  0.0 4.5 %collective-permute-start = (bf16[2,12,24,192]{3,2,1,0:T(8,128)(2,1)}, bf16[2,12,24,192]{3,2,1,0:T(8,128)(2,1)S(1)}, u32[]{:S(2)}, u32[]{:S(2)}) collective-permute-start(bf16[2,12,24,192]{3,2,1,0:T(8,128)(2,1)} %fields_hbm.1), channel_id=1, source_target_pairs={{0,8},{1,9},{2,10},{3,11},{4,12},{5,13},{6,14},{7,15},{8,16},{9,17... | collective-permute-start | bytes 663560 | tf_op jit(solution)/shard_map/ppermute | solution.py:33
  4.5 4.5 %shard_map.118 = (bf16[162,128]{1,0:T(8,128)(2,1)S(1)}, bf16[162,128]{1,0:T(8,128)(2,1)S(1)}, bf16[2,12,24,192]{3,2,1,0:T(8,128)(2,1)S(1)}, f32[2,6,23,1,144]{4,...) custom-call(bf16[2,12,24,192]{3,2,1,0:T(8,128)(2,1)} %fields_hbm.1, ...), custom_call_target="tpu_custom_call" | custom-call | tf_op jit(solution)/shard_map/pallas_call | solution.py:398
  9.0 14.4 %collective-permute-start.1 = (bf16[162,128]{1,0:T(8,128)(2,1)S(1)}, bf16[162,128]{1,0:T(8,128)(2,1)S(1)}, u32[]{:S(2)}, u32[]{:S(2)}) collective-permute-start(bf16[162,128]{1,0:T(8,128)(2,1)S(1)} %get-tuple-element.31), channel_id=1, source_target_pairs={{0,15},{1,8},{2,9},{3,10},{4,11},{5,12},{6,13},{7,14},{8,23},{9,16... | collective-permute-start | bytes 124424 | tf_op jit(solution)/shard_map/ppermute | solution.py:33
  23.4 2.4 %collective-permute-start.2 = (bf16[162,128]{1,0:T(8,128)(2,1)S(1)}, bf16[162,128]{1,0:T(8,128)(2,1)S(1)}, u32[]{:S(2)}, u32[]{:S(2)}) collective-permute-start(bf16[162,128]{1,0:T(8,128)(2,1)S(1)} %get-tuple-element.32), channel_id=1, source_target_pairs={{0,7},{1,0},{2,1},{3,2},{4,3},{5,4},{6,5},{7,6},{8,15},{9,8},{10,9... | collective-permute-start | bytes 124424 | tf_op jit(solution)/shard_map/ppermute | solution.py:33
  25.8 0.0 collective-permute-done.left_ref
  25.8 1.8 %shard_map.119 = (bf16[288,192]{1,0:T(8,128)(2,1)S(1)}, bf16[216,128]{1,0:T(8,128)(2,1)S(1)}, bf16[192,768]{1,0:T(8,128)(2,1)S(1)}, bf16[192,768]{1,0:T(8,128)(2,1)S(1)}) custom-call(bf16[2,12,24,192]{3,2,1,0:T(8,128)(2,1)S(1)} %collective-permute-done.left_ref, bf16[2,12,24,192]{3,2,1,0:T(8,128)(2,1)S(1)} %get-tuple-element.30.own_ref, ...), custom_call_target="tpu_custom_call" | custom-call | tf_op jit(solution)/shard_map/pallas_call | solution.py:413
  27.7 3.2 %collective-permute-start.3 = (bf16[216,128]{1,0:T(8,128)(2,1)S(1)}, bf16[216,128]{1,0:T(8,128)(2,1)S(1)}, u32[]{:S(2)}, u32[]{:S(2)}) collective-permute-start(bf16[216,128]{1,0:T(8,128)(2,1)S(1)} %get-tuple-element.44), channel_id=1, source_target_pairs={{0,7},{1,0},{2,1},{3,2},{4,3},{5,4},{6,5},{7,6},{8,15},{9,8},{10,9... | collective-permute-start | bytes 165896 | tf_op jit(solution)/shard_map/ppermute | solution.py:33
  30.9 0.4 shard_map.120
  31.3 0.0 collective-permute-done.1.corner_ref
  31.3 0.0 collective-permute-done.2.below_ref
  31.3 0.0 copy-start
  31.3 0.0 copy-start.1
  31.3 0.0 copy-start.2
  31.4 0.0 copy-start.3
  31.4 0.0 copy-start.4
  31.4 2.5 %shard_map.121.y_ref = bf16[432,192]{1,0:T(8,128)(2,1)S(1)} custom-call(bf16[2,12,24,192]{3,2,1,0:T(8,128)(2,1)S(1)} %collective-permute-done.left_ref, bf16[2,12,24,192]{3,2,1,0:T(8,128)(2,1)S(1)} %get-tuple-element.30.own_ref, bf16[162,128]{1,0:T(8,128)(2,1)S(1)} %collective-permute-done.1.corner_ref, ...), custom_call_target="tpu_custom_call" | custom-call | flops 3000000000 | bytes 2018304 | tf_op jit(solution)/shard_map/pallas_call | solution.py:360
  33.9 0.0 collective-permute-done.3.got_ref
  33.9 0.0 copy-done
  33.9 0.0 copy-done.1
  33.9 0.0 copy-done.2
  33.9 0.0 copy-done.3
  33.9 0.0 copy-done.4
  33.9 4.2 %shard_map.122 = (bf16[3,6,2,384]{3,2,1,0:T(2,128)(2,1)S(1)}, bf16[3,6,2,384]{3,2,1,0:T(2,128)(2,1)S(1)}, bf16[3,6,2,384]{3,2,1,0:T(2,128)(2,1)S(1)}, bf16[3,6,2...) custom-call(bf16[432,192]{1,0:T(8,128)(2,1)S(1)} %shard_map.121.y_ref, ...), custom_call_target="tpu_custom_call" | custom-call | flops 4000000000 | bytes 5935104 | tf_op jit(solution)/shard_map/pallas_call | solution.py:360
  38.1 2.0 %collective-permute-start.4 = (bf16[3,6,2,384]{3,2,1,0:T(2,128)(2,1)S(1)}, bf16[3,6,2,384]{3,2,1,0:T(2,128)(2,1)S(1)}, u32[]{:S(2)}, u32[]{:S(2)}) collective-permute-start(bf16[3,6,2,384]{3,2,1,0:T(2,128)(2,1)S(1)} %get-tuple-element.46), channel_id=1, source_target_pairs={{0,1},{1,2},{2,3},{3,4},{4,5},{5,6},{6,7},{7,0},{8,9},{9,10},{10,1... | collective-permute-start | bytes 82952 | tf_op jit(solution)/shard_map/ppermute | solution.py:33
  40.2 0.7 %collective-permute-start.5 = (bf16[3,6,2,384]{3,2,1,0:T(2,128)(2,1)S(1)}, bf16[3,6,2,384]{3,2,1,0:T(2,128)(2,1)S(1)}, u32[]{:S(2)}, u32[]{:S(2)}) collective-permute-start(bf16[3,6,2,384]{3,2,1,0:T(2,128)(2,1)S(1)} %get-tuple-element.47), channel_id=1, source_target_pairs={{5,509},{13,5},{21,13},{29,21},{37,29},{45,37},{53,45},{61,53},{69... | collective-permute-start | bytes 82952 | tf_op jit(solution)/shard_map/ppermute | solution.py:33
  40.9 4.3 %collective-permute-start.6 = (bf16[3,6,2,384]{3,2,1,0:T(2,128)(2,1)S(1)}, bf16[3,6,2,384]{3,2,1,0:T(2,128)(2,1)S(1)}, u32[]{:S(2)}, u32[]{:S(2)}) collective-permute-start(bf16[3,6,2,384]{3,2,1,0:T(2,128)(2,1)S(1)} %get-tuple-element.48), channel_id=1, source_target_pairs={{0,505},{1,506},{2,507},{3,508},{4,509},{5,510},{6,511},{7,504},{8... | collective-permute-start | bytes 82952 | tf_op jit(solution)/shard_map/ppermute | solution.py:33
  45.2 11.0 %collective-permute-start.7 = (bf16[3,6,2,384]{3,2,1,0:T(2,128)(2,1)S(1)}, bf16[3,6,2,384]{3,2,1,0:T(2,128)(2,1)S(1)}, u32[]{:S(2)}, u32[]{:S(2)}) collective-permute-start(bf16[3,6,2,384]{3,2,1,0:T(2,128)(2,1)S(1)} %get-tuple-element.49), channel_id=1, source_target_pairs={{0,504},{1,505},{2,506},{3,507},{4,508},{6,510},{7,511},{8,0},{9,1... | collective-permute-start | bytes 82952 | tf_op jit(solution)/shard_map/ppermute | solution.py:33
  56.2 0.0 collective-permute-done.4
  56.2 0.0 collective-permute-done.5
  56.2 3.7 %collective-permute-done.6 = bf16[3,6,2,384]{3,2,1,0:T(2,128)(2,1)S(1)} collective-permute-done((bf16[3,6,2,384]{3,2,1,0:T(2,128)(2,1)S(1)}, bf16[3,6,2,384]{3,2,1,0:T(2,128)(2,1)S(1)}, u32[]{:S(2)}, u32[]{:S(2)}) %collective-permute-start.6) | collective-permute-done | bytes 27680 | tf_op jit(solution)/shard_map/ppermute | solution.py:33
  59.9 0.0 collective-permute-done.7
  59.9 0.8 %maximum_bitcast_fusion = bf16[2,6,12,384]{3,0,2,1:T(2,128)(2,1)} fusion(bf16[3,6,2,384]{3,2,1,0:T(2,128)(2,1)S(1)} %add.3, bf16[3,6,2,384]{3,2,1,0:T(2,128)(2,1)S(1)} %get-tuple-element.52, bf16[3,6,2,384]{3,2,1,0:T(2,128)(2,1)S(1)} %collective-permute-done.6, bf16[3,6,2,384]{3,2,1,0:T(2,128)(2,1)S(1)} %collective-permute-done.4), kind=kLoop, calls=%fused_computation | loop fusion | flops 165888 | bytes 221184 | tf_op jit(solution)/shard_map/transpose | solution.py:460
  (1 shorter events, 0.0 us)
Async XLA Ops:
  0.0 25.8 %collective-permute-start = (bf16[2,12,24,192]{3,2,1,0:T(8,128)(2,1)}, bf16[2,12,24,192]{3,2,1,0:T(8,128)(2,1)S(1)}, u32[]{:S(2)}, u32[]{:S(2)}) collective-permute-start(bf16[2,12,24,192]{3,2,1,0:T(8,128)(2,1)} %fields_hbm.1), channel_id=1, source_target_pairs={{0,8},{1,9},{2,10},{3,11},{4,12},{5,13},{6,14},{7,15},{8,16},{9,17... | collective-permute-start | bytes 663560 | tf_op jit(solution)/shard_map/ppermute | solution.py:33
  9.0 22.3 %collective-permute-start.1 = (bf16[162,128]{1,0:T(8,128)(2,1)S(1)}, bf16[162,128]{1,0:T(8,128)(2,1)S(1)}, u32[]{:S(2)}, u32[]{:S(2)}) collective-permute-start(bf16[162,128]{1,0:T(8,128)(2,1)S(1)} %get-tuple-element.31), channel_id=1, source_target_pairs={{0,15},{1,8},{2,9},{3,10},{4,11},{5,12},{6,13},{7,14},{8,23},{9,16... | collective-permute-start | bytes 124424 | tf_op jit(solution)/shard_map/ppermute | solution.py:33
  23.4 7.9 %collective-permute-start.2 = (bf16[162,128]{1,0:T(8,128)(2,1)S(1)}, bf16[162,128]{1,0:T(8,128)(2,1)S(1)}, u32[]{:S(2)}, u32[]{:S(2)}) collective-permute-start(bf16[162,128]{1,0:T(8,128)(2,1)S(1)} %get-tuple-element.32), channel_id=1, source_target_pairs={{0,7},{1,0},{2,1},{3,2},{4,3},{5,4},{6,5},{7,6},{8,15},{9,8},{10,9... | collective-permute-start | bytes 124424 | tf_op jit(solution)/shard_map/ppermute | solution.py:33
  27.7 6.2 %collective-permute-start.3 = (bf16[216,128]{1,0:T(8,128)(2,1)S(1)}, bf16[216,128]{1,0:T(8,128)(2,1)S(1)}, u32[]{:S(2)}, u32[]{:S(2)}) collective-permute-start(bf16[216,128]{1,0:T(8,128)(2,1)S(1)} %get-tuple-element.44), channel_id=1, source_target_pairs={{0,7},{1,0},{2,1},{3,2},{4,3},{5,4},{6,5},{7,6},{8,15},{9,8},{10,9... | collective-permute-start | bytes 165896 | tf_op jit(solution)/shard_map/ppermute | solution.py:33
  31.3 2.6 %copy-start = (bf16[384,1536]{1,0:T(8,128)(2,1)S(1)}, bf16[384,1536]{1,0:T(8,128)(2,1)}, u32[]{:S(2)}) copy-start(bf16[384,1536]{1,0:T(8,128)(2,1)} %up_ref.1) | copy-start | bytes 3538948
  31.3 2.6 %copy-start.1 = (bf16[1536,384]{1,0:T(8,128)(2,1)S(1)}, bf16[1536,384]{1,0:T(8,128)(2,1)}, u32[]{:S(2)}) copy-start(bf16[1536,384]{1,0:T(8,128)(2,1)} %down_ref.1) | copy-start | bytes 3538948
  31.3 2.6 %copy-start.2 = (bf16[384,1152]{1,0:T(8,128)(2,1)S(1)}, bf16[384,1152]{1,0:T(8,128)(2,1)}, u32[]{:S(2)}) copy-start(bf16[384,1152]{1,0:T(8,128)(2,1)} %qkv_ref.1) | copy-start | bytes 2654212
  31.4 2.6 %copy-start.3 = (bf16[768,384]{1,0:T(8,128)(2,1)S(1)}, bf16[768,384]{1,0:T(8,128)(2,1)}, u32[]{:S(2)}) copy-start(bf16[768,384]{1,0:T(8,128)(2,1)} %merge_ref.1) | copy-start | bytes 1769476
  31.4 2.5 %copy-start.4 = (bf16[384,384]{1,0:T(8,128)(2,1)S(1)}, bf16[384,384]{1,0:T(8,128)(2,1)}, u32[]{:S(2)}) copy-start(bf16[384,384]{1,0:T(8,128)(2,1)} %proj_ref.1) | copy-start | bytes 884740
  38.1 18.0 %collective-permute-start.4 = (bf16[3,6,2,384]{3,2,1,0:T(2,128)(2,1)S(1)}, bf16[3,6,2,384]{3,2,1,0:T(2,128)(2,1)S(1)}, u32[]{:S(2)}, u32[]{:S(2)}) collective-permute-start(bf16[3,6,2,384]{3,2,1,0:T(2,128)(2,1)S(1)} %get-tuple-element.46), channel_id=1, source_target_pairs={{0,1},{1,2},{2,3},{3,4},{4,5},{5,6},{6,7},{7,0},{8,9},{9,10},{10,1... | collective-permute-start | bytes 82952 | tf_op jit(solution)/shard_map/ppermute | solution.py:33
  40.2 16.0 %collective-permute-start.5 = (bf16[3,6,2,384]{3,2,1,0:T(2,128)(2,1)S(1)}, bf16[3,6,2,384]{3,2,1,0:T(2,128)(2,1)S(1)}, u32[]{:S(2)}, u32[]{:S(2)}) collective-permute-start(bf16[3,6,2,384]{3,2,1,0:T(2,128)(2,1)S(1)} %get-tuple-element.47), channel_id=1, source_target_pairs={{5,509},{13,5},{21,13},{29,21},{37,29},{45,37},{53,45},{61,53},{69... | collective-permute-start | bytes 82952 | tf_op jit(solution)/shard_map/ppermute | solution.py:33
  40.9 19.0 %collective-permute-start.6 = (bf16[3,6,2,384]{3,2,1,0:T(2,128)(2,1)S(1)}, bf16[3,6,2,384]{3,2,1,0:T(2,128)(2,1)S(1)}, u32[]{:S(2)}, u32[]{:S(2)}) collective-permute-start(bf16[3,6,2,384]{3,2,1,0:T(2,128)(2,1)S(1)} %get-tuple-element.48), channel_id=1, source_target_pairs={{0,505},{1,506},{2,507},{3,508},{4,509},{5,510},{6,511},{7,504},{8... | collective-permute-start | bytes 82952 | tf_op jit(solution)/shard_map/ppermute | solution.py:33
  45.2 14.7 %collective-permute-start.7 = (bf16[3,6,2,384]{3,2,1,0:T(2,128)(2,1)S(1)}, bf16[3,6,2,384]{3,2,1,0:T(2,128)(2,1)S(1)}, u32[]{:S(2)}, u32[]{:S(2)}) collective-permute-start(bf16[3,6,2,384]{3,2,1,0:T(2,128)(2,1)S(1)} %get-tuple-element.49), channel_id=1, source_target_pairs={{0,504},{1,505},{2,506},{3,507},{4,508},{6,510},{7,511},{8,0},{9,1... | collective-permute-start | bytes 82952 | tf_op jit(solution)/shard_map/ppermute | solution.py:33
